TPU v7x, 32 devices: a whole 2x2x4 slice. The times are simulated.
32 devices in a mesh: dp: 8 (over z, core), tensor: 4 (over y, x).
Axes of the slice: x: 2, y: 2, z: 4, core: 2. Of those that a mesh axis runs over, the one named last changes fastest.
Arguments:
- out_grad: bfloat16 [2048, 4096], P('dp'), may hold values from -8 to 8
- hidden_act: bfloat16 [2048, 15360], P('dp', 'tensor'), may hold values from -6 to 6
- log_ratio: float32 [64], P('dp'), may hold values from -40 to 40
- pair_order: int32 [8, 8], P('dp'), may hold values from 0 to 7, each once within a row
- seq_len: int32 [64], P('dp'), may hold values from 1 to 32, 1280 in all
- master: float32 [4096, 15360], P('dp', 'tensor'), may hold values from -0.046875 to 0.046875
- moment: float32 [4096, 15360], P('dp', 'tensor'), may hold values from -6 to 6
- second: float32 [4096, 15360], P('dp', 'tensor'), may hold values from 0.005 to 0.08
- next_act: bfloat16 [4096, 15360], P('dp', 'tensor'), may hold values from -6 to 6
Outputs:
- new_master: float32 [4096, 15360], P('dp', 'tensor')
- new_moment: float32 [4096, 15360], P('dp', 'tensor')
- new_second: float32 [4096, 15360], P('dp', 'tensor')
- update: float32 [4096, 15360], P('dp', 'tensor')
- next_out: bfloat16 [4096, 4096], P('dp', 'tensor')
Inputs may be any that keep to these rules, and one draw needn't show every extreme that they name: Each row of pair_order holds every number below 8 once.
All inputs are finite; a program needn't handle non-finite values. No bound on the sum of `seq_len` on one device may be relied on, other than what follows from the above.
Results may differ from a plain program's by a relative error of at most 0.02.
Values may be sent and summed in bfloat16 or wider, within the bound.
No kernel may reach another device: no remote copies, remote signals or barrier semaphores. Data moves between devices by JAX's collectives and lax.ppermute only.
A program may use at most 192 MiB of HBM per device.

v0:
```python
import jax
import jax.numpy as jnp
from jax import lax
from jax.sharding import PartitionSpec as P

LEN = 32


beta_dpo = 0.1
beta_one = 0.9
beta_two = 0.999
bias_one = 1.0 - 0.9**10
bias_two = 1.0 - 0.999**10
adam_eps = 1e-08
rate_learn = 0.001


def row_factors(ratios, pair_row, lengths):
    seq_count = ratios.shape[0]
    seq_slots = jnp.arange(seq_count, dtype=jnp.int32)
    chosen = pair_row[0::2]
    rejected = pair_row[1::2]
    pick_chosen = (chosen[:, None] == seq_slots[None, :]).astype(jnp.float32)
    pick_rejected = (rejected[:, None] == seq_slots[None, :]).astype(jnp.float32)
    margin = beta_dpo * (
        jnp.sum(pick_chosen * ratios[None, :], axis=1)
        - jnp.sum(pick_rejected * ratios[None, :], axis=1)
    )
    weight = beta_dpo * jax.nn.sigmoid(-margin)
    coefficient = jnp.sum(weight[:, None] * (pick_rejected - pick_chosen), axis=0)
    position = jnp.arange(LEN, dtype=jnp.int32)
    in_length = (position[None, :] < lengths[:, None]).astype(jnp.float32)
    return coefficient[:, None] * in_length


def body(out_grad, hidden_act, log_ratio, pair_order, seq_len, master, moment, second, next_act):
    factors = row_factors(log_ratio, pair_order[0], seq_len)
    scaled = (out_grad.astype(jnp.float32) * factors.reshape(-1)[:, None]).astype(jnp.bfloat16)
    grad = lax.psum_scatter(
        lax.dot_general(
            scaled, hidden_act, (((0,), (0,)), ((), ())), preferred_element_type=jnp.float32
        ).astype(jnp.bfloat16),
        "dp",
        scatter_dimension=0,
        tiled=True,
    ).astype(jnp.float32)
    new_moment = beta_one * moment + (1.0 - beta_one) * grad
    new_second = beta_two * second + (1.0 - beta_two) * grad * grad
    update = new_moment / bias_one / (jnp.sqrt(new_second / bias_two) + adam_eps)
    new_master = master - rate_learn * update
    weights = new_master.astype(jnp.bfloat16)
    partial_next = lax.dot_general(
        next_act,
        lax.all_gather(weights, "dp", axis=0, tiled=True),
        (((1,), (1,)), ((), ())),
        preferred_element_type=jnp.float32,
    )
    summed = lax.psum_scatter(
        partial_next.astype(jnp.bfloat16), "tensor", scatter_dimension=1, tiled=True
    )
    return (new_master, new_moment, new_second, update, summed)


def solution(mesh):
    return jax.shard_map(
        body,
        mesh=mesh,
        in_specs=(
            P("dp", None),
            P("dp", "tensor"),
            P("dp"),
            P("dp", None),
            P("dp"),
            P("dp", "tensor"),
            P("dp", "tensor"),
            P("dp", "tensor"),
            P("dp", "tensor"),
        ),
        out_specs=(
            P("dp", "tensor"),
            P("dp", "tensor"),
            P("dp", "tensor"),
            P("dp", "tensor"),
            P("dp", "tensor"),
        ),
        check_vma=False,
    )
```

profile of v0, /device:TPU:13, one launch (start us, length us, event | category | flops | bytes accessed | tf_op | source)
XLA Modules:
  0.0 712.3 jit_solution(5939158389052504802)
XLA Ops:
  7.2 0.0 copy-start
  7.2 0.0 reduce-scatter.3.cloned.1.call-start
  7.2 0.9 slice.7
  8.1 0.7 slice.6
  8.8 0.9 select_reduce_fusion
  9.7 0.1 multiply_reduce_fusion
  9.8 0.7 fusion.4
  10.6 0.1 mul.92
  10.6 0.0 copy-done
  10.6 16.4 %convolution_convert_fusion = bf16[4096,3840]{1,0:T(8,128)(2,1)} fusion(bf16[256,3840]{1,0:T(8,128)(2,1)S(1)} %copy-done, bf16[256,4096]{1,0:T(8,128)(2,1)} %param.9, f32[256]{0:T(256)S(1)} %mul.92), kind=kOutput, calls=%fused_computation | convolution fusion | flops 8071938048 | bytes 35521536 | tf_op jit(solution)/shard_map/dot_general | solution.py:40
  27.1 0.0 reduce-scatter.3.cloned.1.call-update
  27.1 0.0 all-gather.2.cloned.1.call-start
  27.2 306.1 %reduce-scatter.3.cloned.1.call-done = bf16[512,3840]{1,0:T(8,128)(2,1)} async-done(((bf16[4096,3840]{1,0:T(8,128)(2,1)}), bf16[512,3840]{1,0:T(8,128)(2,1)}) %reduce-scatter.3.cloned.1.call-update) | async-done | bytes 3932176 | tf_op jit(solution)/shard_map/reduce_scatter | solution.py:39
  333.2 24.5 %fusion.5 = (bf16[512,3840]{1,0:T(8,128)(2,1)}, f32[512,3840]{1,0:T(8,128)}, f32[512,3840]{1,0:T(8,128)}, f32[512,3840]{1,0:T(8,128)}, f32[512,3840]{1,0:T(8,128)}) fusion(f32[512,3840]{1,0:T(8,128)} %param.14, bf16[512,3840]{1,0:T(8,128)(2,1)} %reduce-scatter.3.cloned.1.call-done, f32[512,3840]{1,0:T(8,128)} %param.15, f32[512,3840]{1,0:T(8,128)} %param.16), kind=kLoop, calls=%fused_computation.19 | loop fusion | flops 29491200 | bytes 62914560 | tf_op jit(solution)/shard_map/convert_element_type | solution.py:51
  357.7 0.0 all-gather.2.cloned.1.call-update
  357.7 0.0 reduce-scatter.5.cloned.1.call-start
  357.8 269.1 %all-gather.2.cloned.1.call-done = bf16[4096,3840]{1,0:T(8,128)(2,1)} async-done(((bf16[512,3840]{1,0:T(8,128)(2,1)}), bf16[4096,3840]{1,0:T(8,128)(2,1)}) %all-gather.2.cloned.1.call-update) | async-done | bytes 31457296 | tf_op jit(solution)/shard_map/all_gather | solution.py:54
  626.8 0.0 copy-start.1
  626.8 23.4 %fusion.2 = bf16[512,4096]{0,1:T(8,128)(2,1)} fusion(bf16[4096,3840]{1,0:T(8,128)(2,1)} %all-gather.2.cloned.1.call-done, bf16[512,3840]{1,0:T(8,128)(2,1)} %param.17), kind=kOutput, calls=%fused_computation.8 | convolution fusion | flops 16108224512 | bytes 39583744 | tf_op jit(solution)/shard_map/dot_general | solution.py:52
  650.3 0.0 reduce-scatter.5.cloned.1.call-update
  650.3 53.3 %reduce-scatter.5.cloned.1.call-done = bf16[512,1024]{0,1:T(8,128)(2,1)} async-done(((bf16[512,4096]{0,1:T(8,128)(2,1)}), bf16[512,1024]{0,1:T(8,128)(2,1)}) %reduce-scatter.5.cloned.1.call-update) | async-done | bytes 1048592 | tf_op jit(solution)/shard_map/reduce_scatter | solution.py:58
  703.6 2.3 copy.15
  705.8 0.0 copy-done.1
  (1 shorter events, 0.0 us)
Async XLA Ops:
  7.2 3.5 copy-start
  7.2 326.1 %reduce-scatter.3.cloned.1.call-start = ((), (), s32[]{:S(2)}) async-start(), calls=%async_computation.2 | async-start | bytes 35389440 | tf_op jit(solution)/shard_map/reduce_scatter | solution.py:39
  27.1 599.7 %all-gather.2.cloned.1.call-start = ((), (), s32[]{:S(2)}) async-start(), calls=%async_computation.3 | async-start | bytes 35389440 | tf_op jit(solution)/shard_map/all_gather | solution.py:54
  357.7 345.8 %reduce-scatter.5.cloned.1.call-start = ((), (), s32[]{:S(2)}) async-start(), calls=%async_computation.4 | async-start | bytes 5242880 | tf_op jit(solution)/shard_map/reduce_scatter | solution.py:58
  626.8 79.0 %copy-start.1 = (bf16[256,3840]{1,0:T(8,128)(2,1)S(1)}, bf16[256,3840]{1,0:T(8,128)(2,1)}, u32[]{:S(2)}) copy-start(bf16[256,3840]{1,0:T(8,128)(2,1)} %param.10) | copy-start | bytes 5898244
Sparse Core Ops, SparseCore 0:
  27.2 305.9 reduce-scatter.2
  357.8 268.9 all-gather.1
  650.4 53.0 reduce-scatter.4
where the time goes:
time: 714 us; the launch traced here: 712 us
  waiting for transfers between devices  628 us (88%)
  matrix products  39.9 us (6%)
  other arithmetic  26.2 us (4%)
  between operations  13.8 us (2%)
    reduce_scatter x1, waiting for transfers between devices, body(): lax.psum_scatter(lax.dot_general(scaled, hidden_act, (((0,), (0,)), ((),...  306 us
    all_gather x1, waiting for transfers between devices, body(): lax.all_gather(weights, 'dp', axis=0, tiled=True)  269 us
    reduce_scatter x1, waiting for transfers between devices, body(): lax.psum_scatter(partial_next.astype(jnp.bfloat16), 'tensor', scatter_dim...  53.3 us
    convert_element_type x1, other arithmetic, body(): weights = new_master.astype(jnp.bfloat16)  24.5 us
    dot_general x1, matrix products, body(): lax.dot_general(next_act, lax.all_gather(weights, 'dp', axis=0, tiled=Tru...  23.4 us
    dot_general x1, matrix products, body(): lax.dot_general(scaled, hidden_act, (((0,), (0,)), ((), ())), preferred_e...  16.4 us
  transfers between devices with their start and end apart: 3, of which 3 were waited for; matrix products, arithmetic and copies ran while one was open for 0% of the time, Pallas kernels for 0%

commit v1 on v0

--- a/solution.py
+++ b/solution.py
@@ -1,6 +1,10 @@
+import functools
+
 import jax
 import jax.numpy as jnp
 from jax import lax
+from jax.experimental import pallas as pl
+from jax.experimental.pallas import tpu as pltpu
 from jax.sharding import PartitionSpec as P
 
 LEN = 32
@@ -13,6 +17,8 @@
 bias_two = 1.0 - 0.999**10
 adam_eps = 1e-08
 rate_learn = 0.001
+
+ROW_CHUNKS = 4
 
 
 def row_factors(ratios, pair_row, lengths):
@@ -33,27 +39,34 @@
     return coefficient[:, None] * in_length
 
 
-def body(out_grad, hidden_act, log_ratio, pair_order, seq_len, master, moment, second, next_act):
+def scale_rows(out_grad, log_ratio, pair_order, seq_len):
     factors = row_factors(log_ratio, pair_order[0], seq_len)
-    scaled = (out_grad.astype(jnp.float32) * factors.reshape(-1)[:, None]).astype(jnp.bfloat16)
-    grad = lax.psum_scatter(
-        lax.dot_general(
-            scaled, hidden_act, (((0,), (0,)), ((), ())), preferred_element_type=jnp.float32
-        ).astype(jnp.bfloat16),
-        "dp",
-        scatter_dimension=0,
-        tiled=True,
-    ).astype(jnp.float32)
+    return (out_grad.astype(jnp.float32) * factors.reshape(-1)[:, None]).astype(jnp.bfloat16)
+
+
+def adam(grad, master, moment, second):
     new_moment = beta_one * moment + (1.0 - beta_one) * grad
     new_second = beta_two * second + (1.0 - beta_two) * grad * grad
-    update = new_moment / bias_one / (jnp.sqrt(new_second / bias_two) + adam_eps)
+    update = (new_moment * (1.0 / bias_one)) / (
+        jnp.sqrt(new_second * (1.0 / bias_two)) + adam_eps
+    )
     new_master = master - rate_learn * update
-    weights = new_master.astype(jnp.bfloat16)
+    return new_master, new_moment, new_second, update
+
+
+def body_general(
+    out_grad, hidden_act, log_ratio, pair_order, seq_len, master, moment, second, next_act
+):
+    scaled = scale_rows(out_grad, log_ratio, pair_order, seq_len)
+    mine = lax.all_to_all(scaled, "dp", split_axis=1, concat_axis=0, tiled=True)
+    hidden = lax.all_gather(hidden_act, "dp", axis=0, tiled=True)
+    grad = lax.dot_general(
+        mine, hidden, (((0,), (0,)), ((), ())), preferred_element_type=jnp.float32
+    )
+    new_master, new_moment, new_second, update = adam(grad, master, moment, second)
+    weights = lax.all_gather(new_master.astype(jnp.bfloat16), "dp", axis=0, tiled=True)
     partial_next = lax.dot_general(
-        next_act,
-        lax.all_gather(weights, "dp", axis=0, tiled=True),
-        (((1,), (1,)), ((), ())),
-        preferred_element_type=jnp.float32,
+        next_act, weights, (((1,), (1,)), ((), ())), preferred_element_type=jnp.float32
     )
     summed = lax.psum_scatter(
         partial_next.astype(jnp.bfloat16), "tensor", scatter_dimension=1, tiled=True
@@ -61,9 +74,163 @@
     return (new_master, new_moment, new_second, update, summed)
 
 
+def planes(pairs):
+    return [(2 * a + core, 2 * b + core) for a, b in pairs for core in (0, 1)]
+
+
+PAIR = planes([(0, 1), (1, 0), (2, 3), (3, 2)])
+MIDDLE = planes([(1, 2), (2, 1)])
+OUTWARD = planes([(1, 0), (2, 3)])
+INWARD = planes([(0, 1), (3, 2)])
+CORES = [(2 * z + core, 2 * z + 1 - core) for z in range(4) for core in (0, 1)]
+
+
+def step_kernel(n_act, has_prior, *refs):
+    scaled_ref = refs[0]
+    acts = refs[1 : 1 + n_act]
+    master_ref, moment_ref, second_ref = refs[1 + n_act : 4 + n_act]
+    outs = refs[4 + n_act + (4 if has_prior else 0) :]
+    tokens = acts[0].shape[0]
+    grad = None
+    for i, act in enumerate(acts):
+        term = jnp.dot(
+            scaled_ref[:, i * tokens : (i + 1) * tokens],
+            act[...],
+            preferred_element_type=jnp.float32,
+        )
+        grad = term if grad is None else grad + term
+    new_master, new_moment, new_second, update = adam(
+        grad, master_ref[...], moment_ref[...], second_ref[...]
+    )
+    outs[0][...] = new_master
+    outs[1][...] = new_moment
+    outs[2][...] = new_second
+    outs[3][...] = update
+    outs[4][...] = new_master.astype(jnp.bfloat16)
+
+
+def step_rows(r, scaled_t, acts, master, moment, second, prior):
+    rows_all, cols = master.shape
+    rows = rows_all // ROW_CHUNKS
+    tokens = acts[0].shape[0]
+    tile = 768
+    state = pl.BlockSpec((rows, tile), lambda t: (r, t))
+    in_specs = (
+        [pl.BlockSpec((rows, scaled_t.shape[1]), lambda t: (r, 0))]
+        + [pl.BlockSpec((tokens, tile), lambda t: (0, t))] * len(acts)
+        + [state] * 3
+    )
+    operands = [scaled_t, *acts, master, moment, second]
+    aliases = {}
+    if prior is not None:
+        for i, array in enumerate(prior):
+            aliases[len(operands)] = i
+            operands.append(array)
+            in_specs.append(pl.BlockSpec(memory_space=pl.ANY))
+    full = jax.ShapeDtypeStruct((rows_all, cols), jnp.float32)
+    outs = pl.pallas_call(
+        functools.partial(step_kernel, len(acts), prior is not None),
+        grid=(cols // tile,),
+        in_specs=in_specs,
+        out_specs=[state] * 4 + [pl.BlockSpec((rows, tile), lambda t: (0, t))],
+        out_shape=[full] * 4 + [jax.ShapeDtypeStruct((rows, cols), jnp.bfloat16)],
+        input_output_aliases=aliases,
+        compiler_params=pltpu.CompilerParams(vmem_limit_bytes=48 * 1024 * 1024),
+        cost_estimate=pl.CostEstimate(
+            flops=2 * rows * cols * tokens * len(acts),
+            bytes_accessed=2 * tokens * len(acts) * cols + 30 * rows * cols,
+            transcendentals=rows * cols,
+        ),
+        name="gradient_adam",
+    )(*operands)
+    return outs[:4], outs[4]
+
+
+def times(tokens, rows):
+    return lax.dot_general(
+        tokens, rows, (((1,), (1,)), ((), ())), preferred_element_type=jnp.float32
+    ).astype(jnp.bfloat16)
+
+
+def by_plane(parts, z):
+    odd, high = (z & 1) == 1, (z & 2) == 2
+    a = [jnp.where(odd, parts[i ^ 1], parts[i]) for i in range(4)]
+    return [jnp.where(high, a[i ^ 2], a[i]) for i in range(4)]
+
+
+def body_planes(
+    out_grad, hidden_act, log_ratio, pair_order, seq_len, master, moment, second, next_act
+):
+    send = lambda array, pairs: lax.ppermute(array, "dp", pairs)
+    k = lax.axis_index("dp")
+    j = lax.axis_index("tensor")
+    z, core = k // 2, k % 2
+    inner = (z == 1) | (z == 2)
+    tokens = hidden_act.shape[0]
+    model = out_grad.shape[1]
+    rows_all, cols = master.shape
+
+    pair_act = send(hidden_act, PAIR)
+    middle_act = send(hidden_act, MIDDLE)
+    forward_act = send(pair_act, MIDDLE)
+    far_one = send(middle_act, OUTWARD)
+    far_two = send(forward_act, OUTWARD)
+    third = jnp.where(inner, middle_act, far_one)
+    fourth = jnp.where(inner, forward_act, far_two)
+    acts = []
+    for act in (hidden_act, pair_act, third, fourth):
+        acts += [act, send(act, CORES)]
+
+    scaled = scale_rows(out_grad, log_ratio, pair_order, seq_len)
+    share = tokens // 4
+    part = lax.dynamic_slice_in_dim(scaled, j * share, share, 0)
+    part = lax.all_to_all(
+        part.reshape(share, 8, model // 8), "dp", split_axis=1, concat_axis=0, tiled=False
+    )
+    whole = lax.all_gather(part, "tensor", axis=0, tiled=False)
+    order = jnp.array(
+        [[0, 1, 2, 3], [1, 0, 2, 3], [2, 3, 1, 0], [3, 2, 1, 0]], dtype=jnp.int32
+    )[z]
+    order = jnp.stack([order * 2 + core, order * 2 + 1 - core], axis=1).reshape(8)
+    whole = jnp.take(whole, order, axis=1)
+    scaled_t = whole.transpose(3, 1, 0, 2).reshape(model // 8, 8 * tokens)
+
+    next_two = jnp.concatenate([next_act, send(next_act, CORES)], axis=0)
+    next_pair = send(next_act, INWARD)
+    next_pair = jnp.concatenate([next_pair, send(next_pair, CORES)], axis=0)
+
+    rows = rows_all // ROW_CHUNKS
+    prior = None
+    sums = []
+    for r in range(ROW_CHUNKS):
+        prior, own = step_rows(r, scaled_t, acts, master, moment, second, prior)
+        pair = send(own, PAIR)
+        middle = send(own, MIDDLE)
+        forward = send(pair, MIDDLE)
+        product = [times(next_two, block) for block in (own, pair, forward, middle)]
+        zero = jnp.zeros_like(product[0])
+        other = [zero, zero] + [times(next_pair, block) for block in (forward, middle)]
+        stack = []
+        for a, b in zip(by_plane(product, z), by_plane(other, z)):
+            stack += [a, b]
+        total = lax.psum_scatter(
+            jnp.concatenate(stack, axis=0), "tensor", scatter_dimension=0, tiled=True
+        )
+        count = next_two.shape[0]
+        sums.append(total[:count] + send(total[count:], OUTWARD))
+    columns = jnp.concatenate(sums, axis=1)
+    half = columns.shape[0] // 2
+    mine, theirs = columns[:half], send(columns[half:], CORES)
+    next_out = jnp.concatenate(
+        [jnp.where(core == 0, mine, theirs), jnp.where(core == 0, theirs, mine)], axis=1
+    )
+    return (*prior, next_out)
+
+
 def solution(mesh):
+    fits = mesh.shape["dp"] == 8 and mesh.shape["tensor"] == 4
     return jax.shard_map(
-        body,
+        body_planes if fits else body_general,
         mesh=mesh,
         in_specs=(
             P("dp", None),

time: 714 us -> 536 us (0.75); the launches traced: 712 us -> 525 us
  waiting for transfers between devices: 628 us -> 212 us
  matrix products: 39.9 us -> 122 us
  starting transfers between devices: 0.12 us -> 65.8 us
  Pallas kernels: 0 us -> 50.6 us
  local copies, waits for them, and re-layouts: 3.98 us -> 30 us
    reduce_scatter x2 -> x4, waiting for transfers between devices: 359 us -> 42.4 us  [body_planes(): lax.psum_scatter(jnp.concatenate(stack, axis=0), 'tensor', scatter_dimens...]
    all_gather x1, waiting for transfers between devices: 269 us -> 15.7 us  [body_planes(): whole = lax.all_gather(part, 'tensor', axis=0, tiled=False)]
    ppermute x0 -> x29, waiting for transfers between devices: none -> 107 us  [body_planes(): send = lambda array, pairs: lax.ppermute(array, 'dp', pairs)]
    dot_general x2 -> x24, matrix products: 39.9 us -> 122 us  [times(): lax.dot_general(tokens, rows, (((1,), (1,)), ((), ())), preferred_element...]
    ppermute x0 -> x29, starting transfers between devices: none -> 60.3 us  [body_planes(): send = lambda array, pairs: lax.ppermute(array, 'dp', pairs)]
    pallas_call x0 -> x4, Pallas kernels: none -> 50.6 us  [step_rows(): pl.pallas_call(functools.partial(step_kernel, len(acts), prior is not Non...]
    all_to_all x0 -> x1, waiting for transfers between devices: none -> 46.5 us  [body_planes(): lax.all_to_all(part.reshape(share, 8, model // 8), 'dp', split_axis=1, co...]
    convert_element_type x1, other arithmetic: 24.5 us -> 1.34 us  [scale_rows(): (out_grad.astype(jnp.float32) * factors.reshape(-1)[:, None]).astype(jnp....]
  transfers between devices with their start and end apart: 3 -> 35, of which waited for: 3 -> 11; matrix products, arithmetic and copies ran while one was open for 0% -> 34% of each run, Pallas kernels for 0% -> 10%
where the time goes in v1:
time: 536 us; the launch traced here: 525 us
  waiting for transfers between devices  212 us (40%)
  matrix products  122 us (23%)
  starting transfers between devices  65.8 us (12%)
  Pallas kernels  50.6 us (9%)
  other arithmetic  30.2 us (6%)
  local copies, waits for them, and re-layouts  30 us (6%)
  between operations  14.9 us (3%)
    dot_general x24, matrix products, times(): lax.dot_general(tokens, rows, (((1,), (1,)), ((), ())), preferred_element...  122 us
    ppermute x29, waiting for transfers between devices, body_planes(): send = lambda array, pairs: lax.ppermute(array, 'dp', pairs)  107 us
    ppermute x29, starting transfers between devices, body_planes(): send = lambda array, pairs: lax.ppermute(array, 'dp', pairs)  60.3 us
    pallas_call x4, Pallas kernels, step_rows(): pl.pallas_call(functools.partial(step_kernel, len(acts), prior is not Non...  50.6 us
    all_to_all x1, waiting for transfers between devices, body_planes(): lax.all_to_all(part.reshape(share, 8, model // 8), 'dp', split_axis=1, co...  46.5 us
    reduce_scatter x4, waiting for transfers between devices, body_planes(): lax.psum_scatter(jnp.concatenate(stack, axis=0), 'tensor', scatter_dimens...  42.4 us
    all_gather x1, waiting for transfers between devices, body_planes(): whole = lax.all_gather(part, 'tensor', axis=0, tiled=False)  15.7 us
    unnamed x24, other arithmetic  13.2 us
  transfers between devices with their start and end apart: 35, of which 11 were waited for; matrix products, arithmetic and copies ran while one was open for 34% of the time, Pallas kernels for 10%

profile of v1, /device:TPU:13, one launch (start us, length us, event | category | flops | bytes accessed | tf_op | source)
XLA Modules:
  0.0 525.5 jit_solution(11839993339281821722)
XLA Ops:
  7.4 4.3 collective-permute-start.3
  11.7 39.5 %collective-permute-done.1.refs_3_ = bf16[256,3840]{1,0:T(8,128)(2,1)} collective-permute-done((bf16[256,3840]{1,0:T(8,128)(2,1)}, bf16[256,3840]{1,0:T(8,128)(2,1)}, u32[]{:S(2)}, u32[]{:S(2)}) %collective-permute-start.1) | collective-permute-done | bytes 1966112 | tf_op jit(solution)/shard_map/ppermute | solution.py:164
  51.2 3.2 collective-permute-start.6
  58.2 7.2 %collective-permute-start.4 = (bf16[256,3840]{1,0:T(8,128)(2,1)}, bf16[256,3840]{1,0:T(8,128)(2,1)}, u32[]{:S(2)}, u32[]{:S(2)}) collective-permute-start(bf16[256,3840]{1,0:T(8,128)(2,1)} %collective-permute-done.3), channel_id=1, source_target_pairs={{8,0},{12,4},{16,24},{20,28},{9,1},{13,5},{17,25},{21,29},{10,2},{... | collective-permute-start | bytes 5898248 | tf_op jit(solution)/shard_map/ppermute | solution.py:164
  68.7 5.3 %all-to-all-start = ((bf16[1,64,8,512]{3,1,0,2:T(8,128)(2,1)}), bf16[1,64,8,512]{3,1,0,2:T(8,128)(2,1)S(1)}, u32[]{:S(2)}, u32[]{:S(2)}) async-start(bf16[1,64,8,512]{3,1,0,2:T(8,128)(2,1)} %copy.58), calls=%async_computation | async-start | bytes 1048576 | tf_op jit(solution)/shard_map/all_to_all | solution.py:187
  74.1 22.1 %collective-permute-done.6 = bf16[256,3840]{1,0:T(8,128)(2,1)} collective-permute-done((bf16[256,3840]{1,0:T(8,128)(2,1)}, bf16[256,3840]{1,0:T(8,128)(2,1)}, u32[]{:S(2)}, u32[]{:S(2)}) %collective-permute-start.6) | collective-permute-done | bytes 1966112 | tf_op jit(solution)/shard_map/ppermute | solution.py:164
  98.8 4.5 collective-permute-start
  104.3 46.5 %all-to-all-done = bf16[1,64,8,512]{3,1,0,2:T(8,128)(2,1)S(1)} async-done(((bf16[1,64,8,512]{3,1,0,2:T(8,128)(2,1)}), bf16[1,64,8,512]{3,1,0,2:T(8,128)(2,1)S(1)}, u32[]{:S(2)}, u32[]{:S(2)}) %all-to-all-start) | async-done | bytes 524320 | tf_op jit(solution)/shard_map/all_to_all | solution.py:187
  163.2 4.2 constant_dynamic-update-slice_fusion.3
  168.0 4.2 constant_dynamic-update-slice_fusion
  172.2 15.7 %all-gather.3.cloned.1.call-done = bf16[32,1,64,1,512]{4,2,3,1,0:T(8,128)(2,1)} async-done(((bf16[8,1,64,1,512]{4,2,3,1,0:T(8,128)(2,1)}), bf16[32,1,64,1,512]{4,2,3,1,0:T(8,128)(2,1)}) %all-gather.3.cloned.1.call-update) | async-done | bytes 2097168 | tf_op jit(solution)/shard_map/all_gather | solution.py:190
  187.9 3.6 gather_fusion
  191.5 3.2 broadcast_select_fusion
  194.7 4.0 copy.64.refs_0_
  198.7 12.5 %gradient_adam.4 = (f32[512,3840]{1,0:T(8,128)}, f32[512,3840]{1,0:T(8,128)}, f32[512,3840]{1,0:T(8,128)}, f32[512,3840]{1,0:T(8,128)}, bf16[128,3840]{1,0:T(8,128)(2,1)S(1)}) custom-call(bf16[512,2048]{1,0:T(8,128)(2,1)} %copy.64.refs_0_, bf16[256,3840]{1,0:T(8,128)(2,1)S(1)} %copy-done, bf16[256,3840]{1,0:T(8,128)(2,1)} %collective-permute-done.refs_2_, ...), custom_call_target="tpu_custom_call" | custom-call | flops 2013265920 | bytes 30474240 | tf_op jit(solution)/shard_map/gradient_adam/pallas_call | solution.py:131
  211.1 12.8 %gradient_adam.5 = (f32[512,3840]{1,0:T(8,128)}, f32[512,3840]{1,0:T(8,128)}, f32[512,3840]{1,0:T(8,128)}, f32[512,3840]{1,0:T(8,128)}, bf16[128,3840]{1,0:T(8,128)(2,1)}) custom-call(bf16[512,2048]{1,0:T(8,128)(2,1)} %copy.64.refs_0_, bf16[256,3840]{1,0:T(8,128)(2,1)S(1)} %copy-done, ...), custom_call_target="tpu_custom_call", output_to_operand_aliasing={{0}: (12, {}), {1}: (13, {}), {2}: (14, {}), {3}: (15, {})} | custom-call | flops 2013265920 | bytes 30474240 | tf_op jit(solution)/shard_map/gradient_adam/pallas_call | solution.py:131
  223.9 12.9 %gradient_adam.6 = (f32[512,3840]{1,0:T(8,128)}, f32[512,3840]{1,0:T(8,128)}, f32[512,3840]{1,0:T(8,128)}, f32[512,3840]{1,0:T(8,128)}, bf16[128,3840]{1,0:T(8,128)(2,1)}) custom-call(bf16[512,2048]{1,0:T(8,128)(2,1)} %copy.64.refs_0_, bf16[256,3840]{1,0:T(8,128)(2,1)S(1)} %copy-done, ...), custom_call_target="tpu_custom_call", output_to_operand_aliasing={{0}: (12, {}), {1}: (13, {}), {2}: (14, {}), {3}: (15, {})} | custom-call | flops 2013265920 | bytes 30474240 | tf_op jit(solution)/shard_map/gradient_adam/pallas_call | solution.py:131
  236.8 12.5 %gradient_adam.7 = (f32[512,3840]{1,0:T(8,128)}, f32[512,3840]{1,0:T(8,128)}, f32[512,3840]{1,0:T(8,128)}, f32[512,3840]{1,0:T(8,128)}, bf16[128,3840]{1,0:T(8,128)(2,1)S(1)}) custom-call(bf16[512,2048]{1,0:T(8,128)(2,1)} %copy.64.refs_0_, ...), custom_call_target="tpu_custom_call", output_to_operand_aliasing={{0}: (12, {}), {1}: (13, {}), {2}: (14, {}), {3}: (15, {})} | custom-call | flops 2013265920 | bytes 30474240 | tf_op jit(solution)/shard_map/gradient_adam/pallas_call | solution.py:131
  249.6 4.0 collective-permute-start.24
  255.8 5.4 %convolution_convert_fusion.2 = bf16[1024,128]{1,0:T(8,128)(2,1)S(1)} fusion(bf16[1024,3840]{1,0:T(8,128)(2,1)} %constant_dynamic-update-slice_fusion, bf16[128,3840]{1,0:T(8,128)(2,1)S(1)} %get-tuple-element.44), kind=kOutput, calls=%fused_computation.6 | convolution fusion | flops 1006764032 | bytes 9109504 | tf_op jit(solution)/shard_map/dot_general | solution.py:150
  261.3 5.6 %convolution_convert_fusion.8 = bf16[1024,128]{1,0:T(8,128)(2,1)S(1)} fusion(bf16[1024,3840]{1,0:T(8,128)(2,1)} %constant_dynamic-update-slice_fusion, bf16[128,3840]{1,0:T(8,128)(2,1)} %get-tuple-element.43), kind=kOutput, calls=%fused_computation.12 | convolution fusion | flops 1006764032 | bytes 9109504 | tf_op jit(solution)/shard_map/dot_general | solution.py:150
  266.9 5.8 %convolution_convert_fusion.14 = bf16[1024,128]{1,0:T(8,128)(2,1)S(1)} fusion(bf16[1024,3840]{1,0:T(8,128)(2,1)} %constant_dynamic-update-slice_fusion, bf16[128,3840]{1,0:T(8,128)(2,1)} %get-tuple-element.42), kind=kOutput, calls=%fused_computation.18 | convolution fusion | flops 1006764032 | bytes 9109504 | tf_op jit(solution)/shard_map/dot_general | solution.py:150
  272.7 5.6 %convolution_convert_fusion.20 = bf16[1024,128]{1,0:T(8,128)(2,1)S(1)} fusion(bf16[1024,3840]{1,0:T(8,128)(2,1)} %constant_dynamic-update-slice_fusion, bf16[128,3840]{1,0:T(8,128)(2,1)S(1)} %get-tuple-element.41), kind=kOutput, calls=%fused_computation.24 | convolution fusion | flops 1006764032 | bytes 9109504 | tf_op jit(solution)/shard_map/dot_general | solution.py:150
  284.1 8.3 %convolution_convert_fusion.3 = bf16[1024,128]{1,0:T(8,128)(2,1)S(1)} fusion(bf16[1024,3840]{1,0:T(8,128)(2,1)} %constant_dynamic-update-slice_fusion, bf16[128,3840]{1,0:T(8,128)(2,1)S(1)} %collective-permute-done.25), kind=kOutput, calls=%fused_computation.7 | convolution fusion | flops 1006764032 | bytes 9109504 | tf_op jit(solution)/shard_map/dot_general | solution.py:150
  292.4 24.5 %collective-permute-done.26 = bf16[128,3840]{1,0:T(8,128)(2,1)S(1)} collective-permute-done((bf16[128,3840]{1,0:T(8,128)(2,1)S(1)}, bf16[128,3840]{1,0:T(8,128)(2,1)S(1)}, u32[]{:S(2)}, u32[]{:S(2)}) %collective-permute-start.26) | collective-permute-done | bytes 983072 | tf_op jit(solution)/shard_map/ppermute | solution.py:164
  320.0 5.4 %convolution_convert_fusion.4 = bf16[1024,128]{1,0:T(8,128)(2,1)S(1)} fusion(bf16[1024,3840]{1,0:T(8,128)(2,1)} %constant_dynamic-update-slice_fusion, bf16[128,3840]{1,0:T(8,128)(2,1)S(1)} %collective-permute-done.26), kind=kOutput, calls=%fused_computation.8 | convolution fusion | flops 1006764032 | bytes 9109504 | tf_op jit(solution)/shard_map/dot_general | solution.py:150
  330.2 6.1 %select_dynamic-update-slice_fusion.7 = (bf16[8192,128]{1,0:T(8,128)(2,1)}, bf16[1024,128]{1,0:T(8,128)(2,1)S(1)}) fusion(pred[]{:T(512)S(6)} %eq.33, bf16[1024,128]{1,0:T(8,128)(2,1)S(1)} %convolution_convert_fusion.4, pred[]{:T(512)S(6)} %eq.34, bf16[1024,128]{1,0:T(8,128)(2,1)S(1)} %convolution_convert_fusion.3, ...), kind=kOutput, calls=%fused_computation.44 | convolution fusion | flops 1007157248 | bytes 10158082 | tf_op jit(solution)/shard_map/dot_general | solution.py:150
  344.2 5.8 %convolution_convert_fusion.9 = bf16[1024,128]{1,0:T(8,128)(2,1)S(1)} fusion(bf16[1024,3840]{1,0:T(8,128)(2,1)} %constant_dynamic-update-slice_fusion, bf16[128,3840]{1,0:T(8,128)(2,1)} %collective-permute-done.21), kind=kOutput, calls=%fused_computation.13 | convolution fusion | flops 1006764032 | bytes 9109504 | tf_op jit(solution)/shard_map/dot_general | solution.py:150
  350.0 3.3 collective-permute-start.10
  353.3 8.6 %collective-permute-done.22 = bf16[128,3840]{1,0:T(8,128)(2,1)} collective-permute-done((bf16[128,3840]{1,0:T(8,128)(2,1)}, bf16[128,3840]{1,0:T(8,128)(2,1)}, u32[]{:S(2)}, u32[]{:S(2)}) %collective-permute-start.22) | collective-permute-done | bytes 983072 | tf_op jit(solution)/shard_map/ppermute | solution.py:164
  364.6 5.7 %convolution_convert_fusion.10 = bf16[1024,128]{1,0:T(8,128)(2,1)S(1)} fusion(bf16[1024,3840]{1,0:T(8,128)(2,1)} %constant_dynamic-update-slice_fusion, bf16[128,3840]{1,0:T(8,128)(2,1)} %collective-permute-done.22), kind=kOutput, calls=%fused_computation.14 | convolution fusion | flops 1006764032 | bytes 9109504 | tf_op jit(solution)/shard_map/dot_general | solution.py:150
  370.3 3.4 convolution_convert_fusion.6
  373.7 6.4 %select_dynamic-update-slice_fusion.15 = (bf16[8192,128]{1,0:T(8,128)(2,1)}, bf16[1024,128]{1,0:T(8,128)(2,1)S(1)}) fusion(pred[]{:T(512)S(6)} %eq.33, bf16[1024,128]{1,0:T(8,128)(2,1)S(1)} %convolution_convert_fusion.10, pred[]{:T(512)S(6)} %eq.34, bf16[1024,128]{1,0:T(8,128)(2,1)S(1)} %convolution_convert_fusion.9, ...), kind=kOutput, calls=%fused_computation.52 | convolution fusion | flops 1007157248 | bytes 10158082 | tf_op jit(solution)/shard_map/dot_general | solution.py:150
  380.1 4.1 select_dynamic-update-slice_fusion.14
  389.2 5.8 %convolution_convert_fusion.15 = bf16[1024,128]{1,0:T(8,128)(2,1)S(1)} fusion(bf16[1024,3840]{1,0:T(8,128)(2,1)} %constant_dynamic-update-slice_fusion, bf16[128,3840]{1,0:T(8,128)(2,1)} %collective-permute-done.17), kind=kOutput, calls=%fused_computation.19 | convolution fusion | flops 1006764032 | bytes 9109504 | tf_op jit(solution)/shard_map/dot_general | solution.py:150
  398.2 5.9 %collective-permute-done.18 = bf16[128,3840]{1,0:T(8,128)(2,1)} collective-permute-done((bf16[128,3840]{1,0:T(8,128)(2,1)}, bf16[128,3840]{1,0:T(8,128)(2,1)}, u32[]{:S(2)}, u32[]{:S(2)}) %collective-permute-start.18) | collective-permute-done | bytes 983072 | tf_op jit(solution)/shard_map/ppermute | solution.py:164
  404.0 5.9 %convolution_convert_fusion.16 = bf16[1024,128]{1,0:T(8,128)(2,1)S(1)} fusion(bf16[1024,3840]{1,0:T(8,128)(2,1)} %constant_dynamic-update-slice_fusion, bf16[128,3840]{1,0:T(8,128)(2,1)} %collective-permute-done.18), kind=kOutput, calls=%fused_computation.20 | convolution fusion | flops 1006764032 | bytes 9109504 | tf_op jit(solution)/shard_map/dot_general | solution.py:150
  410.0 3.4 convolution_convert_fusion.12
  413.4 6.4 %select_dynamic-update-slice_fusion.23 = (bf16[8192,128]{1,0:T(8,128)(2,1)}, bf16[1024,128]{1,0:T(8,128)(2,1)S(1)}) fusion(pred[]{:T(512)S(6)} %eq.33, bf16[1024,128]{1,0:T(8,128)(2,1)S(1)} %convolution_convert_fusion.16, pred[]{:T(512)S(6)} %eq.34, bf16[1024,128]{1,0:T(8,128)(2,1)S(1)} %convolution_convert_fusion.15, ...), kind=kOutput, calls=%fused_computation.60 | convolution fusion | flops 1007157248 | bytes 10158082 | tf_op jit(solution)/shard_map/dot_general | solution.py:150
  419.8 4.1 select_dynamic-update-slice_fusion.22
  428.9 5.6 %convolution_convert_fusion.21 = bf16[1024,128]{1,0:T(8,128)(2,1)S(1)} fusion(bf16[1024,3840]{1,0:T(8,128)(2,1)} %constant_dynamic-update-slice_fusion, bf16[128,3840]{1,0:T(8,128)(2,1)S(1)} %collective-permute-done.11), kind=kOutput, calls=%fused_computation.25 | convolution fusion | flops 1006764032 | bytes 9109504 | tf_op jit(solution)/shard_map/dot_general | solution.py:150
  434.5 5.8 %convolution_convert_fusion.22 = bf16[1024,128]{1,0:T(8,128)(2,1)S(1)} fusion(bf16[1024,3840]{1,0:T(8,128)(2,1)} %constant_dynamic-update-slice_fusion, bf16[128,3840]{1,0:T(8,128)(2,1)} %collective-permute-done.12), kind=kOutput, calls=%fused_computation.26 | convolution fusion | flops 1006764032 | bytes 9109504 | tf_op jit(solution)/shard_map/dot_general | solution.py:150
  440.3 3.4 convolution_convert_fusion.18
  443.7 5.9 %select_dynamic-update-slice_fusion.31 = (bf16[8192,128]{1,0:T(8,128)(2,1)S(1)}, bf16[1024,128]{1,0:T(8,128)(2,1)S(1)}) fusion(pred[]{:T(512)S(6)} %eq.33, bf16[1024,128]{1,0:T(8,128)(2,1)S(1)} %convolution_convert_fusion.22, pred[]{:T(512)S(6)} %eq.34, bf16[1024,128]{1,0:T(8,128)(2,1)S(1)} %convolution_convert_fusion.21, ...), kind=kOutput, calls=%fused_computation.68 | convolution fusion | flops 1007157248 | bytes 10158082 | tf_op jit(solution)/shard_map/dot_general | solution.py:150
  449.6 3.5 select_dynamic-update-slice_fusion.30
  460.2 7.3 %reduce-scatter.7.cloned.1.call-done = bf16[2048,128]{1,0:T(8,128)(2,1)} async-done(((bf16[8192,128]{1,0:T(8,128)(2,1)}), bf16[2048,128]{1,0:T(8,128)(2,1)}) %reduce-scatter.7.cloned.1.call-update) | async-done | bytes 524304 | tf_op jit(solution)/shard_map/reduce_scatter | solution.py:216
  470.7 35.1 %reduce-scatter.5.cloned.1.call-done = bf16[2048,128]{1,0:T(8,128)(2,1)} async-done(((bf16[8192,128]{1,0:T(8,128)(2,1)}), bf16[2048,128]{1,0:T(8,128)(2,1)}) %reduce-scatter.5.cloned.1.call-update) | async-done | bytes 524304 | tf_op jit(solution)/shard_map/reduce_scatter | solution.py:216
  509.2 4.7 collective-permute-done.15
  (157 shorter events, 81.6 us)
Async XLA Ops:
  7.2 44.1 %collective-permute-start.1 = (bf16[256,3840]{1,0:T(8,128)(2,1)}, bf16[256,3840]{1,0:T(8,128)(2,1)}, u32[]{:S(2)}, u32[]{:S(2)}) collective-permute-start(bf16[256,3840]{1,0:T(8,128)(2,1)} %refs_1_.7), channel_id=1, source_target_pairs={{0,8},{4,12},{8,0},{12,4},{16,24},{20,28},{24,16},{28,20},{1,9},{5... | collective-permute-start | bytes 5898248 | tf_op jit(solution)/shard_map/ppermute | solution.py:164
  7.4 50.8 %collective-permute-start.3 = (bf16[256,3840]{1,0:T(8,128)(2,1)}, bf16[256,3840]{1,0:T(8,128)(2,1)}, u32[]{:S(2)}, u32[]{:S(2)}) collective-permute-start(bf16[256,3840]{1,0:T(8,128)(2,1)} %refs_1_.7), channel_id=1, source_target_pairs={{8,16},{12,20},{16,8},{20,12},{9,17},{13,21},{17,9},{21,13},{10,18... | collective-permute-start | bytes 5898248 | tf_op jit(solution)/shard_map/ppermute | solution.py:164
  51.2 45.0 %collective-permute-start.6 = (bf16[256,3840]{1,0:T(8,128)(2,1)}, bf16[256,3840]{1,0:T(8,128)(2,1)}, u32[]{:S(2)}, u32[]{:S(2)}) collective-permute-start(bf16[256,3840]{1,0:T(8,128)(2,1)} %collective-permute-done.1.refs_3_), channel_id=1, source_target_pairs={{8,16},{12,20},{16,8},{20,12},{9,17},{13,21},{17,9},{21,13},{10,18... | collective-permute-start | bytes 5898248 | tf_op jit(solution)/shard_map/ppermute | solution.py:164
  54.4 106.6 %collective-permute-start.13 = (bf16[512,3840]{1,0:T(8,128)(2,1)}, bf16[512,3840]{1,0:T(8,128)(2,1)}, u32[]{:S(2)}, u32[]{:S(2)}) collective-permute-start(bf16[512,3840]{1,0:T(8,128)(2,1)} %param.18), channel_id=1, source_target_pairs={{0,8},{4,12},{24,16},{28,20},{1,9},{5,13},{25,17},{29,21},{2,10},{... | collective-permute-start | bytes 11796488 | tf_op jit(solution)/shard_map/ppermute | solution.py:164
  58.2 93.5 %collective-permute-start.4 = (bf16[256,3840]{1,0:T(8,128)(2,1)}, bf16[256,3840]{1,0:T(8,128)(2,1)}, u32[]{:S(2)}, u32[]{:S(2)}) collective-permute-start(bf16[256,3840]{1,0:T(8,128)(2,1)} %collective-permute-done.3), channel_id=1, source_target_pairs={{8,0},{12,4},{16,24},{20,28},{9,1},{13,5},{17,25},{21,29},{10,2},{... | collective-permute-start | bytes 5898248 | tf_op jit(solution)/shard_map/ppermute | solution.py:164
  66.3 32.5 %copy-start = (bf16[256,3840]{1,0:T(8,128)(2,1)S(1)}, bf16[256,3840]{1,0:T(8,128)(2,1)}, u32[]{:S(2)}) copy-start(bf16[256,3840]{1,0:T(8,128)(2,1)} %refs_1_.7) | copy-start | bytes 5898244
  68.7 82.1 %all-to-all-start = ((bf16[1,64,8,512]{3,1,0,2:T(8,128)(2,1)}), bf16[1,64,8,512]{3,1,0,2:T(8,128)(2,1)S(1)}, u32[]{:S(2)}, u32[]{:S(2)}) async-start(bf16[1,64,8,512]{3,1,0,2:T(8,128)(2,1)} %copy.58), calls=%async_computation | async-start | bytes 1048576 | tf_op jit(solution)/shard_map/all_to_all | solution.py:187
  74.1 113.9 %all-gather.3.cloned.1.call-start = ((), (), s32[]{:S(2)}) async-start(), calls=%async_computation.9 | async-start | bytes 2621440 | tf_op jit(solution)/shard_map/all_gather | solution.py:190
  96.2 60.0 %collective-permute-start.7 = (bf16[256,3840]{1,0:T(8,128)(2,1)}, bf16[256,3840]{1,0:T(8,128)(2,1)}, u32[]{:S(2)}, u32[]{:S(2)}) collective-permute-start(bf16[256,3840]{1,0:T(8,128)(2,1)} %collective-permute-done.6), channel_id=1, source_target_pairs={{8,0},{12,4},{16,24},{20,28},{9,1},{13,5},{17,25},{21,29},{10,2},{... | collective-permute-start | bytes 5898248 | tf_op jit(solution)/shard_map/ppermute | solution.py:164
  98.8 99.9 %collective-permute-start = (bf16[256,3840]{1,0:T(8,128)(2,1)S(1)}, bf16[256,3840]{1,0:T(8,128)(2,1)}, u32[]{:S(2)}, u32[]{:S(2)}) collective-permute-start(bf16[256,3840]{1,0:T(8,128)(2,1)S(1)} %copy-done), channel_id=1, source_target_pairs={{0,4},{4,0},{8,12},{12,8},{16,20},{20,16},{24,28},{28,24},{1,5},{5... | collective-permute-start | bytes 5898248 | tf_op jit(solution)/shard_map/ppermute | solution.py:164
  103.3 64.2 %collective-permute-start.9 = (bf16[512,3840]{1,0:T(8,128)(2,1)}, bf16[512,3840]{1,0:T(8,128)(2,1)}, u32[]{:S(2)}, u32[]{:S(2)}) collective-permute-start(bf16[512,3840]{1,0:T(8,128)(2,1)} %param.18), channel_id=1, source_target_pairs={{0,4},{4,0},{8,12},{12,8},{16,20},{20,16},{24,28},{28,24},{1,5},{5... | collective-permute-start | bytes 11796488 | tf_op jit(solution)/shard_map/ppermute | solution.py:164
  151.7 303.8 %reduce-scatter.11.cloned.1.call-start = ((), (), s32[]{:S(2)}) async-start(), calls=%async_computation.8 | async-start | bytes 2621440 | tf_op jit(solution)/shard_map/reduce_scatter | solution.py:216
  151.7 46.9 %collective-permute-start.2 = (bf16[256,3840]{1,0:T(8,128)(2,1)}, bf16[256,3840]{1,0:T(8,128)(2,1)}, u32[]{:S(2)}, u32[]{:S(2)}) collective-permute-start(bf16[256,3840]{1,0:T(8,128)(2,1)} %collective-permute-done.1.refs_3_), channel_id=1, source_target_pairs={{0,4},{4,0},{8,12},{12,8},{16,20},{20,16},{24,28},{28,24},{1,5},{5... | collective-permute-start | bytes 5898248 | tf_op jit(solution)/shard_map/ppermute | solution.py:164
  156.2 42.4 %collective-permute-start.5 = (bf16[256,3840]{1,0:T(8,128)(2,1)}, bf16[256,3840]{1,0:T(8,128)(2,1)}, u32[]{:S(2)}, u32[]{:S(2)}) collective-permute-start(bf16[256,3840]{1,0:T(8,128)(2,1)} %broadcast_select_fusion.2.refs_5_), channel_id=1, source_target_pairs={{0,4},{4,0},{8,12},{12,8},{16,20},{20,16},{24,28},{28,24},{1,5},{5... | collective-permute-start | bytes 5898248 | tf_op jit(solution)/shard_map/ppermute | solution.py:164
  161.1 37.6 %collective-permute-start.8 = (bf16[256,3840]{1,0:T(8,128)(2,1)}, bf16[256,3840]{1,0:T(8,128)(2,1)}, u32[]{:S(2)}, u32[]{:S(2)}) collective-permute-start(bf16[256,3840]{1,0:T(8,128)(2,1)} %broadcast_select_fusion.1.refs_7_), channel_id=1, source_target_pairs={{0,4},{4,0},{8,12},{12,8},{16,20},{20,16},{24,28},{28,24},{1,5},{5... | collective-permute-start | bytes 5898248 | tf_op jit(solution)/shard_map/ppermute | solution.py:164
  167.5 110.8 %collective-permute-start.14 = (bf16[512,3840]{1,0:T(8,128)(2,1)}, bf16[512,3840]{1,0:T(8,128)(2,1)}, u32[]{:S(2)}, u32[]{:S(2)}) collective-permute-start(bf16[512,3840]{1,0:T(8,128)(2,1)} %collective-permute-done.13), channel_id=1, source_target_pairs={{0,4},{4,0},{8,12},{12,8},{16,20},{20,16},{24,28},{28,24},{1,5},{5... | collective-permute-start | bytes 11796488 | tf_op jit(solution)/shard_map/ppermute | solution.py:164
  249.3 30.2 %collective-permute-start.25 = (bf16[128,3840]{1,0:T(8,128)(2,1)S(1)}, bf16[128,3840]{1,0:T(8,128)(2,1)S(1)}, u32[]{:S(2)}, u32[]{:S(2)}) collective-permute-start(bf16[128,3840]{1,0:T(8,128)(2,1)S(1)} %get-tuple-element.44), channel_id=1, source_target_pairs={{0,8},{4,12},{8,0},{12,4},{16,24},{20,28},{24,16},{28,20},{1,9},{5... | collective-permute-start | bytes 2949128 | tf_op jit(solution)/shard_map/ppermute | solution.py:164
  249.6 78.0 %collective-permute-start.24 = (bf16[128,3840]{1,0:T(8,128)(2,1)S(1)}, bf16[128,3840]{1,0:T(8,128)(2,1)S(1)}, u32[]{:S(2)}, u32[]{:S(2)}) collective-permute-start(bf16[128,3840]{1,0:T(8,128)(2,1)S(1)} %get-tuple-element.44), channel_id=1, source_target_pairs={{8,16},{12,20},{16,8},{20,12},{9,17},{13,21},{17,9},{21,13},{10,18... | collective-permute-start | bytes 2949128 | tf_op jit(solution)/shard_map/ppermute | solution.py:164
  253.7 74.0 %collective-permute-start.21 = (bf16[128,3840]{1,0:T(8,128)(2,1)}, bf16[128,3840]{1,0:T(8,128)(2,1)}, u32[]{:S(2)}, u32[]{:S(2)}) collective-permute-start(bf16[128,3840]{1,0:T(8,128)(2,1)} %get-tuple-element.43), channel_id=1, source_target_pairs={{0,8},{4,12},{8,0},{12,4},{16,24},{20,28},{24,16},{28,20},{1,9},{5... | collective-permute-start | bytes 2949128 | tf_op jit(solution)/shard_map/ppermute | solution.py:164
  253.7 120.0 %collective-permute-start.20 = (bf16[128,3840]{1,0:T(8,128)(2,1)}, bf16[128,3840]{1,0:T(8,128)(2,1)}, u32[]{:S(2)}, u32[]{:S(2)}) collective-permute-start(bf16[128,3840]{1,0:T(8,128)(2,1)} %get-tuple-element.43), channel_id=1, source_target_pairs={{8,16},{12,20},{16,8},{20,12},{9,17},{13,21},{17,9},{21,13},{10,18... | collective-permute-start | bytes 2949128 | tf_op jit(solution)/shard_map/ppermute | solution.py:164
  266.9 14.8 %slice-start = ((s8[7864320]{0:T(1024)(128)(4,1)}), s8[4194304]{0:T(1024)(128)(4,1)S(1)}, s32[]{:S(2)}) async-start(s8[7864320]{0:T(1024)(128)(4,1)} %bitcast.72), calls=%async_computation.10 | async-start | bytes 8388608
  272.7 9.1 %slice-start.1 = ((s8[7864320]{0:T(1024)(128)(4,1)}), s8[3670016]{0:T(1024)(128)(4,1)S(1)}, s32[]{:S(2)}) async-start(s8[7864320]{0:T(1024)(128)(4,1)} %bitcast.72), calls=%async_computation.11 | async-start | bytes 7340032
  278.3 71.7 %collective-permute-start.17 = (bf16[128,3840]{1,0:T(8,128)(2,1)}, bf16[128,3840]{1,0:T(8,128)(2,1)}, u32[]{:S(2)}, u32[]{:S(2)}) collective-permute-start(bf16[128,3840]{1,0:T(8,128)(2,1)} %get-tuple-element.42), channel_id=1, source_target_pairs={{0,8},{4,12},{8,0},{12,4},{16,24},{20,28},{24,16},{28,20},{1,9},{5... | collective-permute-start | bytes 2949128 | tf_op jit(solution)/shard_map/ppermute | solution.py:164
  279.5 37.4 %collective-permute-start.26 = (bf16[128,3840]{1,0:T(8,128)(2,1)S(1)}, bf16[128,3840]{1,0:T(8,128)(2,1)S(1)}, u32[]{:S(2)}, u32[]{:S(2)}) collective-permute-start(bf16[128,3840]{1,0:T(8,128)(2,1)S(1)} %collective-permute-done.25), channel_id=1, source_target_pairs={{8,16},{12,20},{16,8},{20,12},{9,17},{13,21},{17,9},{21,13},{10,18... | collective-permute-start | bytes 2949128 | tf_op jit(solution)/shard_map/ppermute | solution.py:164
  284.1 52.2 %copy-start.4 = (bf16[1024,3840]{1,0:T(8,128)(2,1)}, bf16[1024,3840]{1,0:T(8,128)(2,1)S(1)}, u32[]{:S(2)}) copy-start(bf16[1024,3840]{1,0:T(8,128)(2,1)S(1)} %constant_dynamic-update-slice_fusion.2) | copy-start | bytes 23592964
  316.9 96.5 %collective-permute-start.16 = (bf16[128,3840]{1,0:T(8,128)(2,1)}, bf16[128,3840]{1,0:T(8,128)(2,1)}, u32[]{:S(2)}, u32[]{:S(2)}) collective-permute-start(bf16[128,3840]{1,0:T(8,128)(2,1)} %get-tuple-element.42), channel_id=1, source_target_pairs={{8,16},{12,20},{16,8},{20,12},{9,17},{13,21},{17,9},{21,13},{10,18... | collective-permute-start | bytes 2949128 | tf_op jit(solution)/shard_map/ppermute | solution.py:164
  327.6 67.4 %collective-permute-start.11 = (bf16[128,3840]{1,0:T(8,128)(2,1)S(1)}, bf16[128,3840]{1,0:T(8,128)(2,1)S(1)}, u32[]{:S(2)}, u32[]{:S(2)}) collective-permute-start(bf16[128,3840]{1,0:T(8,128)(2,1)S(1)} %get-tuple-element.41), channel_id=1, source_target_pairs={{0,8},{4,12},{8,0},{12,4},{16,24},{20,28},{24,16},{28,20},{1,9},{5... | collective-permute-start | bytes 2949128 | tf_op jit(solution)/shard_map/ppermute | solution.py:164
  327.7 34.2 %collective-permute-start.22 = (bf16[128,3840]{1,0:T(8,128)(2,1)}, bf16[128,3840]{1,0:T(8,128)(2,1)}, u32[]{:S(2)}, u32[]{:S(2)}) collective-permute-start(bf16[128,3840]{1,0:T(8,128)(2,1)} %collective-permute-done.21), channel_id=1, source_target_pairs={{8,16},{12,20},{16,8},{20,12},{9,17},{13,21},{17,9},{21,13},{10,18... | collective-permute-start | bytes 2949128 | tf_op jit(solution)/shard_map/ppermute | solution.py:164
  344.1 113.7 %reduce-scatter.9.cloned.1.call-start = ((), (), s32[]{:S(2)}) async-start(), calls=%async_computation.7 | async-start | bytes 2621440 | tf_op jit(solution)/shard_map/reduce_scatter | solution.py:216
  344.2 26.1 %slice-start.2 = ((s8[7864320]{0:T(1024)(128)(4,1)}), s8[4194304]{0:T(1024)(128)(4,1)S(1)}, s32[]{:S(2)}) async-start(s8[7864320]{0:T(1024)(128)(4,1)} %bitcast.74), calls=%async_computation.12 | async-start | bytes 8388608
  350.0 20.3 %slice-start.3 = ((s8[7864320]{0:T(1024)(128)(4,1)}), s8[3670016]{0:T(1024)(128)(4,1)S(1)}, s32[]{:S(2)}) async-start(s8[7864320]{0:T(1024)(128)(4,1)} %bitcast.74), calls=%async_computation.13 | async-start | bytes 7340032
  350.0 93.7 %collective-permute-start.10 = (bf16[128,3840]{1,0:T(8,128)(2,1)S(1)}, bf16[128,3840]{1,0:T(8,128)(2,1)}, u32[]{:S(2)}, u32[]{:S(2)}) collective-permute-start(bf16[128,3840]{1,0:T(8,128)(2,1)S(1)} %get-tuple-element.41), channel_id=1, source_target_pairs={{8,16},{12,20},{16,8},{20,12},{9,17},{13,21},{17,9},{21,13},{10,18... | collective-permute-start | bytes 2949128 | tf_op jit(solution)/shard_map/ppermute | solution.py:164
  361.9 42.1 %collective-permute-start.18 = (bf16[128,3840]{1,0:T(8,128)(2,1)}, bf16[128,3840]{1,0:T(8,128)(2,1)}, u32[]{:S(2)}, u32[]{:S(2)}) collective-permute-start(bf16[128,3840]{1,0:T(8,128)(2,1)} %collective-permute-done.17), channel_id=1, source_target_pairs={{8,16},{12,20},{16,8},{20,12},{9,17},{13,21},{17,9},{21,13},{10,18... | collective-permute-start | bytes 2949128 | tf_op jit(solution)/shard_map/ppermute | solution.py:164
  389.2 78.3 %reduce-scatter.7.cloned.1.call-start = ((), (), s32[]{:S(2)}) async-start(), calls=%async_computation.6 | async-start | bytes 2621440 | tf_op jit(solution)/shard_map/reduce_scatter | solution.py:216
  389.2 20.7 %slice-start.4 = ((s8[7864320]{0:T(1024)(128)(4,1)}), s8[4194304]{0:T(1024)(128)(4,1)S(1)}, s32[]{:S(2)}) async-start(s8[7864320]{0:T(1024)(128)(4,1)} %bitcast.76), calls=%async_computation.14 | async-start | bytes 8388608
  395.0 14.9 %slice-start.5 = ((s8[7864320]{0:T(1024)(128)(4,1)}), s8[3670016]{0:T(1024)(128)(4,1)S(1)}, s32[]{:S(2)}) async-start(s8[7864320]{0:T(1024)(128)(4,1)} %bitcast.76), calls=%async_computation.15 | async-start | bytes 7340032
  395.0 39.4 %collective-permute-start.12 = (bf16[128,3840]{1,0:T(8,128)(2,1)S(1)}, bf16[128,3840]{1,0:T(8,128)(2,1)}, u32[]{:S(2)}, u32[]{:S(2)}) collective-permute-start(bf16[128,3840]{1,0:T(8,128)(2,1)S(1)} %collective-permute-done.11), channel_id=1, source_target_pairs={{8,16},{12,20},{16,8},{20,12},{9,17},{13,21},{17,9},{21,13},{10,18... | collective-permute-start | bytes 2949128 | tf_op jit(solution)/shard_map/ppermute | solution.py:164
  428.8 77.0 %reduce-scatter.5.cloned.1.call-start = ((), (), s32[]{:S(2)}) async-start(), calls=%async_computation.5 | async-start | bytes 2621440 | tf_op jit(solution)/shard_map/reduce_scatter | solution.py:216
  428.9 11.4 %slice-start.6 = ((s8[7864320]{0:T(1024)(128)(4,1)}), s8[4194304]{0:T(1024)(128)(4,1)S(1)}, s32[]{:S(2)}) async-start(s8[7864320]{0:T(1024)(128)(4,1)} %bitcast.78), calls=%async_computation.16 | async-start | bytes 8388608
  455.5 53.6 %copy-start.5 = (bf16[2048,128]{1,0:T(8,128)(2,1)S(1)}, bf16[2048,128]{1,0:T(8,128)(2,1)}, u32[]{:S(2)}) copy-start(bf16[2048,128]{1,0:T(8,128)(2,1)} %reduce-scatter.11.cloned.1.call-done) | copy-start | bytes 1572868
  456.5 52.5 %collective-permute-start.27 = (bf16[1024,128]{1,0:T(8,128)(2,1)S(1)}, bf16[1024,128]{1,0:T(8,128)(2,1)S(1)}, u32[]{:S(2)}, u32[]{:S(2)}) collective-permute-start(bf16[1024,128]{1,0:T(8,128)(2,1)S(1)} %slice.57), channel_id=1, source_target_pairs={{8,0},{12,4},{16,24},{20,28},{9,1},{13,5},{17,25},{21,29},{10,2},{... | collective-permute-start | bytes 786440 | tf_op jit(solution)/shard_map/ppermute | solution.py:164
  457.9 51.3 %copy-start.6 = (bf16[2048,128]{1,0:T(8,128)(2,1)S(1)}, bf16[2048,128]{1,0:T(8,128)(2,1)}, u32[]{:S(2)}) copy-start(bf16[2048,128]{1,0:T(8,128)(2,1)} %reduce-scatter.9.cloned.1.call-done) | copy-start | bytes 1572868
  458.9 50.2 %collective-permute-start.23 = (bf16[1024,128]{1,0:T(8,128)(2,1)S(1)}, bf16[1024,128]{1,0:T(8,128)(2,1)S(1)}, u32[]{:S(2)}, u32[]{:S(2)}) collective-permute-start(bf16[1024,128]{1,0:T(8,128)(2,1)S(1)} %slice.55), channel_id=1, source_target_pairs={{8,0},{12,4},{16,24},{20,28},{9,1},{13,5},{17,25},{21,29},{10,2},{... | collective-permute-start | bytes 786440 | tf_op jit(solution)/shard_map/ppermute | solution.py:164
  467.5 41.7 %copy-start.7 = (bf16[2048,128]{1,0:T(8,128)(2,1)S(1)}, bf16[2048,128]{1,0:T(8,128)(2,1)}, u32[]{:S(2)}) copy-start(bf16[2048,128]{1,0:T(8,128)(2,1)} %reduce-scatter.7.cloned.1.call-done) | copy-start | bytes 1572868
  468.5 40.6 %collective-permute-start.19 = (bf16[1024,128]{1,0:T(8,128)(2,1)S(1)}, bf16[1024,128]{1,0:T(8,128)(2,1)S(1)}, u32[]{:S(2)}, u32[]{:S(2)}) collective-permute-start(bf16[1024,128]{1,0:T(8,128)(2,1)S(1)} %slice.53), channel_id=1, source_target_pairs={{8,0},{12,4},{16,24},{20,28},{9,1},{13,5},{17,25},{21,29},{10,2},{... | collective-permute-start | bytes 786440 | tf_op jit(solution)/shard_map/ppermute | solution.py:164
  505.8 8.1 %copy-start.8 = (bf16[2048,128]{1,0:T(8,128)(2,1)S(1)}, bf16[2048,128]{1,0:T(8,128)(2,1)}, u32[]{:S(2)}) copy-start(bf16[2048,128]{1,0:T(8,128)(2,1)} %reduce-scatter.5.cloned.1.call-done) | copy-start | bytes 1572868
  506.9 7.1 %collective-permute-start.15 = (bf16[1024,128]{1,0:T(8,128)(2,1)S(1)}, bf16[1024,128]{1,0:T(8,128)(2,1)S(1)}, u32[]{:S(2)}, u32[]{:S(2)}) collective-permute-start(bf16[1024,128]{1,0:T(8,128)(2,1)S(1)} %slice.51), channel_id=1, source_target_pairs={{8,0},{12,4},{16,24},{20,28},{9,1},{13,5},{17,25},{21,29},{10,2},{... | collective-permute-start | bytes 786440 | tf_op jit(solution)/shard_map/ppermute | solution.py:164
  514.2 3.2 collective-permute-start.28
  (4 other events, 12.8 us)
Sparse Core Ops, SparseCore 0:
  151.8 36.1 all-gather.2
  344.3 35.9 reduce-scatter.10
  389.3 38.4 reduce-scatter.8
  430.6 36.8 reduce-scatter.6
  470.6 35.2 reduce-scatter.4

commit v2 on v1

--- a/solution.py
+++ b/solution.py
@@ -18,7 +18,7 @@
 adam_eps = 1e-08
 rate_learn = 0.001
 
-ROW_CHUNKS = 4
+ROW_CHUNKS = 2
 
 
 def row_factors(ratios, pair_row, lengths):
@@ -82,14 +82,25 @@
 MIDDLE = planes([(1, 2), (2, 1)])
 OUTWARD = planes([(1, 0), (2, 3)])
 INWARD = planes([(0, 1), (3, 2)])
+
+
+def homeward(pairs, core):
+    return [
+        ((2 * a + core) * 4 + 2 * y + x, (2 * b + y) * 4 + 2 * (a // 2) + x)
+        for a, b in pairs
+        for y in (0, 1)
+        for x in (0, 1)
+    ]
+
+
 CORES = [(2 * z + core, 2 * z + 1 - core) for z in range(4) for core in (0, 1)]
 
 
-def step_kernel(n_act, has_prior, *refs):
+def step_kernel(n_act, skip, *refs):
     scaled_ref = refs[0]
     acts = refs[1 : 1 + n_act]
     master_ref, moment_ref, second_ref = refs[1 + n_act : 4 + n_act]
-    outs = refs[4 + n_act + (4 if has_prior else 0) :]
+    outs = refs[4 + n_act + skip :]
     tokens = acts[0].shape[0]
     grad = None
     for i, act in enumerate(acts):
@@ -109,7 +120,7 @@
     outs[4][...] = new_master.astype(jnp.bfloat16)
 
 
-def step_rows(r, scaled_t, acts, master, moment, second, prior):
+def step_rows(r, scaled_t, acts, master, moment, second, prior, behind):
     rows_all, cols = master.shape
     rows = rows_all // ROW_CHUNKS
     tokens = acts[0].shape[0]
@@ -127,23 +138,25 @@
             aliases[len(operands)] = i
             operands.append(array)
             in_specs.append(pl.BlockSpec(memory_space=pl.ANY))
+    for array in behind:
+        operands.append(array)
+        in_specs.append(pl.BlockSpec(memory_space=pl.ANY))
     full = jax.ShapeDtypeStruct((rows_all, cols), jnp.float32)
     outs = pl.pallas_call(
-        functools.partial(step_kernel, len(acts), prior is not None),
+        functools.partial(step_kernel, len(acts), len(operands) - 4 - len(acts)),
         grid=(cols // tile,),
         in_specs=in_specs,
         out_specs=[state] * 4 + [pl.BlockSpec((rows, tile), lambda t: (0, t))],
         out_shape=[full] * 4 + [jax.ShapeDtypeStruct((rows, cols), jnp.bfloat16)],
         input_output_aliases=aliases,
-        compiler_params=pltpu.CompilerParams(vmem_limit_bytes=48 * 1024 * 1024),
-        cost_estimate=pl.CostEstimate(
-            flops=2 * rows * cols * tokens * len(acts),
-            bytes_accessed=2 * tokens * len(acts) * cols + 30 * rows * cols,
-            transcendentals=rows * cols,
-        ),
+        compiler_params=pltpu.CompilerParams(vmem_limit_bytes=60 * 1024 * 1024),
+        cost_estimate=SMALL,
         name="gradient_adam",
     )(*operands)
     return outs[:4], outs[4]
+
+
+SMALL = pl.CostEstimate(flops=1000, bytes_accessed=1000, transcendentals=0)
 
 
 def times(tokens, rows):
@@ -152,16 +165,81 @@
     ).astype(jnp.bfloat16)
 
 
-def by_plane(parts, z):
-    odd, high = (z & 1) == 1, (z & 2) == 2
-    a = [jnp.where(odd, parts[i ^ 1], parts[i]) for i in range(4)]
-    return [jnp.where(high, a[i ^ 2], a[i]) for i in range(4)]
+def product_kernel(x_first, n_weights, tiles, place_ref, mine_ref, other_ref, *refs):
+    weights = refs[:n_weights]
+    out_ref, all_ref = refs[-2:]
+    rows = weights[0].shape[0]
+    step = pl.program_id(0)
+
+    @pl.when(step == 0)
+    def _():
+        for i, ref in enumerate(weights):
+            all_ref[i * rows : (i + 1) * rows] = ref[...]
+
+    def store(tokens_ref):
+        out = times(tokens_ref[...], all_ref[...])
+        give = place_ref[0]
+        half = out.shape[1] // 2
+        for at, block in ((give, out[:, :half]), (1 - give, out[:, half:])):
+            if x_first:
+                out_ref[at, 0] = block
+            else:
+                out_ref[0, at] = block
+
+    pl.when(step < tiles)(functools.partial(store, mine_ref))
+    pl.when(step >= tiles)(functools.partial(store, other_ref))
+
+
+def products(place, x_first, tokens, weights, behind=()):
+    count, cols = tokens[0].shape
+    rows = weights[0].shape[0]
+    features = rows * len(weights) // 2
+    tile = 256
+    tiles = count // tile
+
+    def out_map(t, place):
+        y = jnp.where(t < tiles, place[1], 1 - place[1])
+        return (0, y, t % tiles, 0) if x_first else (y, 0, t % tiles, 0)
+
+    in_specs = [
+        pl.BlockSpec((tile, cols), lambda t, place: (jnp.minimum(t, tiles - 1), 0)),
+        pl.BlockSpec((tile, cols), lambda t, place: (jnp.maximum(t - tiles, 0), 0)),
+    ]
+    in_specs += [pl.BlockSpec((rows, cols), lambda t, place: (0, 0))] * len(weights)
+    in_specs += [pl.BlockSpec(memory_space=pl.ANY)] * len(behind)
+    return pl.pallas_call(
+        functools.partial(product_kernel, x_first, len(weights), tiles),
+        grid_spec=pltpu.PrefetchScalarGridSpec(
+            num_scalar_prefetch=1,
+            grid=(2 * tiles,),
+            in_specs=in_specs,
+            out_specs=pl.BlockSpec(
+                (2, 1, tile, features) if x_first else (1, 2, tile, features), out_map
+            ),
+            scratch_shapes=[pltpu.VMEM((rows * len(weights), cols), jnp.bfloat16)],
+        ),
+        out_shape=jax.ShapeDtypeStruct((2, 2, count, features), jnp.bfloat16),
+        compiler_params=pltpu.CompilerParams(vmem_limit_bytes=60 * 1024 * 1024),
+        cost_estimate=SMALL,
+        name="product",
+    )(place, *tokens, *weights, *behind)
+
+
+def add_up(stack, x_first, behind=None):
+    for step in ((1, 2) if x_first else (2, 1)):
+        given = lax.ppermute(stack[1], "tensor", [(i, i ^ step) for i in range(4)])
+        if behind is not None:
+            given, behind = lax.optimization_barrier((given, behind))
+        stack = (stack[0].astype(jnp.float32) + given.astype(jnp.float32)).astype(jnp.bfloat16)
+    return stack
 
 
 def body_planes(
     out_grad, hidden_act, log_ratio, pair_order, seq_len, master, moment, second, next_act
 ):
     send = lambda array, pairs: lax.ppermute(array, "dp", pairs)
+    after = lax.optimization_barrier
+    send_all = lambda array, pairs: lax.ppermute(array, ("dp", "tensor"), pairs)
     k = lax.axis_index("dp")
     j = lax.axis_index("tensor")
     z, core = k // 2, k % 2
@@ -172,59 +250,91 @@
 
     pair_act = send(hidden_act, PAIR)
     middle_act = send(hidden_act, MIDDLE)
+
+    scaled = scale_rows(out_grad, log_ratio, pair_order, seq_len)
+    share = tokens // 4
+    width = model // 4
+    part = lax.dynamic_slice_in_dim(scaled, j * share, share, 0)
+    pieces = [lax.dynamic_slice_in_dim(part, (z ^ d) * width, width, 1) for d in range(4)]
+    for d in (1, 2, 3):
+        pieces[d] = send(pieces[d], planes([(p, p ^ d) for p in range(4)]))
+
+    pair_act, middle_act, own_act, own_next, pieces = after(
+        (pair_act, middle_act, hidden_act, next_act, pieces)
+    )
     forward_act = send(pair_act, MIDDLE)
     far_one = send(middle_act, OUTWARD)
+    rows = next_act.shape[0] // 2
+    next_inward = [send(own_next[:rows], INWARD), send(own_next[rows:], INWARD)]
+    pieces = [
+        pieces[0],
+        pieces[1],
+        jnp.where(inner, pieces[3], pieces[2]),
+        jnp.where(inner, pieces[2], pieces[3]),
+    ]
+    pieces = jnp.stack(pieces)
+    half = width // 2
+    keep = lax.dynamic_slice_in_dim(pieces, core * half, half, 2)
+    give = lax.dynamic_slice_in_dim(pieces, (1 - core) * half, half, 2)
+    part = jnp.stack([keep, send(give, CORES)], axis=1).reshape(1, 8, share, half)
+    x, y = j % 2, j // 2
+    given = lax.ppermute(part, "tensor", [(i, i ^ 1) for i in range(4)])
+    part = jnp.concatenate([jnp.where(x == 0, part, given), jnp.where(x == 0, given, part)], 0)
+    given = lax.ppermute(part, "tensor", [(i, i ^ 2) for i in range(4)])
+    own_swap = send(own_act, CORES)
+    pair_act, own_swap = after((pair_act, own_swap))
+    pair_swap = send(pair_act, CORES)
+
+    forward_act, far_one, middle_act, own_next, pair_swap, part, next_inward[0] = after(
+        (forward_act, far_one, middle_act, own_next, pair_swap, part, next_inward[0])
+    )
     far_two = send(forward_act, OUTWARD)
+    next_middle = send(own_next, MIDDLE)
+    whole = jnp.concatenate([jnp.where(y == 0, part, given), jnp.where(y == 0, given, part)], 0)
+    scaled_t = whole.transpose(3, 1, 0, 2).reshape(half, 8 * tokens)
     third = jnp.where(inner, middle_act, far_one)
+    third_swap = send(third, CORES)
+    own_next, third_swap = after((own_next, third_swap))
+    next_own = [next_act, send(own_next, CORES)]
     fourth = jnp.where(inner, forward_act, far_two)
-    acts = []
-    for act in (hidden_act, pair_act, third, fourth):
-        acts += [act, send(act, CORES)]
-
-    scaled = scale_rows(out_grad, log_ratio, pair_order, seq_len)
-    share = tokens // 4
-    part = lax.dynamic_slice_in_dim(scaled, j * share, share, 0)
-    part = lax.all_to_all(
-        part.reshape(share, 8, model // 8), "dp", split_axis=1, concat_axis=0, tiled=False
-    )
-    whole = lax.all_gather(part, "tensor", axis=0, tiled=False)
-    order = jnp.array(
-        [[0, 1, 2, 3], [1, 0, 2, 3], [2, 3, 1, 0], [3, 2, 1, 0]], dtype=jnp.int32
-    )[z]
-    order = jnp.stack([order * 2 + core, order * 2 + 1 - core], axis=1).reshape(8)
-    whole = jnp.take(whole, order, axis=1)
-    scaled_t = whole.transpose(3, 1, 0, 2).reshape(model // 8, 8 * tokens)
-
-    next_two = jnp.concatenate([next_act, send(next_act, CORES)], axis=0)
-    next_pair = send(next_act, INWARD)
-    next_pair = jnp.concatenate([next_pair, send(next_pair, CORES)], axis=0)
-
-    rows = rows_all // ROW_CHUNKS
-    prior = None
-    sums = []
-    for r in range(ROW_CHUNKS):
-        prior, own = step_rows(r, scaled_t, acts, master, moment, second, prior)
-        pair = send(own, PAIR)
-        middle = send(own, MIDDLE)
-        forward = send(pair, MIDDLE)
-        product = [times(next_two, block) for block in (own, pair, forward, middle)]
-        zero = jnp.zeros_like(product[0])
-        other = [zero, zero] + [times(next_pair, block) for block in (forward, middle)]
-        stack = []
-        for a, b in zip(by_plane(product, z), by_plane(other, z)):
-            stack += [a, b]
-        total = lax.psum_scatter(
-            jnp.concatenate(stack, axis=0), "tensor", scatter_dimension=0, tiled=True
+    fourth_swap = send(fourth, CORES)
+    acts = [hidden_act, own_swap, pair_act, pair_swap, third, third_swap, fourth, fourth_swap]
+
+    behind = [next_own[1], next_inward[1]]
+    prior, own_one = step_rows(0, scaled_t, acts, master, moment, second, None, behind)
+    pair_one = send(own_one, PAIR)
+    next_inward, _ = after((next_inward, own_one))
+    next_far = [send(array, MIDDLE) for array in next_inward]
+    prior, own_two = step_rows(1, scaled_t, acts, master, moment, second, prior, [next_middle])
+    pair_two = send(own_two, PAIR)
+
+    place = jnp.stack([(z & 1) ^ x, core ^ y])
+    next_middle, _ = after((next_middle, own_two))
+    next_middle = [next_middle, send(next_middle, CORES)]
+    one, two = (own_one, pair_one), (own_two, pair_two)
+    near_one = products(place, True, next_own, one)
+    middle_one = products(place, False, next_middle, one, [near_one])
+    near_two = products(place, True, next_own, two, [middle_one])
+    middle_two = products(place, False, next_middle, two, [near_two])
+    next_far, _ = after((next_far, own_two))
+    next_far = [[array, send(array, CORES)] for array in next_far]
+    both = (own_one, own_two, pair_one, pair_two)
+    far_one = products(place, True, next_far[0], both, [middle_two])
+    far_two = products(place, False, next_far[1], both, [far_one])
+    near = [add_up(near_one, True, middle_one), add_up(near_two, True, middle_two)]
+    middle = [add_up(middle_one, False), add_up(middle_two, False, far_one)]
+    far = [add_up(far_one, True, far_two), add_up(far_two, False)]
+    near, middle = jnp.concatenate(near, axis=1), jnp.concatenate(middle, axis=1)
+    far = jnp.concatenate(far, axis=0)
+
+    parts = []
+    for side in (0, 1):
+        parts.append(
+            send_all(near, homeward([(p, p) for p in range(4)], side))
+            + send_all(middle, homeward([(1, 2), (2, 1)], side))
+            + send_all(far, homeward([(1, 3), (2, 0)], side))
         )
-        count = next_two.shape[0]
-        sums.append(total[:count] + send(total[count:], OUTWARD))
-    columns = jnp.concatenate(sums, axis=1)
-    half = columns.shape[0] // 2
-    mine, theirs = columns[:half], send(columns[half:], CORES)
-    next_out = jnp.concatenate(
-        [jnp.where(core == 0, mine, theirs), jnp.where(core == 0, theirs, mine)], axis=1
-    )
-    return (*prior, next_out)
+    return (*prior, jnp.concatenate(parts, axis=1))
 
 
 def solution(mesh):

time: 536 us -> 459 us (0.86)
  matrix products: 122 us -> 0 us
  Pallas kernels: 50.6 us -> 104 us
  waiting for transfers between devices: 212 us -> 250 us
  between operations: 14.9 us -> 1.23 us
  other arithmetic: 30.2 us -> 16.8 us
  local copies, waits for them, and re-layouts: 30 us -> 17.9 us
    dot_general x24 -> x0, matrix products: 122 us -> none  [times(): lax.dot_general(tokens, rows, (((1,), (1,)), ((), ())), preferred_element...]
    ppermute x29 -> x24, waiting for transfers between devices: 107 us -> 191 us  [body_planes(): send = lambda array, pairs: lax.ppermute(array, 'dp', pairs)]
    ppermute x0 -> x20, waiting for transfers between devices: none -> 59.3 us  [the longest x1 24.7 us: body_planes(): given = lax.ppermute(part, 'tensor', [(i, i ^ 2) for i in range(4)])]
    pallas_call x4 -> x8, Pallas kernels: 50.6 us -> 104 us  [the longest x6 64 us: products(): pl.pallas_call(functools.partial(product_kernel, x_first, len(weights), t...]
    all_to_all x1 -> x0, waiting for transfers between devices: 46.5 us -> none  [body_planes(): lax.all_to_all(part.reshape(share, 8, model // 8), 'dp', split_axis=1, co...]
    reduce_scatter x4 -> x0, waiting for transfers between devices: 42.4 us -> none  [body_planes(): lax.psum_scatter(jnp.concatenate(stack, axis=0), 'tensor', scatter_dimens...]
    ppermute x0 -> x20, starting transfers between devices: none -> 26.2 us  [the longest x6 15.1 us: body_planes(): send_all = lambda array, pairs: lax.ppermute(array, ('dp', 'tensor'), pairs)]
    ppermute x29 -> x24, starting transfers between devices: 60.3 us -> 34.3 us  [body_planes(): send = lambda array, pairs: lax.ppermute(array, 'dp', pairs)]
  transfers between devices with their start and end apart: 35 -> 44, of which waited for: 11 -> 19; matrix products, arithmetic and copies ran while one was open for 34% -> 6% of each run, Pallas kernels for 10% -> 19%
where the time goes in v2:
time: 459 us; the launch traced here: 451 us
  waiting for transfers between devices  250 us (54%)
  Pallas kernels  104 us (23%)
  starting transfers between devices  60.6 us (13%)
  local copies, waits for them, and re-layouts  17.9 us (4%)
  other arithmetic  16.8 us (4%)
    ppermute x24, waiting for transfers between devices, body_planes(): send = lambda array, pairs: lax.ppermute(array, 'dp', pairs)  191 us
    pallas_call x6, Pallas kernels, products(): pl.pallas_call(functools.partial(product_kernel, x_first, len(weights), t...  64 us
    pallas_call x2, Pallas kernels, step_rows(): pl.pallas_call(functools.partial(step_kernel, len(acts), len(operands) -...  40.1 us
    ppermute x24, starting transfers between devices, body_planes(): send = lambda array, pairs: lax.ppermute(array, 'dp', pairs)  34.3 us
    ppermute x1, waiting for transfers between devices, body_planes(): given = lax.ppermute(part, 'tensor', [(i, i ^ 2) for i in range(4)])  24.7 us
    ppermute x6, starting transfers between devices, body_planes(): send_all = lambda array, pairs: lax.ppermute(array, ('dp', 'tensor'), pairs)  15.1 us
    ppermute x6, waiting for transfers between devices, body_planes(): send_all = lambda array, pairs: lax.ppermute(array, ('dp', 'tensor'), pairs)  13.4 us
    ppermute x1, waiting for transfers between devices, body_planes(): given = lax.ppermute(part, 'tensor', [(i, i ^ 1) for i in range(4)])  12.1 us
  transfers between devices with their start and end apart: 44, of which 19 were waited for; matrix products, arithmetic and copies ran while one was open for 6% of the time, Pallas kernels for 19%

profile of v2, /device:TPU:13, one launch (start us, length us, event | category | flops | bytes accessed | tf_op | source)
XLA Modules:
  0.0 450.8 jit_solution(12973237418428253467)
XLA Ops:
  0.6 3.2 collective-permute-start.1
  7.2 2.3 multiply_convert_fusion
  9.9 1.3 collective-permute-start.4
  11.2 2.3 collective-permute-start.3
  13.4 40.3 %collective-permute-done.4 = bf16[64,1024]{1,0:T(8,128)(2,1)S(1)} collective-permute-done((bf16[64,1024]{1,0:T(8,128)(2,1)S(1)}, bf16[64,1024]{1,0:T(8,128)(2,1)S(1)}, u32[]{:S(2)}, u32[]{:S(2)}) %collective-permute-start.4) | collective-permute-done | bytes 131104 | tf_op jit(solution)/shard_map/ppermute | solution.py:240
  53.7 3.0 collective-permute-done.3
  56.8 1.6 collective-permute-start.7
  58.4 2.4 collective-permute-start.5
  60.9 4.8 %collective-permute-start.6 = (bf16[256,3840]{1,0:T(8,128)(2,1)}, bf16[256,3840]{1,0:T(8,128)(2,1)}, u32[]{:S(2)}, u32[]{:S(2)}) collective-permute-start(bf16[256,3840]{1,0:T(8,128)(2,1)} %collective-permute-done.1), channel_id=1, source_target_pairs={{8,0},{12,4},{16,24},{20,28},{9,1},{13,5},{17,25},{21,29},{10,2},{... | collective-permute-start | bytes 5898248 | tf_op jit(solution)/shard_map/ppermute | solution.py:240
  65.7 4.3 fusion.13
  73.3 3.6 collective-permute-done.9
  78.3 12.1 %collective-permute-done.10 = bf16[1,8,64,512]{3,2,1,0:T(8,128)(2,1)S(1)} collective-permute-done((bf16[1,8,64,512]{3,2,1,0:T(8,128)(2,1)S(1)}, bf16[1,8,64,512]{3,2,1,0:T(8,128)(2,1)S(1)}, u32[]{:S(2)}, u32[]{:S(2)}) %collective-permute-start.10) | collective-permute-done | bytes 524320 | tf_op jit(solution)/shard_map/ppermute | solution.py:281
  90.6 14.3 %collective-permute-done.5 = bf16[256,3840]{1,0:T(8,128)(2,1)} collective-permute-done((bf16[256,3840]{1,0:T(8,128)(2,1)S(1)}, bf16[256,3840]{1,0:T(8,128)(2,1)}, u32[]{:S(2)}, u32[]{:S(2)}) %collective-permute-start.5) | collective-permute-done | bytes 1966112 | tf_op jit(solution)/shard_map/ppermute | solution.py:240
  104.8 2.0 collective-permute-done.6
  106.9 9.4 %collective-permute-done.11 = bf16[256,3840]{1,0:T(8,128)(2,1)} collective-permute-done((bf16[256,3840]{1,0:T(8,128)(2,1)}, bf16[256,3840]{1,0:T(8,128)(2,1)}, u32[]{:S(2)}, u32[]{:S(2)}) %collective-permute-start.11) | collective-permute-done | bytes 1966112 | tf_op jit(solution)/shard_map/ppermute | solution.py:240
  116.3 1.8 broadcast_select_fusion.1.refs_5_
  119.3 1.4 collective-permute-start.14
  120.7 2.2 collective-permute-done.13.refs_6_
  122.9 1.3 copy-done.11
  124.6 3.2 collective-permute-start.18
  127.8 1.3 collective-permute-start.17
  129.1 34.1 %collective-permute-done.14 = bf16[256,3840]{1,0:T(8,128)(2,1)S(1)} collective-permute-done((bf16[256,3840]{1,0:T(8,128)(2,1)}, bf16[256,3840]{1,0:T(8,128)(2,1)S(1)}, u32[]{:S(2)}, u32[]{:S(2)}) %collective-permute-start.14) | collective-permute-done | bytes 1966112 | tf_op jit(solution)/shard_map/ppermute | solution.py:240
  163.2 3.1 broadcast_select_fusion.refs_7_
  167.2 24.7 %collective-permute-done.12 = bf16[2,8,64,512]{3,2,1,0:T(8,128)(2,1)S(1)} collective-permute-done((bf16[2,8,64,512]{3,2,1,0:T(8,128)(2,1)S(1)}, bf16[2,8,64,512]{3,2,1,0:T(8,128)(2,1)S(1)}, u32[]{:S(2)}, u32[]{:S(2)}) %collective-permute-start.12) | collective-permute-done | bytes 1048608 | tf_op jit(solution)/shard_map/ppermute | solution.py:283
  192.3 2.5 copy.23.refs_0_
  194.8 20.1 %gradient_adam.2 = (f32[512,3840]{1,0:T(8,128)}, f32[512,3840]{1,0:T(8,128)}, f32[512,3840]{1,0:T(8,128)}, f32[512,3840]{1,0:T(8,128)}, bf16[256,3840]{1,0:T(8,128)(2,1)}) custom-call(bf16[512,2048]{1,0:T(8,128)(2,1)} %copy.23.refs_0_, bf16[256,3840]{1,0:T(8,128)(2,1)} %refs_1_.3, bf16[256,3840]{1,0:T(8,128)(2,1)} %copy-done.10, ...), custom_call_target="tpu_custom_call" | custom-call | flops 1000 | bytes 1000 | tf_op jit(solution)/shard_map/gradient_adam/pallas_call | solution.py:145
  214.9 20.0 %gradient_adam.3 = (f32[512,3840]{1,0:T(8,128)}, f32[512,3840]{1,0:T(8,128)}, f32[512,3840]{1,0:T(8,128)}, f32[512,3840]{1,0:T(8,128)}, bf16[256,3840]{1,0:T(8,128)(2,1)}) custom-call(bf16[512,2048]{1,0:T(8,128)(2,1)} %copy.23.refs_0_, bf16[256,3840]{1,0:T(8,128)(2,1)} %refs_1_.3, ...), custom_call_target="tpu_custom_call", output_to_operand_aliasing={{0}: (12, {}), {1}: (13, {}), {2}: (14, {}), {3}: (15, {})} | custom-call | flops 1000 | bytes 1000 | tf_op jit(solution)/shard_map/gradient_adam/pallas_call | solution.py:145
  235.6 3.2 collective-permute-start.30
  238.8 2.1 collective-permute-start.31
  241.0 1.5 collective-permute-start.23
  242.5 39.8 %collective-permute-done.30.mine_ref = bf16[256,3840]{1,0:T(8,128)(2,1)} collective-permute-done((bf16[256,3840]{1,0:T(8,128)(2,1)}, bf16[256,3840]{1,0:T(8,128)(2,1)}, u32[]{:S(2)}, u32[]{:S(2)}) %collective-permute-start.30) | collective-permute-done | bytes 1966112 | tf_op jit(solution)/shard_map/ppermute | solution.py:240
  282.3 42.1 %collective-permute-done.31.mine_ref = bf16[256,3840]{1,0:T(8,128)(2,1)} collective-permute-done((bf16[256,3840]{1,0:T(8,128)(2,1)}, bf16[256,3840]{1,0:T(8,128)(2,1)}, u32[]{:S(2)}, u32[]{:S(2)}) %collective-permute-start.31) | collective-permute-done | bytes 1966112 | tf_op jit(solution)/shard_map/ppermute | solution.py:240
  325.8 10.5 %product.6.refs_2_ = bf16[2,2,512,256]{3,2,1,0:T(8,128)(2,1)} custom-call(s32[2]{0:T(128)} %pad_add_fusion.place_ref, bf16[512,3840]{1,0:T(8,128)(2,1)} %mine_ref.3, bf16[512,3840]{1,0:T(8,128)(2,1)} %collective-permute-done.16.refs_12_.other_ref, bf16[256,3840]{1,0:T(8,128)(2,1)} %get-tuple-element.69.refs_0_, ...), custom_call_target="tpu_custom_call" | custom-call | flops 1000 | bytes 1000 | tf_op jit(solution)/shard_map/product/pallas_call | solution.py:210
  339.0 10.4 %product.7.refs_2_ = bf16[2,2,512,256]{3,2,1,0:T(8,128)(2,1)} custom-call(s32[2]{0:T(128)} %pad_add_fusion.place_ref, bf16[512,3840]{1,0:T(8,128)(2,1)} %collective-permute-done.18.refs_16_.mine_ref, bf16[512,3840]{1,0:T(8,128)(2,1)} %collective-permute-done.21.other_ref, bf16[256,3840]{1,0:T(8,128)(2,1)} %get-tuple-element.69.refs_0_, ...), custom_call_target="tpu_custom_call" | custom-call | flops 1000 | bytes 1000 | tf_op jit(solution)/shard_map/product/pallas_call | solution.py:210
  349.4 1.7 collective-permute-done.20
  352.2 10.5 %product.8.refs_2_ = bf16[2,2,512,256]{3,2,1,0:T(8,128)(2,1)} custom-call(s32[2]{0:T(128)} %pad_add_fusion.place_ref, bf16[512,3840]{1,0:T(8,128)(2,1)} %mine_ref.3, bf16[512,3840]{1,0:T(8,128)(2,1)} %collective-permute-done.16.refs_12_.other_ref, bf16[256,3840]{1,0:T(8,128)(2,1)} %get-tuple-element.70.refs_0_.refs_1_, ...), custom_call_target="tpu_custom_call" | custom-call | flops 1000 | bytes 1000 | tf_op jit(solution)/shard_map/product/pallas_call | solution.py:210
  364.7 10.4 %product.9.refs_4_ = bf16[2,2,512,256]{3,2,1,0:T(8,128)(2,1)} custom-call(s32[2]{0:T(128)} %pad_add_fusion.place_ref, bf16[512,3840]{1,0:T(8,128)(2,1)} %collective-permute-done.18.refs_16_.mine_ref, bf16[512,3840]{1,0:T(8,128)(2,1)} %collective-permute-done.21.other_ref, bf16[256,3840]{1,0:T(8,128)(2,1)} %get-tuple-element.70.refs_0_.refs_1_, ...), custom_call_target="tpu_custom_call" | custom-call | flops 1000 | bytes 1000 | tf_op jit(solution)/shard_map/product/pallas_call | solution.py:210
  375.0 11.1 %product.10.refs_4_ = bf16[2,2,256,512]{3,2,1,0:T(8,128)(2,1)} custom-call(s32[2]{0:T(128)} %pad_add_fusion.place_ref, bf16[256,3840]{1,0:T(8,128)(2,1)} %collective-permute-done.30.mine_ref, bf16[256,3840]{1,0:T(8,128)(2,1)} %collective-permute-done.32.other_ref, bf16[256,3840]{1,0:T(8,128)(2,1)} %get-tuple-element.69.refs_0_, ...), custom_call_target="tpu_custom_call" | custom-call | flops 1000 | bytes 1000 | tf_op jit(solution)/shard_map/product/pallas_call | solution.py:210
  390.5 11.2 %product.11 = bf16[2,2,256,512]{3,2,1,0:T(8,128)(2,1)} custom-call(s32[2]{0:T(128)} %pad_add_fusion.place_ref, bf16[256,3840]{1,0:T(8,128)(2,1)} %collective-permute-done.31.mine_ref, bf16[256,3840]{1,0:T(8,128)(2,1)} %collective-permute-done.36.other_ref, bf16[256,3840]{1,0:T(8,128)(2,1)} %get-tuple-element.69.refs_0_, ...), custom_call_target="tpu_custom_call" | custom-call | flops 1000 | bytes 1000 | tf_op jit(solution)/shard_map/product/pallas_call | solution.py:210
  405.1 1.3 collective-permute-start.28
  409.6 2.5 collective-permute-done.35
  415.8 4.1 collective-permute-done.25
  419.9 2.7 collective-permute-start.41
  423.5 8.3 %collective-permute-start.42 = (bf16[512,512]{1,0:T(8,128)(2,1)S(1)}, bf16[512,512]{1,0:T(8,128)(2,1)S(1)}, u32[]{:S(2)}, u32[]{:S(2)}) collective-permute-start(bf16[512,512]{1,0:T(8,128)(2,1)S(1)} %pad_maximum_fusion.5), channel_id=1, source_target_pairs={{12,16},{13,17},{14,20},{15,21},{20,10},{21,11},{22,14},{23,15}} | collective-permute-start | bytes 1572872 | tf_op jit(solution)/shard_map/ppermute | solution.py:242
  432.0 1.3 collective-permute-start.43
  434.1 1.3 collective-permute-start.34
  436.1 2.2 collective-permute-done.42
  438.3 11.2 %collective-permute-done.43 = bf16[512,512]{1,0:T(8,128)(2,1)S(1)} collective-permute-done((bf16[512,512]{1,0:T(8,128)(2,1)S(1)}, bf16[512,512]{1,0:T(8,128)(2,1)S(1)}, u32[]{:S(2)}, u32[]{:S(2)}) %collective-permute-start.43) | collective-permute-done | bytes 524320 | tf_op jit(solution)/shard_map/ppermute | solution.py:242
  (127 shorter events, 37.6 us)
Async XLA Ops:
  0.6 56.1 %collective-permute-start.1 = (bf16[256,3840]{1,0:T(8,128)(2,1)}, bf16[256,3840]{1,0:T(8,128)(2,1)}, u32[]{:S(2)}, u32[]{:S(2)}) collective-permute-start(bf16[256,3840]{1,0:T(8,128)(2,1)} %refs_1_.3), channel_id=1, source_target_pairs={{8,16},{12,20},{16,8},{20,12},{9,17},{13,21},{17,9},{21,13},{10,18... | collective-permute-start | bytes 5898248 | tf_op jit(solution)/shard_map/ppermute | solution.py:240
  3.8 52.9 %collective-permute-start = (bf16[256,3840]{1,0:T(8,128)(2,1)}, bf16[256,3840]{1,0:T(8,128)(2,1)S(1)}, u32[]{:S(2)}, u32[]{:S(2)}) collective-permute-start(bf16[256,3840]{1,0:T(8,128)(2,1)} %refs_1_.3), channel_id=1, source_target_pairs={{0,8},{4,12},{8,0},{12,4},{16,24},{20,28},{24,16},{28,20},{1,9},{5... | collective-permute-start | bytes 5898248 | tf_op jit(solution)/shard_map/ppermute | solution.py:240
  7.2 49.5 %copy-start.8 = (bf16[256,3840]{1,0:T(8,128)(2,1)S(1)}, bf16[256,3840]{1,0:T(8,128)(2,1)}, u32[]{:S(2)}) copy-start(bf16[256,3840]{1,0:T(8,128)(2,1)} %refs_1_.3) | copy-start | bytes 5898244
  9.9 43.8 %collective-permute-start.4 = (bf16[64,1024]{1,0:T(8,128)(2,1)S(1)}, bf16[64,1024]{1,0:T(8,128)(2,1)S(1)}, u32[]{:S(2)}, u32[]{:S(2)}) collective-permute-start(bf16[64,1024]{1,0:T(8,128)(2,1)S(1)} %get-tuple-element.87), channel_id=1, source_target_pairs={{0,24},{4,28},{8,16},{12,20},{16,8},{20,12},{24,0},{28,4},{1,25},{... | collective-permute-start | bytes 393224 | tf_op jit(solution)/shard_map/ppermute | solution.py:240
  11.2 45.6 %collective-permute-start.3 = (bf16[64,1024]{1,0:T(8,128)(2,1)S(1)}, bf16[64,1024]{1,0:T(8,128)(2,1)S(1)}, u32[]{:S(2)}, u32[]{:S(2)}) collective-permute-start(bf16[64,1024]{1,0:T(8,128)(2,1)S(1)} %get-tuple-element.88), channel_id=1, source_target_pairs={{0,16},{4,20},{8,24},{12,28},{16,0},{20,4},{24,8},{28,12},{1,17},{... | collective-permute-start | bytes 393224 | tf_op jit(solution)/shard_map/ppermute | solution.py:240
  13.4 43.3 %collective-permute-start.2 = (bf16[64,1024]{1,0:T(8,128)(2,1)S(1)}, bf16[64,1024]{1,0:T(8,128)(2,1)S(1)}, u32[]{:S(2)}, u32[]{:S(2)}) collective-permute-start(bf16[64,1024]{1,0:T(8,128)(2,1)S(1)} %get-tuple-element.89), channel_id=1, source_target_pairs={{0,8},{4,12},{8,0},{12,4},{16,24},{20,28},{24,16},{28,20},{1,9},{5... | collective-permute-start | bytes 393224 | tf_op jit(solution)/shard_map/ppermute | solution.py:240
  56.8 14.5 %copy-start.9 = (bf16[256,3840]{1,0:T(8,128)(2,1)}, bf16[256,3840]{1,0:T(8,128)(2,1)S(1)}, u32[]{:S(2)}) copy-start(bf16[256,3840]{1,0:T(8,128)(2,1)S(1)} %collective-permute-done.refs_3_) | copy-start | bytes 5898244
  56.8 14.5 %collective-permute-start.7 = (bf16[256,3840]{1,0:T(8,128)(2,1)S(1)}, bf16[256,3840]{1,0:T(8,128)(2,1)S(1)}, u32[]{:S(2)}, u32[]{:S(2)}) collective-permute-start(bf16[256,3840]{1,0:T(8,128)(2,1)S(1)} %copy-done.8), channel_id=1, source_target_pairs={{0,4},{4,0},{8,12},{12,8},{16,20},{20,16},{24,28},{28,24},{1,5},{5... | collective-permute-start | bytes 5898248 | tf_op jit(solution)/shard_map/ppermute | solution.py:240
  58.4 46.4 %collective-permute-start.5 = (bf16[256,3840]{1,0:T(8,128)(2,1)S(1)}, bf16[256,3840]{1,0:T(8,128)(2,1)}, u32[]{:S(2)}, u32[]{:S(2)}) collective-permute-start(bf16[256,3840]{1,0:T(8,128)(2,1)S(1)} %collective-permute-done.refs_3_), channel_id=1, source_target_pairs={{8,16},{12,20},{16,8},{20,12},{9,17},{13,21},{17,9},{21,13},{10,18... | collective-permute-start | bytes 5898248 | tf_op jit(solution)/shard_map/ppermute | solution.py:240
  60.9 46.0 %collective-permute-start.6 = (bf16[256,3840]{1,0:T(8,128)(2,1)}, bf16[256,3840]{1,0:T(8,128)(2,1)}, u32[]{:S(2)}, u32[]{:S(2)}) collective-permute-start(bf16[256,3840]{1,0:T(8,128)(2,1)} %collective-permute-done.1), channel_id=1, source_target_pairs={{8,0},{12,4},{16,24},{20,28},{9,1},{13,5},{17,25},{21,29},{10,2},{... | collective-permute-start | bytes 5898248 | tf_op jit(solution)/shard_map/ppermute | solution.py:240
  70.0 46.3 %collective-permute-start.11 = (bf16[256,3840]{1,0:T(8,128)(2,1)}, bf16[256,3840]{1,0:T(8,128)(2,1)}, u32[]{:S(2)}, u32[]{:S(2)}) collective-permute-start(bf16[256,3840]{1,0:T(8,128)(2,1)} %get-tuple-element.84), channel_id=1, source_target_pairs={{0,8},{4,12},{24,16},{28,20},{1,9},{5,13},{25,17},{29,21},{2,10},{... | collective-permute-start | bytes 5898248 | tf_op jit(solution)/shard_map/ppermute | solution.py:240
  72.6 43.7 %collective-permute-start.8 = (bf16[256,3840]{1,0:T(8,128)(2,1)S(1)}, bf16[256,3840]{1,0:T(8,128)(2,1)}, u32[]{:S(2)}, u32[]{:S(2)}) collective-permute-start(bf16[256,3840]{1,0:T(8,128)(2,1)S(1)} %collective-permute-done.refs_3_), channel_id=1, source_target_pairs={{0,4},{4,0},{8,12},{12,8},{16,20},{20,16},{24,28},{28,24},{1,5},{5... | collective-permute-start | bytes 5898248 | tf_op jit(solution)/shard_map/ppermute | solution.py:240
  73.0 3.9 collective-permute-start.9
  77.0 13.4 %collective-permute-start.10 = (bf16[1,8,64,512]{3,2,1,0:T(8,128)(2,1)S(1)}, bf16[1,8,64,512]{3,2,1,0:T(8,128)(2,1)S(1)}, u32[]{:S(2)}, u32[]{:S(2)}) collective-permute-start(bf16[1,8,64,512]{3,2,1,0:T(8,128)(2,1)S(1)} %bitcast.104), channel_id=1, source_target_pairs={{0,1},{1,0},{2,3},{3,2},{4,5},{5,4},{6,7},{7,6},{8,9},{9,8},{10,11... | collective-permute-start | bytes 1572872 | tf_op jit(solution)/shard_map/ppermute | solution.py:281
  118.1 48.2 %copy-start.1 = (bf16[256,3840]{1,0:T(8,128)(2,1)}, bf16[256,3840]{1,0:T(8,128)(2,1)S(1)}, u32[]{:S(2)}) copy-start(bf16[256,3840]{1,0:T(8,128)(2,1)S(1)} %broadcast_select_fusion.1.refs_5_) | copy-start | bytes 5898244
  118.1 4.8 %collective-permute-start.13 = (bf16[256,3840]{1,0:T(8,128)(2,1)S(1)}, bf16[256,3840]{1,0:T(8,128)(2,1)S(1)}, u32[]{:S(2)}, u32[]{:S(2)}) collective-permute-start(bf16[256,3840]{1,0:T(8,128)(2,1)S(1)} %broadcast_select_fusion.1.refs_5_), channel_id=1, source_target_pairs={{0,4},{4,0},{8,12},{12,8},{16,20},{20,16},{24,28},{28,24},{1,5},{5... | collective-permute-start | bytes 5898248 | tf_op jit(solution)/shard_map/ppermute | solution.py:240
  119.3 43.9 %collective-permute-start.14 = (bf16[256,3840]{1,0:T(8,128)(2,1)}, bf16[256,3840]{1,0:T(8,128)(2,1)S(1)}, u32[]{:S(2)}, u32[]{:S(2)}) collective-permute-start(bf16[256,3840]{1,0:T(8,128)(2,1)} %collective-permute-done.5), channel_id=1, source_target_pairs={{8,0},{12,4},{16,24},{20,28},{9,1},{13,5},{17,25},{21,29},{10,2},{... | collective-permute-start | bytes 5898248 | tf_op jit(solution)/shard_map/ppermute | solution.py:240
  124.2 70.6 %collective-permute-start.16 = (bf16[512,3840]{1,0:T(8,128)(2,1)}, bf16[512,3840]{1,0:T(8,128)(2,1)}, u32[]{:S(2)}, u32[]{:S(2)}) collective-permute-start(bf16[512,3840]{1,0:T(8,128)(2,1)} %mine_ref.3), channel_id=1, source_target_pairs={{0,4},{4,0},{8,12},{12,8},{16,20},{20,16},{24,28},{28,24},{1,5},{5... | collective-permute-start | bytes 11796488 | tf_op jit(solution)/shard_map/ppermute | solution.py:240
  124.6 90.3 %collective-permute-start.18 = (bf16[512,3840]{1,0:T(8,128)(2,1)}, bf16[512,3840]{1,0:T(8,128)(2,1)}, u32[]{:S(2)}, u32[]{:S(2)}) collective-permute-start(bf16[512,3840]{1,0:T(8,128)(2,1)} %mine_ref.3), channel_id=1, source_target_pairs={{8,16},{12,20},{16,8},{20,12},{9,17},{13,21},{17,9},{21,13},{10,18... | collective-permute-start | bytes 11796488 | tf_op jit(solution)/shard_map/ppermute | solution.py:240
  127.8 67.0 %collective-permute-start.17 = (bf16[256,3840]{1,0:T(8,128)(2,1)}, bf16[256,3840]{1,0:T(8,128)(2,1)}, u32[]{:S(2)}, u32[]{:S(2)}) collective-permute-start(bf16[256,3840]{1,0:T(8,128)(2,1)} %get-tuple-element.83), channel_id=1, source_target_pairs={{0,8},{4,12},{24,16},{28,20},{1,9},{5,13},{25,17},{29,21},{2,10},{... | collective-permute-start | bytes 5898248 | tf_op jit(solution)/shard_map/ppermute | solution.py:240
  166.3 28.5 %collective-permute-start.15 = (bf16[256,3840]{1,0:T(8,128)(2,1)}, bf16[256,3840]{1,0:T(8,128)(2,1)}, u32[]{:S(2)}, u32[]{:S(2)}) collective-permute-start(bf16[256,3840]{1,0:T(8,128)(2,1)} %broadcast_select_fusion.refs_7_), channel_id=1, source_target_pairs={{0,4},{4,0},{8,12},{12,8},{16,20},{20,16},{24,28},{28,24},{1,5},{5... | collective-permute-start | bytes 5898248 | tf_op jit(solution)/shard_map/ppermute | solution.py:240
  167.0 24.9 %collective-permute-start.12 = (bf16[2,8,64,512]{3,2,1,0:T(8,128)(2,1)S(1)}, bf16[2,8,64,512]{3,2,1,0:T(8,128)(2,1)S(1)}, u32[]{:S(2)}, u32[]{:S(2)}) collective-permute-start(bf16[2,8,64,512]{3,2,1,0:T(8,128)(2,1)S(1)} %pad_maximum_fusion), channel_id=1, source_target_pairs={{0,2},{1,3},{2,0},{3,1},{4,6},{5,7},{6,4},{7,5},{8,10},{9,11},{10,... | collective-permute-start | bytes 3145736 | tf_op jit(solution)/shard_map/ppermute | solution.py:283
  214.9 26.0 %copy-start = (bf16[256,3840]{1,0:T(8,128)(2,1)S(1)}, bf16[256,3840]{1,0:T(8,128)(2,1)}, u32[]{:S(2)}) copy-start(bf16[256,3840]{1,0:T(8,128)(2,1)} %get-tuple-element.69.refs_0_) | copy-start | bytes 5898244
  234.9 104.1 %collective-permute-start.21 = (bf16[512,3840]{1,0:T(8,128)(2,1)}, bf16[512,3840]{1,0:T(8,128)(2,1)}, u32[]{:S(2)}, u32[]{:S(2)}) collective-permute-start(bf16[512,3840]{1,0:T(8,128)(2,1)} %collective-permute-done.18.refs_16_.mine_ref), channel_id=1, source_target_pairs={{0,4},{4,0},{8,12},{12,8},{16,20},{20,16},{24,28},{28,24},{1,5},{5... | collective-permute-start | bytes 11796488 | tf_op jit(solution)/shard_map/ppermute | solution.py:240
  235.6 46.6 %collective-permute-start.30 = (bf16[256,3840]{1,0:T(8,128)(2,1)}, bf16[256,3840]{1,0:T(8,128)(2,1)}, u32[]{:S(2)}, u32[]{:S(2)}) collective-permute-start(bf16[256,3840]{1,0:T(8,128)(2,1)} %collective-permute-done.11), channel_id=1, source_target_pairs={{8,16},{12,20},{16,8},{20,12},{9,17},{13,21},{17,9},{21,13},{10,18... | collective-permute-start | bytes 5898248 | tf_op jit(solution)/shard_map/ppermute | solution.py:240
  238.8 85.6 %collective-permute-start.31 = (bf16[256,3840]{1,0:T(8,128)(2,1)}, bf16[256,3840]{1,0:T(8,128)(2,1)}, u32[]{:S(2)}, u32[]{:S(2)}) collective-permute-start(bf16[256,3840]{1,0:T(8,128)(2,1)} %collective-permute-done.17.refs_13_), channel_id=1, source_target_pairs={{8,16},{12,20},{16,8},{20,12},{9,17},{13,21},{17,9},{21,13},{10,18... | collective-permute-start | bytes 5898248 | tf_op jit(solution)/shard_map/ppermute | solution.py:240
  240.9 84.9 %collective-permute-start.19 = (bf16[256,3840]{1,0:T(8,128)(2,1)S(1)}, bf16[256,3840]{1,0:T(8,128)(2,1)}, u32[]{:S(2)}, u32[]{:S(2)}) collective-permute-start(bf16[256,3840]{1,0:T(8,128)(2,1)S(1)} %copy-done), channel_id=1, source_target_pairs={{0,8},{4,12},{8,0},{12,4},{16,24},{20,28},{24,16},{28,20},{1,9},{5... | collective-permute-start | bytes 5898248 | tf_op jit(solution)/shard_map/ppermute | solution.py:240
  241.0 111.1 %collective-permute-start.23 = (bf16[256,3840]{1,0:T(8,128)(2,1)}, bf16[256,3840]{1,0:T(8,128)(2,1)}, u32[]{:S(2)}, u32[]{:S(2)}) collective-permute-start(bf16[256,3840]{1,0:T(8,128)(2,1)} %get-tuple-element.70.refs_0_.refs_1_), channel_id=1, source_target_pairs={{0,8},{4,12},{8,0},{12,4},{16,24},{20,28},{24,16},{28,20},{1,9},{5... | collective-permute-start | bytes 5898248 | tf_op jit(solution)/shard_map/ppermute | solution.py:240
  324.4 50.6 %collective-permute-start.32 = (bf16[256,3840]{1,0:T(8,128)(2,1)}, bf16[256,3840]{1,0:T(8,128)(2,1)}, u32[]{:S(2)}, u32[]{:S(2)}) collective-permute-start(bf16[256,3840]{1,0:T(8,128)(2,1)} %collective-permute-done.30.mine_ref), channel_id=1, source_target_pairs={{0,4},{4,0},{8,12},{12,8},{16,20},{20,16},{24,28},{28,24},{1,5},{5... | collective-permute-start | bytes 5898248 | tf_op jit(solution)/shard_map/ppermute | solution.py:240
  337.4 13.6 %collective-permute-start.20 = (bf16[2,512,256]{2,1,0:T(8,128)(2,1)S(1)}, bf16[2,512,256]{2,1,0:T(8,128)(2,1)S(1)}, u32[]{:S(2)}, u32[]{:S(2)}) collective-permute-start(bf16[2,512,256]{2,1,0:T(8,128)(2,1)S(1)} %slice_bitcast_fusion.10), channel_id=1, source_target_pairs={{0,1},{1,0},{2,3},{3,2},{4,5},{5,4},{6,7},{7,6},{8,9},{9,8},{10,11... | collective-permute-start | bytes 1572872 | tf_op jit(solution)/shard_map/ppermute | solution.py:230
  338.7 51.5 %collective-permute-start.36 = (bf16[256,3840]{1,0:T(8,128)(2,1)}, bf16[256,3840]{1,0:T(8,128)(2,1)}, u32[]{:S(2)}, u32[]{:S(2)}) collective-permute-start(bf16[256,3840]{1,0:T(8,128)(2,1)} %collective-permute-done.31.mine_ref), channel_id=1, source_target_pairs={{0,4},{4,0},{8,12},{12,8},{16,20},{20,16},{24,28},{28,24},{1,5},{5... | collective-permute-start | bytes 5898248 | tf_op jit(solution)/shard_map/ppermute | solution.py:240
  351.9 50.8 %collective-permute-start.22 = (bf16[512,256]{1,0:T(8,128)(2,1)}, bf16[512,256]{1,0:T(8,128)(2,1)S(1)}, u32[]{:S(2)}, u32[]{:S(2)}) collective-permute-start(bf16[512,256]{1,0:T(8,128)(2,1)} %slice_bitcast_fusion.22), channel_id=1, source_target_pairs={{0,2},{1,3},{2,0},{3,1},{4,6},{5,7},{6,4},{7,5},{8,10},{9,11},{10,... | collective-permute-start | bytes 786440 | tf_op jit(solution)/shard_map/ppermute | solution.py:230
  363.5 40.4 %collective-permute-start.27 = (bf16[2,512,256]{2,1,0:T(8,128)(2,1)}, bf16[2,512,256]{2,1,0:T(8,128)(2,1)}, u32[]{:S(2)}, u32[]{:S(2)}) collective-permute-start(bf16[2,512,256]{2,1,0:T(8,128)(2,1)} %slice_bitcast_fusion.6), channel_id=1, source_target_pairs={{0,2},{1,3},{2,0},{3,1},{4,6},{5,7},{6,4},{7,5},{8,10},{9,11},{10,... | collective-permute-start | bytes 1572872 | tf_op jit(solution)/shard_map/ppermute | solution.py:230
  388.6 17.8 %collective-permute-start.24 = (bf16[2,512,256]{2,1,0:T(8,128)(2,1)}, bf16[2,512,256]{2,1,0:T(8,128)(2,1)}, u32[]{:S(2)}, u32[]{:S(2)}) collective-permute-start(bf16[2,512,256]{2,1,0:T(8,128)(2,1)} %slice_bitcast_fusion.8), channel_id=1, source_target_pairs={{0,1},{1,0},{2,3},{3,2},{4,5},{5,4},{6,7},{7,6},{8,9},{9,8},{10,11... | collective-permute-start | bytes 1572872 | tf_op jit(solution)/shard_map/ppermute | solution.py:230
  389.8 18.3 %collective-permute-start.29 = (bf16[2,512,256]{2,1,0:T(8,128)(2,1)}, bf16[2,512,256]{2,1,0:T(8,128)(2,1)}, u32[]{:S(2)}, u32[]{:S(2)}) collective-permute-start(bf16[2,512,256]{2,1,0:T(8,128)(2,1)} %slice_bitcast_fusion.4), channel_id=1, source_target_pairs={{0,2},{1,3},{2,0},{3,1},{4,6},{5,7},{6,4},{7,5},{8,10},{9,11},{10,... | collective-permute-start | bytes 1572872 | tf_op jit(solution)/shard_map/ppermute | solution.py:230
  390.2 21.9 %collective-permute-start.35 = (bf16[2,256,512]{2,1,0:T(8,128)(2,1)}, bf16[2,256,512]{2,1,0:T(8,128)(2,1)}, u32[]{:S(2)}, u32[]{:S(2)}) collective-permute-start(bf16[2,256,512]{2,1,0:T(8,128)(2,1)} %slice_bitcast_fusion.2), channel_id=1, source_target_pairs={{0,1},{1,0},{2,3},{3,2},{4,5},{5,4},{6,7},{7,6},{8,9},{9,8},{10,11... | collective-permute-start | bytes 1572872 | tf_op jit(solution)/shard_map/ppermute | solution.py:230
  402.7 11.6 %collective-permute-start.38 = (bf16[2,256,512]{2,1,0:T(8,128)(2,1)S(1)}, bf16[2,256,512]{2,1,0:T(8,128)(2,1)S(1)}, u32[]{:S(2)}, u32[]{:S(2)}) collective-permute-start(bf16[2,256,512]{2,1,0:T(8,128)(2,1)S(1)} %slice_bitcast_fusion), channel_id=1, source_target_pairs={{0,2},{1,3},{2,0},{3,1},{4,6},{5,7},{6,4},{7,5},{8,10},{9,11},{10,... | collective-permute-start | bytes 1572872 | tf_op jit(solution)/shard_map/ppermute | solution.py:230
  405.1 18.2 %collective-permute-start.28 = (bf16[512,256]{1,0:T(8,128)(2,1)S(1)}, bf16[512,256]{1,0:T(8,128)(2,1)S(1)}, u32[]{:S(2)}, u32[]{:S(2)}) collective-permute-start(bf16[512,256]{1,0:T(8,128)(2,1)S(1)} %slice_bitcast_fusion.18), channel_id=1, source_target_pairs={{0,1},{1,0},{2,3},{3,2},{4,5},{5,4},{6,7},{7,6},{8,9},{9,8},{10,11... | collective-permute-start | bytes 786440 | tf_op jit(solution)/shard_map/ppermute | solution.py:230
  407.6 12.2 %collective-permute-start.25 = (bf16[512,256]{1,0:T(8,128)(2,1)S(1)}, bf16[512,256]{1,0:T(8,128)(2,1)S(1)}, u32[]{:S(2)}, u32[]{:S(2)}) collective-permute-start(bf16[512,256]{1,0:T(8,128)(2,1)S(1)} %slice_bitcast_fusion.20), channel_id=1, source_target_pairs={{0,2},{1,3},{2,0},{3,1},{4,6},{5,7},{6,4},{7,5},{8,10},{9,11},{10,... | collective-permute-start | bytes 786440 | tf_op jit(solution)/shard_map/ppermute | solution.py:230
  409.3 14.0 %collective-permute-start.33 = (bf16[512,256]{1,0:T(8,128)(2,1)S(1)}, bf16[512,256]{1,0:T(8,128)(2,1)S(1)}, u32[]{:S(2)}, u32[]{:S(2)}) collective-permute-start(bf16[512,256]{1,0:T(8,128)(2,1)S(1)} %slice_bitcast_fusion.16), channel_id=1, source_target_pairs={{0,1},{1,0},{2,3},{3,2},{4,5},{5,4},{6,7},{7,6},{8,9},{9,8},{10,11... | collective-permute-start | bytes 786440 | tf_op jit(solution)/shard_map/ppermute | solution.py:230
  413.4 18.4 %collective-permute-start.37 = (bf16[256,512]{1,0:T(8,128)(2,1)S(1)}, bf16[256,512]{1,0:T(8,128)(2,1)S(1)}, u32[]{:S(2)}, u32[]{:S(2)}) collective-permute-start(bf16[256,512]{1,0:T(8,128)(2,1)S(1)} %slice_bitcast_fusion.14), channel_id=1, source_target_pairs={{0,2},{1,3},{2,0},{3,1},{4,6},{5,7},{6,4},{7,5},{8,10},{9,11},{10,... | collective-permute-start | bytes 786440 | tf_op jit(solution)/shard_map/ppermute | solution.py:230
  414.5 17.4 %collective-permute-start.39 = (bf16[256,512]{1,0:T(8,128)(2,1)S(1)}, bf16[256,512]{1,0:T(8,128)(2,1)S(1)}, u32[]{:S(2)}, u32[]{:S(2)}) collective-permute-start(bf16[256,512]{1,0:T(8,128)(2,1)S(1)} %slice_bitcast_fusion.12), channel_id=1, source_target_pairs={{0,1},{1,0},{2,3},{3,2},{4,5},{5,4},{6,7},{7,6},{8,9},{9,8},{10,11... | collective-permute-start | bytes 786440 | tf_op jit(solution)/shard_map/ppermute | solution.py:230
  419.9 15.4 %collective-permute-start.41 = (bf16[512,512]{1,0:T(8,128)(2,1)S(1)}, bf16[512,512]{1,0:T(8,128)(2,1)S(1)}, u32[]{:S(2)}, u32[]{:S(2)}) collective-permute-start(bf16[512,512]{1,0:T(8,128)(2,1)S(1)} %pad_maximum_fusion.4), channel_id=1, source_target_pairs={{4,0},{5,1},{6,4},{7,5},{12,8},{13,9},{14,12},{15,13},{20,18},{21,... | collective-permute-start | bytes 1572872 | tf_op jit(solution)/shard_map/ppermute | solution.py:242
  423.5 14.8 %collective-permute-start.42 = (bf16[512,512]{1,0:T(8,128)(2,1)S(1)}, bf16[512,512]{1,0:T(8,128)(2,1)S(1)}, u32[]{:S(2)}, u32[]{:S(2)}) collective-permute-start(bf16[512,512]{1,0:T(8,128)(2,1)S(1)} %pad_maximum_fusion.5), channel_id=1, source_target_pairs={{12,16},{13,17},{14,20},{15,21},{20,10},{21,11},{22,14},{23,15}} | collective-permute-start | bytes 1572872 | tf_op jit(solution)/shard_map/ppermute | solution.py:242
  432.0 17.5 %collective-permute-start.43 = (bf16[512,512]{1,0:T(8,128)(2,1)S(1)}, bf16[512,512]{1,0:T(8,128)(2,1)S(1)}, u32[]{:S(2)}, u32[]{:S(2)}) collective-permute-start(bf16[512,512]{1,0:T(8,128)(2,1)S(1)} %pad_maximum_fusion.6), channel_id=1, source_target_pairs={{12,24},{13,25},{14,28},{15,29},{20,2},{21,3},{22,6},{23,7}} | collective-permute-start | bytes 1572872 | tf_op jit(solution)/shard_map/ppermute | solution.py:242
  433.4 16.2 %collective-permute-start.26 = (bf16[512,512]{1,0:T(8,128)(2,1)S(1)}, bf16[512,512]{1,0:T(8,128)(2,1)S(1)}, u32[]{:S(2)}, u32[]{:S(2)}) collective-permute-start(bf16[512,512]{1,0:T(8,128)(2,1)S(1)} %pad_maximum_fusion.4), channel_id=1, source_target_pairs={{0,0},{1,1},{2,4},{3,5},{8,8},{9,9},{10,12},{11,13},{16,18},{17,19... | collective-permute-start | bytes 1572872 | tf_op jit(solution)/shard_map/ppermute | solution.py:242
  434.1 15.5 %collective-permute-start.34 = (bf16[512,512]{1,0:T(8,128)(2,1)S(1)}, bf16[512,512]{1,0:T(8,128)(2,1)S(1)}, u32[]{:S(2)}, u32[]{:S(2)}) collective-permute-start(bf16[512,512]{1,0:T(8,128)(2,1)S(1)} %pad_maximum_fusion.5), channel_id=1, source_target_pairs={{8,16},{9,17},{10,20},{11,21},{16,10},{17,11},{18,14},{19,15}} | collective-permute-start | bytes 1572872 | tf_op jit(solution)/shard_map/ppermute | solution.py:242
  435.4 14.2 %collective-permute-start.40 = (bf16[512,512]{1,0:T(8,128)(2,1)S(1)}, bf16[512,512]{1,0:T(8,128)(2,1)S(1)}, u32[]{:S(2)}, u32[]{:S(2)}) collective-permute-start(bf16[512,512]{1,0:T(8,128)(2,1)S(1)} %pad_maximum_fusion.6), channel_id=1, source_target_pairs={{8,24},{9,25},{10,28},{11,29},{16,2},{17,3},{18,6},{19,7}} | collective-permute-start | bytes 1572872 | tf_op jit(solution)/shard_map/ppermute | solution.py:242
  (9 other events, 65.5 us)

commit v3 on v2

--- a/solution.py
+++ b/solution.py
@@ -18,7 +18,7 @@
 adam_eps = 1e-08
 rate_learn = 0.001
 
-ROW_CHUNKS = 2
+ROW_PARTS = ((0, 2), (2, 2), (4, 4))
 
 
 def row_factors(ratios, pair_row, lengths):
@@ -84,9 +84,9 @@
 INWARD = planes([(0, 1), (3, 2)])
 
 
-def homeward(pairs, core):
+def homeward(pairs, core, flip=0):
     return [
-        ((2 * a + core) * 4 + 2 * y + x, (2 * b + y) * 4 + 2 * (a // 2) + x)
+        ((2 * a + core) * 4 + 2 * y + x, (2 * b + (y ^ flip)) * 4 + 2 * (a // 2) + x)
         for a, b in pairs
         for y in (0, 1)
         for x in (0, 1)
@@ -120,9 +120,10 @@
     outs[4][...] = new_master.astype(jnp.bfloat16)
 
 
-def step_rows(r, scaled_t, acts, master, moment, second, prior, behind):
+def step_rows(part, scaled_t, acts, master, moment, second, prior, behind):
     rows_all, cols = master.shape
-    rows = rows_all // ROW_CHUNKS
+    rows = rows_all // 8 * part[1]
+    r = part[0] // part[1]
     tokens = acts[0].shape[0]
     tile = 768
     state = pl.BlockSpec((rows, tile), lambda t: (r, t))
@@ -168,13 +169,15 @@
 def product_kernel(x_first, n_weights, tiles, place_ref, mine_ref, other_ref, *refs):
     weights = refs[:n_weights]
     out_ref, all_ref = refs[-2:]
-    rows = weights[0].shape[0]
     step = pl.program_id(0)
 
     @pl.when(step == 0)
     def _():
-        for i, ref in enumerate(weights):
-            all_ref[i * rows : (i + 1) * rows] = ref[...]
+        first = 0
+        for ref in weights:
+            rows = ref.shape[0]
+            all_ref[first : first + rows] = ref[...]
+            first += rows
 
     def store(tokens_ref):
         out = times(tokens_ref[...], all_ref[...])
@@ -192,8 +195,7 @@
 
 def products(place, x_first, tokens, weights, behind=()):
     count, cols = tokens[0].shape
-    rows = weights[0].shape[0]
-    features = rows * len(weights) // 2
+    features = sum(block.shape[0] for block in weights) // 2
     tile = 256
     tiles = count // tile
 
@@ -205,7 +207,7 @@
         pl.BlockSpec((tile, cols), lambda t, place: (jnp.minimum(t, tiles - 1), 0)),
         pl.BlockSpec((tile, cols), lambda t, place: (jnp.maximum(t - tiles, 0), 0)),
     ]
-    in_specs += [pl.BlockSpec((rows, cols), lambda t, place: (0, 0))] * len(weights)
+    in_specs += [pl.BlockSpec(block.shape, lambda t, place: (0, 0)) for block in weights]
     in_specs += [pl.BlockSpec(memory_space=pl.ANY)] * len(behind)
     return pl.pallas_call(
         functools.partial(product_kernel, x_first, len(weights), tiles),
@@ -216,7 +218,7 @@
             out_specs=pl.BlockSpec(
                 (2, 1, tile, features) if x_first else (1, 2, tile, features), out_map
             ),
-            scratch_shapes=[pltpu.VMEM((rows * len(weights), cols), jnp.bfloat16)],
+            scratch_shapes=[pltpu.VMEM((2 * features, cols), jnp.bfloat16)],
         ),
         out_shape=jax.ShapeDtypeStruct((2, 2, count, features), jnp.bfloat16),
         compiler_params=pltpu.CompilerParams(vmem_limit_bytes=60 * 1024 * 1024),
@@ -225,13 +227,9 @@
     )(place, *tokens, *weights, *behind)
 
 
-def add_up(stack, x_first, behind=None):
-    for step in ((1, 2) if x_first else (2, 1)):
-        given = lax.ppermute(stack[1], "tensor", [(i, i ^ step) for i in range(4)])
-        if behind is not None:
-            given, behind = lax.optimization_barrier((given, behind))
-        stack = (stack[0].astype(jnp.float32) + given.astype(jnp.float32)).astype(jnp.bfloat16)
-    return stack
+def add_step(stack, step):
+    given = lax.ppermute(stack[1], "tensor", [(i, i ^ step) for i in range(4)])
+    return (stack[0].astype(jnp.float32) + given.astype(jnp.float32)).astype(jnp.bfloat16)
 
 
 def body_planes(
@@ -259,13 +257,14 @@
     for d in (1, 2, 3):
         pieces[d] = send(pieces[d], planes([(p, p ^ d) for p in range(4)]))
 
-    pair_act, middle_act, own_act, own_next, pieces = after(
-        (pair_act, middle_act, hidden_act, next_act, pieces)
+    rows = next_act.shape[0] // 2
+    next_parts = [next_act[:rows], next_act[rows:]]
+    pair_act, middle_act, own_act, own_next, next_parts, pieces = after(
+        (pair_act, middle_act, hidden_act, next_act, next_parts, pieces)
     )
     forward_act = send(pair_act, MIDDLE)
     far_one = send(middle_act, OUTWARD)
-    rows = next_act.shape[0] // 2
-    next_inward = [send(own_next[:rows], INWARD), send(own_next[rows:], INWARD)]
+    next_inward = send(own_next, INWARD)
     pieces = [
         pieces[0],
         pieces[1],
@@ -285,55 +284,78 @@
     pair_act, own_swap = after((pair_act, own_swap))
     pair_swap = send(pair_act, CORES)
 
-    forward_act, far_one, middle_act, own_next, pair_swap, part, next_inward[0] = after(
-        (forward_act, far_one, middle_act, own_next, pair_swap, part, next_inward[0])
+    forward_act, far_one, middle_act, own_next, next_parts, pair_swap, part = after(
+        (forward_act, far_one, middle_act, own_next, next_parts, pair_swap, part)
     )
     far_two = send(forward_act, OUTWARD)
-    next_middle = send(own_next, MIDDLE)
+    next_middle = [send(array, MIDDLE) for array in next_parts]
+    third = jnp.where(inner, middle_act, far_one)
+    third, given = after((third, given))
+    third_swap = send(third, CORES)
     whole = jnp.concatenate([jnp.where(y == 0, part, given), jnp.where(y == 0, given, part)], 0)
     scaled_t = whole.transpose(3, 1, 0, 2).reshape(half, 8 * tokens)
-    third = jnp.where(inner, middle_act, far_one)
-    third_swap = send(third, CORES)
     own_next, third_swap = after((own_next, third_swap))
     next_own = [next_act, send(own_next, CORES)]
+    far_two, next_middle[0], scaled_t = after((far_two, next_middle[0], scaled_t))
     fourth = jnp.where(inner, forward_act, far_two)
     fourth_swap = send(fourth, CORES)
     acts = [hidden_act, own_swap, pair_act, pair_swap, third, third_swap, fourth, fourth_swap]
 
-    behind = [next_own[1], next_inward[1]]
-    prior, own_one = step_rows(0, scaled_t, acts, master, moment, second, None, behind)
-    pair_one = send(own_one, PAIR)
-    next_inward, _ = after((next_inward, own_one))
-    next_far = [send(array, MIDDLE) for array in next_inward]
-    prior, own_two = step_rows(1, scaled_t, acts, master, moment, second, prior, [next_middle])
-    pair_two = send(own_two, PAIR)
+    next_far = send(next_inward, MIDDLE)
 
     place = jnp.stack([(z & 1) ^ x, core ^ y])
-    next_middle, _ = after((next_middle, own_two))
-    next_middle = [next_middle, send(next_middle, CORES)]
-    one, two = (own_one, pair_one), (own_two, pair_two)
-    near_one = products(place, True, next_own, one)
-    middle_one = products(place, False, next_middle, one, [near_one])
-    near_two = products(place, True, next_own, two, [middle_one])
-    middle_two = products(place, False, next_middle, two, [near_two])
-    next_far, _ = after((next_far, own_two))
-    next_far = [[array, send(array, CORES)] for array in next_far]
-    both = (own_one, own_two, pair_one, pair_two)
-    far_one = products(place, True, next_far[0], both, [middle_two])
-    far_two = products(place, False, next_far[1], both, [far_one])
-    near = [add_up(near_one, True, middle_one), add_up(near_two, True, middle_two)]
-    middle = [add_up(middle_one, False), add_up(middle_two, False, far_one)]
-    far = [add_up(far_one, True, far_two), add_up(far_two, False)]
-    near, middle = jnp.concatenate(near, axis=1), jnp.concatenate(middle, axis=1)
-    far = jnp.concatenate(far, axis=0)
-
-    parts = []
+    prior, owns, pairs = None, [], []
+    for part in ROW_PARTS:
+        behind = pairs[:1] if len(owns) == 2 else [next_own[1], next_inward]
+        prior, own = step_rows(part, scaled_t, acts, master, moment, second, prior, behind)
+        owns.append(own)
+        pairs.append(send(own, PAIR))
+    one, two = tuple(owns[:2] + pairs[:2]), (owns[2], pairs[2])
+    both = tuple(owns + pairs)
+
+    def swapped(array, behind):
+        array, _ = after((array, behind))
+        return [array, send(array, CORES)]
+
+    near_one = products(place, True, next_own, one, owns[2:])
+    next_far = swapped(next_far, near_one)
+    far_one = products(place, False, next_far, one, [near_one])
+    near_two = products(place, True, next_own, two, [far_one])
+    near_one, far_one = add_step(add_step(near_one, 1), 2), add_step(add_step(far_one, 2), 1)
+    far_two = products(place, False, next_far, two, [near_two])
+    next_middle[0] = swapped(next_middle[0], near_one)
+    next_middle[1] = swapped(next_middle[1], near_two)
+    middle_one = products(place, False, next_middle[0], both, [far_two, near_one, far_one])
+    middle_two = products(place, True, next_middle[1], both, [middle_one])
+
+    def late_sum(stack, steps):
+        for step in steps:
+            given = lax.ppermute(stack[1], "tensor", [(i, i ^ step) for i in range(4)])
+            given, _ = after((given, middle_two))
+            stack = (stack[0].astype(jnp.float32) + given.astype(jnp.float32)).astype(jnp.bfloat16)
+        return stack
+
+    near = jnp.concatenate([near_one, late_sum(near_two, (1, 2))], axis=1)
+    far = jnp.concatenate([far_one, late_sum(far_two, (2, 1))], axis=1)
+    middle_one = late_sum(middle_one, (2, 1))
+
+    own, across, outside = [(p, p) for p in range(4)], [(1, 2), (2, 1)], [(1, 3), (2, 0)]
+    parts = [
+        [
+            send_all(near, homeward(own, side)),
+            send_all(far, homeward(outside, side)),
+            send_all(middle_one, homeward(across, side)),
+        ]
+        for side in (0, 1)
+    ]
+    given = lax.ppermute(middle_two[1], "tensor", [(i, i ^ 1) for i in range(4)])
+    given, parts = after((given, parts))
+    last_sum = (middle_two[0].astype(jnp.float32) + given.astype(jnp.float32)).astype(jnp.bfloat16)
     for side in (0, 1):
-        parts.append(
-            send_all(near, homeward([(p, p) for p in range(4)], side))
-            + send_all(middle, homeward([(1, 2), (2, 1)], side))
-            + send_all(far, homeward([(1, 3), (2, 0)], side))
-        )
+        last = send_all(last_sum[0], homeward(across, side))
+        last = last + send_all(last_sum[1], homeward(across, side, 1))
+        near, far, first = parts[side]
+        parts[side] = near + far + jnp.concatenate([first, last], axis=0)
     return (*prior, jnp.concatenate(parts, axis=1))
 
 

time: 459 us -> 411 us (0.90); the launches traced: 451 us -> 409 us
  waiting for transfers between devices: 250 us -> 184 us
  starting transfers between devices: 60.6 us -> 69.3 us
  Pallas kernels: 104 us -> 112 us
  local copies, waits for them, and re-layouts: 17.9 us -> 24.4 us
    ppermute x24, waiting for transfers between devices: 191 us -> 127 us  [body_planes(): send = lambda array, pairs: lax.ppermute(array, 'dp', pairs)]
    ppermute x1, waiting for transfers between devices: 24.7 us -> 0.05 us  [body_planes(): given = lax.ppermute(part, 'tensor', [(i, i ^ 2) for i in range(4)])]
    ppermute x12 -> x11, waiting for transfers between devices: 9.14 us -> 26.3 us  [the longest x4 18 us: add_step(): given = lax.ppermute(stack[1], 'tensor', [(i, i ^ step) for i in range(4)])]
    pallas_call x2 -> x3, Pallas kernels: 40.1 us -> 47.6 us  [step_rows(): pl.pallas_call(functools.partial(step_kernel, len(acts), len(operands) -...]
    ppermute x6 -> x10, starting transfers between devices: 15.1 us -> 22.3 us  [body_planes(): send_all = lambda array, pairs: lax.ppermute(array, ('dp', 'tensor'), pairs)]
    ppermute x6 -> x10, waiting for transfers between devices: 13.4 us -> 19.9 us  [body_planes(): send_all = lambda array, pairs: lax.ppermute(array, ('dp', 'tensor'), pairs)]
    ppermute x12 -> x11, starting transfers between devices: 9.67 us -> 6.77 us  [the longest x6 3.42 us: late_sum(): given = lax.ppermute(stack[1], 'tensor', [(i, i ^ step) for i in range(4)])]
  transfers between devices with their start and end apart: 44 -> 47, of which waited for: 19 -> 23; matrix products, arithmetic and copies ran while one was open for 6% -> 9% of each run, Pallas kernels for 19% -> 27%
where the time goes in v3:
time: 411 us; the launch traced here: 409 us
  waiting for transfers between devices  184 us (45%)
  Pallas kernels  112 us (27%)
  starting transfers between devices  69.3 us (17%)
  local copies, waits for them, and re-layouts  24.4 us (6%)
  other arithmetic  18.6 us (5%)
    ppermute x24, waiting for transfers between devices, body_planes(): send = lambda array, pairs: lax.ppermute(array, 'dp', pairs)  127 us
    pallas_call x6, Pallas kernels, products(): pl.pallas_call(functools.partial(product_kernel, x_first, len(weights), t...  64 us
    pallas_call x3, Pallas kernels, step_rows(): pl.pallas_call(functools.partial(step_kernel, len(acts), len(operands) -...  47.6 us
    ppermute x24, starting transfers between devices, body_planes(): send = lambda array, pairs: lax.ppermute(array, 'dp', pairs)  38.7 us
    ppermute x10, starting transfers between devices, body_planes(): send_all = lambda array, pairs: lax.ppermute(array, ('dp', 'tensor'), pairs)  22.3 us
    ppermute x10, waiting for transfers between devices, body_planes(): send_all = lambda array, pairs: lax.ppermute(array, ('dp', 'tensor'), pairs)  19.9 us
    ppermute x4, waiting for transfers between devices, add_step(): given = lax.ppermute(stack[1], 'tensor', [(i, i ^ step) for i in range(4)])  18 us
    ppermute x1, waiting for transfers between devices, body_planes(): given = lax.ppermute(part, 'tensor', [(i, i ^ 1) for i in range(4)])  10.8 us
  transfers between devices with their start and end apart: 47, of which 23 were waited for; matrix products, arithmetic and copies ran while one was open for 9% of the time, Pallas kernels for 27%

profile of v3, /device:TPU:13, one launch (start us, length us, event | category | flops | bytes accessed | tf_op | source)
XLA Modules:
  0.0 409.3 jit_solution(1732321842586352348)
XLA Ops:
  0.9 4.3 %collective-permute-start.1 = (bf16[256,3840]{1,0:T(8,128)(2,1)}, bf16[256,3840]{1,0:T(8,128)(2,1)}, u32[]{:S(2)}, u32[]{:S(2)}) collective-permute-start(bf16[256,3840]{1,0:T(8,128)(2,1)} %refs_1_.5), channel_id=1, source_target_pairs={{8,16},{12,20},{16,8},{20,12},{9,17},{13,21},{17,9},{21,13},{10,18... | collective-permute-start | bytes 5898248 | tf_op jit(solution)/shard_map/ppermute | solution.py:238
  8.5 2.2 multiply_convert_fusion
  13.7 4.3 %fusion.12 = (bf16[256,3840]{1,0:T(8,128)(2,1)}, bf16[256,3840]{1,0:T(8,128)(2,1)}) fusion(bf16[512,3840]{1,0:T(8,128)(2,1)} %mine_ref.3), kind=kLoop, calls=%fused_computation.75 | loop fusion | bytes 7864320 | tf_op jit(solution)/shard_map/slice | solution.py:261
  18.0 29.5 %collective-permute-done.2 = bf16[64,1024]{1,0:T(8,128)(2,1)S(1)} collective-permute-done((bf16[64,1024]{1,0:T(8,128)(2,1)S(1)}, bf16[64,1024]{1,0:T(8,128)(2,1)S(1)}, u32[]{:S(2)}, u32[]{:S(2)}) %collective-permute-start.2) | collective-permute-done | bytes 131104 | tf_op jit(solution)/shard_map/ppermute | solution.py:238
  47.5 7.5 %collective-permute-done.3 = bf16[64,1024]{1,0:T(8,128)(2,1)S(1)} collective-permute-done((bf16[64,1024]{1,0:T(8,128)(2,1)S(1)}, bf16[64,1024]{1,0:T(8,128)(2,1)S(1)}, u32[]{:S(2)}, u32[]{:S(2)}) %collective-permute-start.3) | collective-permute-done | bytes 131104 | tf_op jit(solution)/shard_map/ppermute | solution.py:238
  55.0 3.9 collective-permute-done.4
  60.5 3.4 collective-permute-start.5
  63.8 2.6 collective-permute-start.6
  68.5 3.6 collective-permute-done.9
  74.7 10.8 %collective-permute-done.10 = bf16[1,8,64,512]{3,2,1,0:T(8,128)(2,1)S(1)} collective-permute-done((bf16[1,8,64,512]{3,2,1,0:T(8,128)(2,1)S(1)}, bf16[1,8,64,512]{3,2,1,0:T(8,128)(2,1)S(1)}, u32[]{:S(2)}, u32[]{:S(2)}) %collective-permute-start.10) | collective-permute-done | bytes 524320 | tf_op jit(solution)/shard_map/ppermute | solution.py:280
  86.0 20.9 %collective-permute-done.5 = bf16[256,3840]{1,0:T(8,128)(2,1)} collective-permute-done((bf16[256,3840]{1,0:T(8,128)(2,1)S(1)}, bf16[256,3840]{1,0:T(8,128)(2,1)}, u32[]{:S(2)}, u32[]{:S(2)}) %collective-permute-start.5) | collective-permute-done | bytes 1966112 | tf_op jit(solution)/shard_map/ppermute | solution.py:238
  107.7 1.8 broadcast_select_fusion.1.refs_5_
  109.5 1.8 collective-permute-start.14
  111.3 4.4 %collective-permute-start.11 = (bf16[256,3840]{1,0:T(8,128)(2,1)}, bf16[256,3840]{1,0:T(8,128)(2,1)}, u32[]{:S(2)}, u32[]{:S(2)}) collective-permute-start(bf16[256,3840]{1,0:T(8,128)(2,1)} %collective-permute-done.5), channel_id=1, source_target_pairs={{8,0},{12,4},{16,24},{20,28},{9,1},{13,5},{17,25},{21,29},{10,2},{... | collective-permute-start | bytes 5898248 | tf_op jit(solution)/shard_map/ppermute | solution.py:238
  115.7 2.3 collective-permute-start.12
  123.1 38.5 %collective-permute-done.17.refs_13_.refs_17_ = bf16[512,3840]{1,0:T(8,128)(2,1)} collective-permute-done((bf16[512,3840]{1,0:T(8,128)(2,1)}, bf16[512,3840]{1,0:T(8,128)(2,1)}, u32[]{:S(2)}, u32[]{:S(2)}) %collective-permute-start.17) | collective-permute-done | bytes 3932192 | tf_op jit(solution)/shard_map/ppermute | solution.py:238
  161.5 2.3 collective-permute-start.21
  163.8 1.8 broadcast_select_fusion.refs_7_
  165.6 1.8 collective-permute-start.15
  167.4 4.0 copy.29.refs_0_
  171.4 13.9 %gradient_adam.3 = (f32[512,3840]{1,0:T(8,128)}, f32[512,3840]{1,0:T(8,128)}, f32[512,3840]{1,0:T(8,128)}, f32[512,3840]{1,0:T(8,128)}, bf16[128,3840]{1,0:T(8,128)(2,1)}) custom-call(bf16[512,2048]{1,0:T(8,128)(2,1)} %copy.29.refs_0_, bf16[256,3840]{1,0:T(8,128)(2,1)} %refs_1_.5, bf16[256,3840]{1,0:T(8,128)(2,1)} %copy-done.7, bf16[256,3840]{1,0:T(8,128)(2,1)} %copy-done.6, ...), custom_call_target="tpu_custom_call" | custom-call | flops 1000 | bytes 1000 | tf_op jit(solution)/shard_map/gradient_adam/pallas_call | solution.py:146
  185.4 13.8 %gradient_adam.4 = (f32[512,3840]{1,0:T(8,128)}, f32[512,3840]{1,0:T(8,128)}, f32[512,3840]{1,0:T(8,128)}, f32[512,3840]{1,0:T(8,128)}, bf16[128,3840]{1,0:T(8,128)(2,1)}) custom-call(bf16[512,2048]{1,0:T(8,128)(2,1)} %copy.29.refs_0_, bf16[256,3840]{1,0:T(8,128)(2,1)} %refs_1_.5, ...), custom_call_target="tpu_custom_call", output_to_operand_aliasing={{0}: (12, {}), {1}: (13, {}), {2}: (14, {}), {3}: (15, {})} | custom-call | flops 1000 | bytes 1000 | tf_op jit(solution)/shard_map/gradient_adam/pallas_call | solution.py:146
  201.4 7.0 %collective-permute-done.18.refs_16_.refs_2_.refs_3_ = bf16[128,3840]{1,0:T(8,128)(2,1)S(1)} collective-permute-done((bf16[128,3840]{1,0:T(8,128)(2,1)}, bf16[128,3840]{1,0:T(8,128)(2,1)S(1)}, u32[]{:S(2)}, u32[]{:S(2)}) %collective-permute-start.18) | collective-permute-done | bytes 983072 | tf_op jit(solution)/shard_map/ppermute | solution.py:238
  209.4 19.9 %gradient_adam.5 = (f32[512,3840]{1,0:T(8,128)}, f32[512,3840]{1,0:T(8,128)}, f32[512,3840]{1,0:T(8,128)}, f32[512,3840]{1,0:T(8,128)}, bf16[256,3840]{1,0:T(8,128)(2,1)}) custom-call(bf16[512,2048]{1,0:T(8,128)(2,1)} %copy.29.refs_0_, bf16[256,3840]{1,0:T(8,128)(2,1)} %refs_1_.5, ...), custom_call_target="tpu_custom_call", output_to_operand_aliasing={{0}: (12, {}), {1}: (13, {}), {2}: (14, {}), {3}: (15, {})} | custom-call | flops 1000 | bytes 1000 | tf_op jit(solution)/shard_map/gradient_adam/pallas_call | solution.py:146
  230.4 10.4 %product.6.refs_4_ = bf16[2,2,512,256]{3,2,1,0:T(8,128)(2,1)} custom-call(s32[2]{0:T(128)} %pad_add_fusion.place_ref, bf16[512,3840]{1,0:T(8,128)(2,1)} %mine_ref.3, bf16[512,3840]{1,0:T(8,128)(2,1)} %collective-permute-done.16.refs_12_.refs_16_.other_ref, bf16[128,3840]{1,0:T(8,128)(2,1)} %get-tuple-element.96.refs_0_, ...), custom_call_target="tpu_custom_call" | custom-call | flops 1000 | bytes 1000 | tf_op jit(solution)/shard_map/product/pallas_call | solution.py:212
  240.8 7.9 %collective-permute-done.21.mine_ref = bf16[512,3840]{1,0:T(8,128)(2,1)} collective-permute-done((bf16[512,3840]{1,0:T(8,128)(2,1)}, bf16[512,3840]{1,0:T(8,128)(2,1)}, u32[]{:S(2)}, u32[]{:S(2)}) %collective-permute-start.21) | collective-permute-done | bytes 3932192 | tf_op jit(solution)/shard_map/ppermute | solution.py:238
  248.7 2.4 collective-permute-start.23
  252.5 2.5 collective-permute-start.19
  255.0 10.9 %collective-permute-done.25 = bf16[2,512,256]{2,1,0:T(8,128)(2,1)S(1)} collective-permute-done((bf16[2,512,256]{2,1,0:T(8,128)(2,1)S(1)}, bf16[2,512,256]{2,1,0:T(8,128)(2,1)S(1)}, u32[]{:S(2)}, u32[]{:S(2)}) %collective-permute-start.25) | collective-permute-done | bytes 524320 | tf_op jit(solution)/shard_map/ppermute | solution.py:231
  267.4 7.0 %collective-permute-done.26 = bf16[512,256]{1,0:T(8,128)(2,1)S(1)} collective-permute-done((bf16[512,256]{1,0:T(8,128)(2,1)S(1)}, bf16[512,256]{1,0:T(8,128)(2,1)S(1)}, u32[]{:S(2)}, u32[]{:S(2)}) %collective-permute-start.26) | collective-permute-done | bytes 262176 | tf_op jit(solution)/shard_map/ppermute | solution.py:231
  276.7 10.4 %product.7.refs_2_ = bf16[2,2,512,256]{3,2,1,0:T(8,128)(2,1)} custom-call(s32[2]{0:T(128)} %pad_add_fusion.place_ref, bf16[512,3840]{1,0:T(8,128)(2,1)} %collective-permute-done.21.mine_ref, bf16[512,3840]{1,0:T(8,128)(2,1)} %collective-permute-done.23.other_ref, bf16[128,3840]{1,0:T(8,128)(2,1)} %get-tuple-element.96.refs_0_, ...), custom_call_target="tpu_custom_call" | custom-call | flops 1000 | bytes 1000 | tf_op jit(solution)/shard_map/product/pallas_call | solution.py:212
  287.1 1.9 slice_bitcast_fusion.8
  289.2 7.5 %collective-permute-done.20.refs_1_.refs_5_ = bf16[256,3840]{1,0:T(8,128)(2,1)S(1)} collective-permute-done((bf16[256,3840]{1,0:T(8,128)(2,1)S(1)}, bf16[256,3840]{1,0:T(8,128)(2,1)S(1)}, u32[]{:S(2)}, u32[]{:S(2)}) %collective-permute-start.20) | collective-permute-done | bytes 1966112 | tf_op jit(solution)/shard_map/ppermute | solution.py:238
  298.0 10.4 %product.8.refs_2_ = bf16[2,2,512,256]{3,2,1,0:T(8,128)(2,1)} custom-call(s32[2]{0:T(128)} %pad_add_fusion.place_ref, bf16[512,3840]{1,0:T(8,128)(2,1)} %mine_ref.3, bf16[512,3840]{1,0:T(8,128)(2,1)} %collective-permute-done.16.refs_12_.refs_16_.other_ref, bf16[256,3840]{1,0:T(8,128)(2,1)} %get-tuple-element.102.refs_4_.refs_0_.refs_2_, ...), custom_call_target="tpu_custom_call" | custom-call | flops 1000 | bytes 1000 | tf_op jit(solution)/shard_map/product/pallas_call | solution.py:212
  312.0 10.4 %product.9.refs_6_ = bf16[2,2,512,256]{3,2,1,0:T(8,128)(2,1)} custom-call(s32[2]{0:T(128)} %pad_add_fusion.place_ref, bf16[512,3840]{1,0:T(8,128)(2,1)} %collective-permute-done.21.mine_ref, bf16[512,3840]{1,0:T(8,128)(2,1)} %collective-permute-done.23.other_ref, bf16[256,3840]{1,0:T(8,128)(2,1)} %get-tuple-element.102.refs_4_.refs_0_.refs_2_, ...), custom_call_target="tpu_custom_call" | custom-call | flops 1000 | bytes 1000 | tf_op jit(solution)/shard_map/product/pallas_call | solution.py:212
  323.2 11.1 %product.10.refs_6_ = bf16[2,2,256,512]{3,2,1,0:T(8,128)(2,1)} custom-call(s32[2]{0:T(128)} %pad_add_fusion.place_ref, bf16[256,3840]{1,0:T(8,128)(2,1)} %collective-permute-done.12.mine_ref, bf16[256,3840]{1,0:T(8,128)(2,1)} %collective-permute-done.27.other_ref, bf16[128,3840]{1,0:T(8,128)(2,1)} %get-tuple-element.96.refs_0_, ...), custom_call_target="tpu_custom_call" | custom-call | flops 1000 | bytes 1000 | tf_op jit(solution)/shard_map/product/pallas_call | solution.py:212
  334.3 2.0 slice_bitcast_fusion.1
  339.7 11.3 %product.11 = bf16[2,2,256,512]{3,2,1,0:T(8,128)(2,1)} custom-call(s32[2]{0:T(128)} %pad_add_fusion.place_ref, bf16[256,3840]{1,0:T(8,128)(2,1)} %collective-permute-done.19.mine_ref, bf16[256,3840]{1,0:T(8,128)(2,1)} %collective-permute-done.24.other_ref, bf16[128,3840]{1,0:T(8,128)(2,1)} %get-tuple-element.96.refs_0_, ...), custom_call_target="tpu_custom_call" | custom-call | flops 1000 | bytes 1000 | tf_op jit(solution)/shard_map/product/pallas_call | solution.py:212
  353.4 7.6 %collective-permute-done.34 = bf16[2,512,256]{2,1,0:T(8,128)(2,1)} collective-permute-done((bf16[2,512,256]{2,1,0:T(8,128)(2,1)}, bf16[2,512,256]{2,1,0:T(8,128)(2,1)}, u32[]{:S(2)}, u32[]{:S(2)}) %collective-permute-start.34) | collective-permute-done | bytes 524320 | tf_op jit(solution)/shard_map/ppermute | solution.py:333
  365.6 3.3 collective-permute-start.42
  369.9 2.5 collective-permute-start.41
  372.5 1.9 collective-permute-done.39
  375.1 4.5 %collective-permute-start.40 = (bf16[512,512]{1,0:T(8,128)(2,1)S(1)}, bf16[512,512]{1,0:T(8,128)(2,1)S(1)}, u32[]{:S(2)}, u32[]{:S(2)}) collective-permute-start(bf16[512,512]{1,0:T(8,128)(2,1)S(1)} %pad_maximum_fusion.4), channel_id=1, source_target_pairs={{4,0},{5,1},{6,4},{7,5},{12,8},{13,9},{14,12},{15,13},{20,18},{21,... | collective-permute-start | bytes 1572872 | tf_op jit(solution)/shard_map/ppermute | solution.py:240
  380.3 5.2 %collective-permute-done.41 = bf16[512,512]{1,0:T(8,128)(2,1)S(1)} collective-permute-done((bf16[512,512]{1,0:T(8,128)(2,1)S(1)}, bf16[512,512]{1,0:T(8,128)(2,1)S(1)}, u32[]{:S(2)}, u32[]{:S(2)}) %collective-permute-start.41) | collective-permute-done | bytes 524320 | tf_op jit(solution)/shard_map/ppermute | solution.py:240
  385.4 5.2 %collective-permute-done.40 = bf16[512,512]{1,0:T(8,128)(2,1)S(1)} collective-permute-done((bf16[512,512]{1,0:T(8,128)(2,1)S(1)}, bf16[512,512]{1,0:T(8,128)(2,1)S(1)}, u32[]{:S(2)}, u32[]{:S(2)}) %collective-permute-start.40) | collective-permute-done | bytes 524320 | tf_op jit(solution)/shard_map/ppermute | solution.py:240
  393.4 2.5 collective-permute-start.45
  395.9 4.2 %collective-permute-start.46 = (bf16[256,512]{1,0:T(8,128)(2,1)S(1)}, bf16[256,512]{1,0:T(8,128)(2,1)S(1)}, u32[]{:S(2)}, u32[]{:S(2)}) collective-permute-start(bf16[256,512]{1,0:T(8,128)(2,1)S(1)} %get-tuple-element.133), channel_id=1, source_target_pairs={{12,20},{13,21},{14,16},{15,17},{20,14},{21,15},{22,10},{23,11}} | collective-permute-start | bytes 786440 | tf_op jit(solution)/shard_map/ppermute | solution.py:240
  403.7 4.3 %collective-permute-done.46 = bf16[256,512]{1,0:T(8,128)(2,1)S(1)} collective-permute-done((bf16[256,512]{1,0:T(8,128)(2,1)S(1)}, bf16[256,512]{1,0:T(8,128)(2,1)S(1)}, u32[]{:S(2)}, u32[]{:S(2)}) %collective-permute-start.46) | collective-permute-done | bytes 262176 | tf_op jit(solution)/shard_map/ppermute | solution.py:240
  (142 shorter events, 54.8 us)
Async XLA Ops:
  0.6 58.2 %collective-permute-start = (bf16[256,3840]{1,0:T(8,128)(2,1)}, bf16[256,3840]{1,0:T(8,128)(2,1)S(1)}, u32[]{:S(2)}, u32[]{:S(2)}) collective-permute-start(bf16[256,3840]{1,0:T(8,128)(2,1)} %refs_1_.5), channel_id=1, source_target_pairs={{0,8},{4,12},{8,0},{12,4},{16,24},{20,28},{24,16},{28,20},{1,9},{5... | collective-permute-start | bytes 5898248 | tf_op jit(solution)/shard_map/ppermute | solution.py:238
  0.9 58.0 %collective-permute-start.1 = (bf16[256,3840]{1,0:T(8,128)(2,1)}, bf16[256,3840]{1,0:T(8,128)(2,1)}, u32[]{:S(2)}, u32[]{:S(2)}) collective-permute-start(bf16[256,3840]{1,0:T(8,128)(2,1)} %refs_1_.5), channel_id=1, source_target_pairs={{8,16},{12,20},{16,8},{20,12},{9,17},{13,21},{17,9},{21,13},{10,18... | collective-permute-start | bytes 5898248 | tf_op jit(solution)/shard_map/ppermute | solution.py:238
  11.0 36.5 %collective-permute-start.2 = (bf16[64,1024]{1,0:T(8,128)(2,1)S(1)}, bf16[64,1024]{1,0:T(8,128)(2,1)S(1)}, u32[]{:S(2)}, u32[]{:S(2)}) collective-permute-start(bf16[64,1024]{1,0:T(8,128)(2,1)S(1)} %get-tuple-element.129), channel_id=1, source_target_pairs={{0,8},{4,12},{8,0},{12,4},{16,24},{20,28},{24,16},{28,20},{1,9},{5... | collective-permute-start | bytes 393224 | tf_op jit(solution)/shard_map/ppermute | solution.py:238
  11.1 43.9 %collective-permute-start.3 = (bf16[64,1024]{1,0:T(8,128)(2,1)S(1)}, bf16[64,1024]{1,0:T(8,128)(2,1)S(1)}, u32[]{:S(2)}, u32[]{:S(2)}) collective-permute-start(bf16[64,1024]{1,0:T(8,128)(2,1)S(1)} %get-tuple-element.128), channel_id=1, source_target_pairs={{0,16},{4,20},{8,24},{12,28},{16,0},{20,4},{24,8},{28,12},{1,17},{... | collective-permute-start | bytes 393224 | tf_op jit(solution)/shard_map/ppermute | solution.py:238
  12.3 46.6 %copy-start.5 = (bf16[256,3840]{1,0:T(8,128)(2,1)S(1)}, bf16[256,3840]{1,0:T(8,128)(2,1)}, u32[]{:S(2)}) copy-start(bf16[256,3840]{1,0:T(8,128)(2,1)} %refs_1_.5) | copy-start | bytes 5898244
  12.3 46.6 %collective-permute-start.4 = (bf16[64,1024]{1,0:T(8,128)(2,1)S(1)}, bf16[64,1024]{1,0:T(8,128)(2,1)S(1)}, u32[]{:S(2)}, u32[]{:S(2)}) collective-permute-start(bf16[64,1024]{1,0:T(8,128)(2,1)S(1)} %get-tuple-element.127), channel_id=1, source_target_pairs={{0,24},{4,28},{8,16},{12,20},{16,8},{20,12},{24,0},{28,4},{1,25},{... | collective-permute-start | bytes 393224 | tf_op jit(solution)/shard_map/ppermute | solution.py:238
  58.9 7.6 %collective-permute-start.7 = (bf16[256,3840]{1,0:T(8,128)(2,1)S(1)}, bf16[256,3840]{1,0:T(8,128)(2,1)S(1)}, u32[]{:S(2)}, u32[]{:S(2)}) collective-permute-start(bf16[256,3840]{1,0:T(8,128)(2,1)S(1)} %copy-done.5), channel_id=1, source_target_pairs={{0,4},{4,0},{8,12},{12,8},{16,20},{20,16},{24,28},{28,24},{1,5},{5... | collective-permute-start | bytes 5898248 | tf_op jit(solution)/shard_map/ppermute | solution.py:238
  60.5 46.4 %collective-permute-start.5 = (bf16[256,3840]{1,0:T(8,128)(2,1)S(1)}, bf16[256,3840]{1,0:T(8,128)(2,1)}, u32[]{:S(2)}, u32[]{:S(2)}) collective-permute-start(bf16[256,3840]{1,0:T(8,128)(2,1)S(1)} %collective-permute-done.refs_3_), channel_id=1, source_target_pairs={{8,16},{12,20},{16,8},{20,12},{9,17},{13,21},{17,9},{21,13},{10,18... | collective-permute-start | bytes 5898248 | tf_op jit(solution)/shard_map/ppermute | solution.py:238
  63.8 43.8 %collective-permute-start.6 = (bf16[256,3840]{1,0:T(8,128)(2,1)}, bf16[256,3840]{1,0:T(8,128)(2,1)}, u32[]{:S(2)}, u32[]{:S(2)}) collective-permute-start(bf16[256,3840]{1,0:T(8,128)(2,1)} %collective-permute-done.1), channel_id=1, source_target_pairs={{8,0},{12,4},{16,24},{20,28},{9,1},{13,5},{17,25},{21,29},{10,2},{... | collective-permute-start | bytes 5898248 | tf_op jit(solution)/shard_map/ppermute | solution.py:238
  67.7 40.0 %collective-permute-start.8 = (bf16[256,3840]{1,0:T(8,128)(2,1)S(1)}, bf16[256,3840]{1,0:T(8,128)(2,1)}, u32[]{:S(2)}, u32[]{:S(2)}) collective-permute-start(bf16[256,3840]{1,0:T(8,128)(2,1)S(1)} %collective-permute-done.refs_3_), channel_id=1, source_target_pairs={{0,4},{4,0},{8,12},{12,8},{16,20},{20,16},{24,28},{28,24},{1,5},{5... | collective-permute-start | bytes 5898248 | tf_op jit(solution)/shard_map/ppermute | solution.py:238
  68.2 3.9 collective-permute-start.9
  72.1 13.4 %collective-permute-start.10 = (bf16[1,8,64,512]{3,2,1,0:T(8,128)(2,1)S(1)}, bf16[1,8,64,512]{3,2,1,0:T(8,128)(2,1)S(1)}, u32[]{:S(2)}, u32[]{:S(2)}) collective-permute-start(bf16[1,8,64,512]{3,2,1,0:T(8,128)(2,1)S(1)} %bitcast.101), channel_id=1, source_target_pairs={{0,1},{1,0},{2,3},{3,2},{4,5},{5,4},{6,7},{7,6},{8,9},{9,8},{10,11... | collective-permute-start | bytes 1572872 | tf_op jit(solution)/shard_map/ppermute | solution.py:280
  73.4 88.1 %collective-permute-start.17 = (bf16[512,3840]{1,0:T(8,128)(2,1)}, bf16[512,3840]{1,0:T(8,128)(2,1)}, u32[]{:S(2)}, u32[]{:S(2)}) collective-permute-start(bf16[512,3840]{1,0:T(8,128)(2,1)} %mine_ref.3), channel_id=1, source_target_pairs={{0,8},{4,12},{24,16},{28,20},{1,9},{5,13},{25,17},{29,21},{2,10},{... | collective-permute-start | bytes 11796488 | tf_op jit(solution)/shard_map/ppermute | solution.py:238
  85.7 23.8 %collective-permute-start.13 = (bf16[2,8,64,512]{3,2,1,0:T(8,128)(2,1)S(1)}, bf16[2,8,64,512]{3,2,1,0:T(8,128)(2,1)S(1)}, u32[]{:S(2)}, u32[]{:S(2)}) collective-permute-start(bf16[2,8,64,512]{3,2,1,0:T(8,128)(2,1)S(1)} %pad_maximum_fusion), channel_id=1, source_target_pairs={{0,2},{1,3},{2,0},{3,1},{4,6},{5,7},{6,4},{7,5},{8,10},{9,11},{10,... | collective-permute-start | bytes 3145736 | tf_op jit(solution)/shard_map/ppermute | solution.py:282
  109.5 8.5 %collective-permute-start.14 = (bf16[256,3840]{1,0:T(8,128)(2,1)S(1)}, bf16[256,3840]{1,0:T(8,128)(2,1)S(1)}, u32[]{:S(2)}, u32[]{:S(2)}) collective-permute-start(bf16[256,3840]{1,0:T(8,128)(2,1)S(1)} %broadcast_select_fusion.1.refs_5_), channel_id=1, source_target_pairs={{0,4},{4,0},{8,12},{12,8},{16,20},{20,16},{24,28},{28,24},{1,5},{5... | collective-permute-start | bytes 5898248 | tf_op jit(solution)/shard_map/ppermute | solution.py:238
  111.3 52.5 %collective-permute-start.11 = (bf16[256,3840]{1,0:T(8,128)(2,1)}, bf16[256,3840]{1,0:T(8,128)(2,1)}, u32[]{:S(2)}, u32[]{:S(2)}) collective-permute-start(bf16[256,3840]{1,0:T(8,128)(2,1)} %collective-permute-done.5), channel_id=1, source_target_pairs={{8,0},{12,4},{16,24},{20,28},{9,1},{13,5},{17,25},{21,29},{10,2},{... | collective-permute-start | bytes 5898248 | tf_op jit(solution)/shard_map/ppermute | solution.py:238
  115.7 48.1 %collective-permute-start.12 = (bf16[256,3840]{1,0:T(8,128)(2,1)}, bf16[256,3840]{1,0:T(8,128)(2,1)}, u32[]{:S(2)}, u32[]{:S(2)}) collective-permute-start(bf16[256,3840]{1,0:T(8,128)(2,1)} %get-tuple-element.75), channel_id=1, source_target_pairs={{8,16},{12,20},{16,8},{20,12},{9,17},{13,21},{17,9},{21,13},{10,18... | collective-permute-start | bytes 5898248 | tf_op jit(solution)/shard_map/ppermute | solution.py:238
  119.4 51.9 %collective-permute-start.16 = (bf16[512,3840]{1,0:T(8,128)(2,1)}, bf16[512,3840]{1,0:T(8,128)(2,1)}, u32[]{:S(2)}, u32[]{:S(2)}) collective-permute-start(bf16[512,3840]{1,0:T(8,128)(2,1)} %mine_ref.3), channel_id=1, source_target_pairs={{0,4},{4,0},{8,12},{12,8},{16,20},{20,16},{24,28},{28,24},{1,5},{5... | collective-permute-start | bytes 11796488 | tf_op jit(solution)/shard_map/ppermute | solution.py:238
  161.5 87.2 %collective-permute-start.21 = (bf16[512,3840]{1,0:T(8,128)(2,1)}, bf16[512,3840]{1,0:T(8,128)(2,1)}, u32[]{:S(2)}, u32[]{:S(2)}) collective-permute-start(bf16[512,3840]{1,0:T(8,128)(2,1)} %collective-permute-done.17.refs_13_.refs_17_), channel_id=1, source_target_pairs={{8,16},{12,20},{16,8},{20,12},{9,17},{13,21},{17,9},{21,13},{10,18... | collective-permute-start | bytes 11796488 | tf_op jit(solution)/shard_map/ppermute | solution.py:238
  165.6 5.8 %collective-permute-start.15 = (bf16[256,3840]{1,0:T(8,128)(2,1)S(1)}, bf16[256,3840]{1,0:T(8,128)(2,1)}, u32[]{:S(2)}, u32[]{:S(2)}) collective-permute-start(bf16[256,3840]{1,0:T(8,128)(2,1)S(1)} %broadcast_select_fusion.refs_7_), channel_id=1, source_target_pairs={{0,4},{4,0},{8,12},{12,8},{16,20},{20,16},{24,28},{28,24},{1,5},{5... | collective-permute-start | bytes 5898248 | tf_op jit(solution)/shard_map/ppermute | solution.py:238
  185.3 23.1 %collective-permute-start.18 = (bf16[128,3840]{1,0:T(8,128)(2,1)}, bf16[128,3840]{1,0:T(8,128)(2,1)S(1)}, u32[]{:S(2)}, u32[]{:S(2)}) collective-permute-start(bf16[128,3840]{1,0:T(8,128)(2,1)} %get-tuple-element.96.refs_0_), channel_id=1, source_target_pairs={{0,8},{4,12},{8,0},{12,4},{16,24},{20,28},{24,16},{28,20},{1,9},{5... | collective-permute-start | bytes 2949128 | tf_op jit(solution)/shard_map/ppermute | solution.py:238
  199.2 30.2 %collective-permute-start.22 = (bf16[128,3840]{1,0:T(8,128)(2,1)}, bf16[128,3840]{1,0:T(8,128)(2,1)S(1)}, u32[]{:S(2)}, u32[]{:S(2)}) collective-permute-start(bf16[128,3840]{1,0:T(8,128)(2,1)} %get-tuple-element.103.refs_1_), channel_id=1, source_target_pairs={{0,8},{4,12},{8,0},{12,4},{16,24},{20,28},{24,16},{28,20},{1,9},{5... | collective-permute-start | bytes 2949128 | tf_op jit(solution)/shard_map/ppermute | solution.py:238
  248.7 27.9 %collective-permute-start.23 = (bf16[512,3840]{1,0:T(8,128)(2,1)}, bf16[512,3840]{1,0:T(8,128)(2,1)}, u32[]{:S(2)}, u32[]{:S(2)}) collective-permute-start(bf16[512,3840]{1,0:T(8,128)(2,1)} %collective-permute-done.21.mine_ref), channel_id=1, source_target_pairs={{0,4},{4,0},{8,12},{12,8},{16,20},{20,16},{24,28},{28,24},{1,5},{5... | collective-permute-start | bytes 11796488 | tf_op jit(solution)/shard_map/ppermute | solution.py:238
  252.2 13.7 %collective-permute-start.25 = (bf16[2,512,256]{2,1,0:T(8,128)(2,1)S(1)}, bf16[2,512,256]{2,1,0:T(8,128)(2,1)S(1)}, u32[]{:S(2)}, u32[]{:S(2)}) collective-permute-start(bf16[2,512,256]{2,1,0:T(8,128)(2,1)S(1)} %slice_bitcast_fusion.10), channel_id=1, source_target_pairs={{0,1},{1,0},{2,3},{3,2},{4,5},{5,4},{6,7},{7,6},{8,9},{9,8},{10,11... | collective-permute-start | bytes 1572872 | tf_op jit(solution)/shard_map/ppermute | solution.py:231
  252.5 44.2 %collective-permute-start.20 = (bf16[256,3840]{1,0:T(8,128)(2,1)S(1)}, bf16[256,3840]{1,0:T(8,128)(2,1)S(1)}, u32[]{:S(2)}, u32[]{:S(2)}) collective-permute-start(bf16[256,3840]{1,0:T(8,128)(2,1)S(1)} %copy-done), channel_id=1, source_target_pairs={{0,8},{4,12},{8,0},{12,4},{16,24},{20,28},{24,16},{28,20},{1,9},{5... | collective-permute-start | bytes 5898248 | tf_op jit(solution)/shard_map/ppermute | solution.py:238
  252.5 55.9 %collective-permute-start.19 = (bf16[256,3840]{1,0:T(8,128)(2,1)}, bf16[256,3840]{1,0:T(8,128)(2,1)}, u32[]{:S(2)}, u32[]{:S(2)}) collective-permute-start(bf16[256,3840]{1,0:T(8,128)(2,1)} %get-tuple-element.101), channel_id=1, source_target_pairs={{8,16},{12,20},{16,8},{20,12},{9,17},{13,21},{17,9},{21,13},{10,18... | collective-permute-start | bytes 5898248 | tf_op jit(solution)/shard_map/ppermute | solution.py:238
  267.1 7.3 %collective-permute-start.26 = (bf16[512,256]{1,0:T(8,128)(2,1)S(1)}, bf16[512,256]{1,0:T(8,128)(2,1)S(1)}, u32[]{:S(2)}, u32[]{:S(2)}) collective-permute-start(bf16[512,256]{1,0:T(8,128)(2,1)S(1)} %slice_bitcast_fusion.22), channel_id=1, source_target_pairs={{0,2},{1,3},{2,0},{3,1},{4,6},{5,7},{6,4},{7,5},{8,10},{9,11},{10,... | collective-permute-start | bytes 786440 | tf_op jit(solution)/shard_map/ppermute | solution.py:231
  275.2 48.0 %collective-permute-start.27 = (bf16[256,3840]{1,0:T(8,128)(2,1)}, bf16[256,3840]{1,0:T(8,128)(2,1)}, u32[]{:S(2)}, u32[]{:S(2)}) collective-permute-start(bf16[256,3840]{1,0:T(8,128)(2,1)} %collective-permute-done.12.mine_ref), channel_id=1, source_target_pairs={{0,4},{4,0},{8,12},{12,8},{16,20},{20,16},{24,28},{28,24},{1,5},{5... | collective-permute-start | bytes 5898248 | tf_op jit(solution)/shard_map/ppermute | solution.py:238
  289.0 20.4 %collective-permute-start.28 = (bf16[2,512,256]{2,1,0:T(8,128)(2,1)}, bf16[2,512,256]{2,1,0:T(8,128)(2,1)}, u32[]{:S(2)}, u32[]{:S(2)}) collective-permute-start(bf16[2,512,256]{2,1,0:T(8,128)(2,1)} %slice_bitcast_fusion.8), channel_id=1, source_target_pairs={{0,2},{1,3},{2,0},{3,1},{4,6},{5,7},{6,4},{7,5},{8,10},{9,11},{10,... | collective-permute-start | bytes 1572872 | tf_op jit(solution)/shard_map/ppermute | solution.py:231
  308.4 31.2 %collective-permute-start.24 = (bf16[256,3840]{1,0:T(8,128)(2,1)}, bf16[256,3840]{1,0:T(8,128)(2,1)}, u32[]{:S(2)}, u32[]{:S(2)}) collective-permute-start(bf16[256,3840]{1,0:T(8,128)(2,1)} %collective-permute-done.19.mine_ref), channel_id=1, source_target_pairs={{0,4},{4,0},{8,12},{12,8},{16,20},{20,16},{24,28},{28,24},{1,5},{5... | collective-permute-start | bytes 5898248 | tf_op jit(solution)/shard_map/ppermute | solution.py:238
  310.8 11.7 %collective-permute-start.29 = (bf16[512,256]{1,0:T(8,128)(2,1)S(1)}, bf16[512,256]{1,0:T(8,128)(2,1)S(1)}, u32[]{:S(2)}, u32[]{:S(2)}) collective-permute-start(bf16[512,256]{1,0:T(8,128)(2,1)S(1)} %slice_bitcast_fusion.20), channel_id=1, source_target_pairs={{0,1},{1,0},{2,3},{3,2},{4,5},{5,4},{6,7},{7,6},{8,9},{9,8},{10,11... | collective-permute-start | bytes 786440 | tf_op jit(solution)/shard_map/ppermute | solution.py:231
  336.2 14.7 %collective-permute-start.37 = (bf16[2,256,512]{2,1,0:T(8,128)(2,1)}, bf16[2,256,512]{2,1,0:T(8,128)(2,1)}, u32[]{:S(2)}, u32[]{:S(2)}) collective-permute-start(bf16[2,256,512]{2,1,0:T(8,128)(2,1)} %slice_bitcast_fusion.1), channel_id=1, source_target_pairs={{0,2},{1,3},{2,0},{3,1},{4,6},{5,7},{6,4},{7,5},{8,10},{9,11},{10,... | collective-permute-start | bytes 1572872 | tf_op jit(solution)/shard_map/ppermute | solution.py:333
  337.3 23.7 %collective-permute-start.34 = (bf16[2,512,256]{2,1,0:T(8,128)(2,1)}, bf16[2,512,256]{2,1,0:T(8,128)(2,1)}, u32[]{:S(2)}, u32[]{:S(2)}) collective-permute-start(bf16[2,512,256]{2,1,0:T(8,128)(2,1)} %slice_bitcast_fusion.3), channel_id=1, source_target_pairs={{0,2},{1,3},{2,0},{3,1},{4,6},{5,7},{6,4},{7,5},{8,10},{9,11},{10,... | collective-permute-start | bytes 1572872 | tf_op jit(solution)/shard_map/ppermute | solution.py:333
  339.4 23.2 %collective-permute-start.31 = (bf16[2,512,256]{2,1,0:T(8,128)(2,1)}, bf16[2,512,256]{2,1,0:T(8,128)(2,1)S(1)}, u32[]{:S(2)}, u32[]{:S(2)}) collective-permute-start(bf16[2,512,256]{2,1,0:T(8,128)(2,1)} %slice_bitcast_fusion.5), channel_id=1, source_target_pairs={{0,1},{1,0},{2,3},{3,2},{4,5},{5,4},{6,7},{7,6},{8,9},{9,8},{10,11... | collective-permute-start | bytes 1572872 | tf_op jit(solution)/shard_map/ppermute | solution.py:333
  352.3 12.0 %collective-permute-start.38 = (bf16[256,512]{1,0:T(8,128)(2,1)S(1)}, bf16[256,512]{1,0:T(8,128)(2,1)S(1)}, u32[]{:S(2)}, u32[]{:S(2)}) collective-permute-start(bf16[256,512]{1,0:T(8,128)(2,1)S(1)} %slice_bitcast_fusion.14), channel_id=1, source_target_pairs={{0,1},{1,0},{2,3},{3,2},{4,5},{5,4},{6,7},{7,6},{8,9},{9,8},{10,11... | collective-permute-start | bytes 786440 | tf_op jit(solution)/shard_map/ppermute | solution.py:333
  362.3 6.8 %collective-permute-start.35 = (bf16[512,256]{1,0:T(8,128)(2,1)S(1)}, bf16[512,256]{1,0:T(8,128)(2,1)S(1)}, u32[]{:S(2)}, u32[]{:S(2)}) collective-permute-start(bf16[512,256]{1,0:T(8,128)(2,1)S(1)} %slice_bitcast_fusion.16), channel_id=1, source_target_pairs={{0,1},{1,0},{2,3},{3,2},{4,5},{5,4},{6,7},{7,6},{8,9},{9,8},{10,11... | collective-permute-start | bytes 786440 | tf_op jit(solution)/shard_map/ppermute | solution.py:333
  362.8 7.1 %collective-permute-start.32 = (bf16[512,256]{1,0:T(8,128)(2,1)S(1)}, bf16[512,256]{1,0:T(8,128)(2,1)S(1)}, u32[]{:S(2)}, u32[]{:S(2)}) collective-permute-start(bf16[512,256]{1,0:T(8,128)(2,1)S(1)} %slice_bitcast_fusion.18), channel_id=1, source_target_pairs={{0,2},{1,3},{2,0},{3,1},{4,6},{5,7},{6,4},{7,5},{8,10},{9,11},{10,... | collective-permute-start | bytes 786440 | tf_op jit(solution)/shard_map/ppermute | solution.py:333
  363.0 17.2 %collective-permute-start.30 = (bf16[2,256,512]{2,1,0:T(8,128)(2,1)S(1)}, bf16[2,256,512]{2,1,0:T(8,128)(2,1)S(1)}, u32[]{:S(2)}, u32[]{:S(2)}) collective-permute-start(bf16[2,256,512]{2,1,0:T(8,128)(2,1)S(1)} %slice_bitcast_fusion.7), channel_id=1, source_target_pairs={{0,1},{1,0},{2,3},{3,2},{4,5},{5,4},{6,7},{7,6},{8,9},{9,8},{10,11... | collective-permute-start | bytes 1572872 | tf_op jit(solution)/shard_map/ppermute | solution.py:351
  364.3 10.1 %collective-permute-start.39 = (bf16[256,512]{1,0:T(8,128)(2,1)S(1)}, bf16[256,512]{1,0:T(8,128)(2,1)S(1)}, u32[]{:S(2)}, u32[]{:S(2)}) collective-permute-start(bf16[256,512]{1,0:T(8,128)(2,1)S(1)} %fusion.6), channel_id=1, source_target_pairs={{8,16},{9,17},{10,20},{11,21},{16,10},{17,11},{18,14},{19,15}} | collective-permute-start | bytes 786440 | tf_op jit(solution)/shard_map/ppermute | solution.py:240
  365.6 9.5 %collective-permute-start.42 = (bf16[256,512]{1,0:T(8,128)(2,1)S(1)}, bf16[256,512]{1,0:T(8,128)(2,1)S(1)}, u32[]{:S(2)}, u32[]{:S(2)}) collective-permute-start(bf16[256,512]{1,0:T(8,128)(2,1)S(1)} %fusion.6), channel_id=1, source_target_pairs={{12,16},{13,17},{14,20},{15,21},{20,10},{21,11},{22,14},{23,15}} | collective-permute-start | bytes 786440 | tf_op jit(solution)/shard_map/ppermute | solution.py:240
  369.1 11.1 %collective-permute-start.36 = (bf16[512,512]{1,0:T(8,128)(2,1)S(1)}, bf16[512,512]{1,0:T(8,128)(2,1)S(1)}, u32[]{:S(2)}, u32[]{:S(2)}) collective-permute-start(bf16[512,512]{1,0:T(8,128)(2,1)S(1)} %pad_maximum_fusion.5), channel_id=1, source_target_pairs={{8,24},{9,25},{10,28},{11,29},{16,2},{17,3},{18,6},{19,7}} | collective-permute-start | bytes 1572872 | tf_op jit(solution)/shard_map/ppermute | solution.py:240
  369.9 15.6 %collective-permute-start.41 = (bf16[512,512]{1,0:T(8,128)(2,1)S(1)}, bf16[512,512]{1,0:T(8,128)(2,1)S(1)}, u32[]{:S(2)}, u32[]{:S(2)}) collective-permute-start(bf16[512,512]{1,0:T(8,128)(2,1)S(1)} %pad_maximum_fusion.5), channel_id=1, source_target_pairs={{12,24},{13,25},{14,28},{15,29},{20,2},{21,3},{22,6},{23,7}} | collective-permute-start | bytes 1572872 | tf_op jit(solution)/shard_map/ppermute | solution.py:240
  374.4 11.0 %collective-permute-start.33 = (bf16[512,512]{1,0:T(8,128)(2,1)S(1)}, bf16[512,512]{1,0:T(8,128)(2,1)S(1)}, u32[]{:S(2)}, u32[]{:S(2)}) collective-permute-start(bf16[512,512]{1,0:T(8,128)(2,1)S(1)} %pad_maximum_fusion.4), channel_id=1, source_target_pairs={{0,0},{1,1},{2,4},{3,5},{8,8},{9,9},{10,12},{11,13},{16,18},{17,19... | collective-permute-start | bytes 1572872 | tf_op jit(solution)/shard_map/ppermute | solution.py:240
  375.1 15.5 %collective-permute-start.40 = (bf16[512,512]{1,0:T(8,128)(2,1)S(1)}, bf16[512,512]{1,0:T(8,128)(2,1)S(1)}, u32[]{:S(2)}, u32[]{:S(2)}) collective-permute-start(bf16[512,512]{1,0:T(8,128)(2,1)S(1)} %pad_maximum_fusion.4), channel_id=1, source_target_pairs={{4,0},{5,1},{6,4},{7,5},{12,8},{13,9},{14,12},{15,13},{20,18},{21,... | collective-permute-start | bytes 1572872 | tf_op jit(solution)/shard_map/ppermute | solution.py:240
  390.8 9.3 %collective-permute-start.43 = (bf16[256,512]{1,0:T(8,128)(2,1)S(1)}, bf16[256,512]{1,0:T(8,128)(2,1)S(1)}, u32[]{:S(2)}, u32[]{:S(2)}) collective-permute-start(bf16[256,512]{1,0:T(8,128)(2,1)S(1)} %get-tuple-element.134), channel_id=1, source_target_pairs={{8,16},{9,17},{10,20},{11,21},{16,10},{17,11},{18,14},{19,15}} | collective-permute-start | bytes 786440 | tf_op jit(solution)/shard_map/ppermute | solution.py:240
  392.1 9.7 %collective-permute-start.44 = (bf16[256,512]{1,0:T(8,128)(2,1)S(1)}, bf16[256,512]{1,0:T(8,128)(2,1)S(1)}, u32[]{:S(2)}, u32[]{:S(2)}) collective-permute-start(bf16[256,512]{1,0:T(8,128)(2,1)S(1)} %get-tuple-element.133), channel_id=1, source_target_pairs={{8,20},{9,21},{10,16},{11,17},{16,14},{17,15},{18,10},{19,11}} | collective-permute-start | bytes 786440 | tf_op jit(solution)/shard_map/ppermute | solution.py:240
  393.4 10.3 %collective-permute-start.45 = (bf16[256,512]{1,0:T(8,128)(2,1)S(1)}, bf16[256,512]{1,0:T(8,128)(2,1)S(1)}, u32[]{:S(2)}, u32[]{:S(2)}) collective-permute-start(bf16[256,512]{1,0:T(8,128)(2,1)S(1)} %get-tuple-element.134), channel_id=1, source_target_pairs={{12,16},{13,17},{14,20},{15,21},{20,10},{21,11},{22,14},{23,15}} | collective-permute-start | bytes 786440 | tf_op jit(solution)/shard_map/ppermute | solution.py:240
  395.9 12.1 %collective-permute-start.46 = (bf16[256,512]{1,0:T(8,128)(2,1)S(1)}, bf16[256,512]{1,0:T(8,128)(2,1)S(1)}, u32[]{:S(2)}, u32[]{:S(2)}) collective-permute-start(bf16[256,512]{1,0:T(8,128)(2,1)S(1)} %get-tuple-element.133), channel_id=1, source_target_pairs={{12,20},{13,21},{14,16},{15,17},{20,14},{21,15},{22,10},{23,11}} | collective-permute-start | bytes 786440 | tf_op jit(solution)/shard_map/ppermute | solution.py:240
  (16 other events, 138.3 us)

commit v4 on v3

--- a/solution.py
+++ b/solution.py
@@ -97,15 +97,20 @@
 
 
 def step_kernel(n_act, skip, *refs):
-    scaled_ref = refs[0]
+    scaled_ref, scaled_t = refs[0], refs[-1]
     acts = refs[1 : 1 + n_act]
     master_ref, moment_ref, second_ref = refs[1 + n_act : 4 + n_act]
-    outs = refs[4 + n_act + skip :]
+    outs = refs[4 + n_act + skip : -1]
     tokens = acts[0].shape[0]
+
+    @pl.when(pl.program_id(0) == 0)
+    def _():
+        scaled_t[...] = scaled_ref[...].T
+
     grad = None
     for i, act in enumerate(acts):
         term = jnp.dot(
-            scaled_ref[:, i * tokens : (i + 1) * tokens],
+            scaled_t[:, i * tokens : (i + 1) * tokens],
             act[...],
             preferred_element_type=jnp.float32,
         )
@@ -120,7 +125,7 @@
     outs[4][...] = new_master.astype(jnp.bfloat16)
 
 
-def step_rows(part, scaled_t, acts, master, moment, second, prior, behind):
+def step_rows(part, scaled_all, acts, master, moment, second, prior, behind):
     rows_all, cols = master.shape
     rows = rows_all // 8 * part[1]
     r = part[0] // part[1]
@@ -128,11 +133,11 @@
     tile = 768
     state = pl.BlockSpec((rows, tile), lambda t: (r, t))
     in_specs = (
-        [pl.BlockSpec((rows, scaled_t.shape[1]), lambda t: (r, 0))]
+        [pl.BlockSpec((scaled_all.shape[0], rows), lambda t: (0, r))]
         + [pl.BlockSpec((tokens, tile), lambda t: (0, t))] * len(acts)
         + [state] * 3
     )
-    operands = [scaled_t, *acts, master, moment, second]
+    operands = [scaled_all, *acts, master, moment, second]
     aliases = {}
     if prior is not None:
         for i, array in enumerate(prior):
@@ -150,6 +155,7 @@
         out_specs=[state] * 4 + [pl.BlockSpec((rows, tile), lambda t: (0, t))],
         out_shape=[full] * 4 + [jax.ShapeDtypeStruct((rows, cols), jnp.bfloat16)],
         input_output_aliases=aliases,
+        scratch_shapes=[pltpu.VMEM((rows, scaled_all.shape[0]), jnp.bfloat16)],
         compiler_params=pltpu.CompilerParams(vmem_limit_bytes=60 * 1024 * 1024),
         cost_estimate=SMALL,
         name="gradient_adam",
@@ -264,7 +270,13 @@
     )
     forward_act = send(pair_act, MIDDLE)
     far_one = send(middle_act, OUTWARD)
-    next_inward = send(own_next, INWARD)
+    inward, quarter = [], next_act.shape[0] // 4
+    for i in range(4):
+        part_next = own_next[i * quarter : (i + 1) * quarter]
+        if inward:
+            part_next, inward[-1] = after((part_next, inward[-1]))
+        inward.append(send(part_next, INWARD))
+    next_inward = jnp.concatenate(inward, axis=0)
     pieces = [
         pieces[0],
         pieces[1],
@@ -293,10 +305,10 @@
     third, given = after((third, given))
     third_swap = send(third, CORES)
     whole = jnp.concatenate([jnp.where(y == 0, part, given), jnp.where(y == 0, given, part)], 0)
-    scaled_t = whole.transpose(3, 1, 0, 2).reshape(half, 8 * tokens)
+    scaled_all = whole.transpose(1, 0, 2, 3).reshape(8 * tokens, half)
     own_next, third_swap = after((own_next, third_swap))
     next_own = [next_act, send(own_next, CORES)]
-    far_two, next_middle[0], scaled_t = after((far_two, next_middle[0], scaled_t))
+    far_two, next_middle[0], scaled_all = after((far_two, next_middle[0], scaled_all))
     fourth = jnp.where(inner, forward_act, far_two)
     fourth_swap = send(fourth, CORES)
     acts = [hidden_act, own_swap, pair_act, pair_swap, third, third_swap, fourth, fourth_swap]
@@ -307,37 +319,42 @@
     prior, owns, pairs = None, [], []
     for part in ROW_PARTS:
         behind = pairs[:1] if len(owns) == 2 else [next_own[1], next_inward]
-        prior, own = step_rows(part, scaled_t, acts, master, moment, second, prior, behind)
+        prior, own = step_rows(part, scaled_all, acts, master, moment, second, prior, behind)
         owns.append(own)
-        pairs.append(send(own, PAIR))
-    one, two = tuple(owns[:2] + pairs[:2]), (owns[2], pairs[2])
+        if len(owns) < 3:
+            pairs.append(send(own, PAIR))
+    last_rows = owns[2].shape[0] // 2
+    pairs += [send(part, PAIR) for part in (owns[2][:last_rows], owns[2][last_rows:])]
+    one, two = tuple(owns[:2] + pairs[:2]), (owns[2], *pairs[2:])
     both = tuple(owns + pairs)
 
     def swapped(array, behind):
         array, _ = after((array, behind))
         return [array, send(array, CORES)]
 
+    def sum_behind(stack, steps, behinds):
+        for step, behind in zip(steps, behinds):
+            given = lax.ppermute(stack[1], "tensor", [(i, i ^ step) for i in range(4)])
+            given, _ = after((given, behind))
+            stack = (stack[0].astype(jnp.float32) + given.astype(jnp.float32)).astype(jnp.bfloat16)
+        return stack
+
     near_one = products(place, True, next_own, one, owns[2:])
-    next_far = swapped(next_far, near_one)
+    next_far, pairs[2], _ = after((next_far, pairs[2], near_one))
+    next_far = [next_far, send(next_far, CORES)]
     far_one = products(place, False, next_far, one, [near_one])
     near_two = products(place, True, next_own, two, [far_one])
-    near_one, far_one = add_step(add_step(near_one, 1), 2), add_step(add_step(far_one, 2), 1)
     far_two = products(place, False, next_far, two, [near_two])
-    next_middle[0] = swapped(next_middle[0], near_one)
-    next_middle[1] = swapped(next_middle[1], near_two)
-    middle_one = products(place, False, next_middle[0], both, [far_two, near_one, far_one])
-    middle_two = products(place, True, next_middle[1], both, [middle_one])
-
-    def late_sum(stack, steps):
-        for step in steps:
-            given = lax.ppermute(stack[1], "tensor", [(i, i ^ step) for i in range(4)])
-            given, _ = after((given, middle_two))
-            stack = (stack[0].astype(jnp.float32) + given.astype(jnp.float32)).astype(jnp.bfloat16)
-        return stack
-
-    near = jnp.concatenate([near_one, late_sum(near_two, (1, 2))], axis=1)
-    far = jnp.concatenate([far_one, late_sum(far_two, (2, 1))], axis=1)
-    middle_one = late_sum(middle_one, (2, 1))
+    near_one = sum_behind(near_one, (1, 2), (far_one, near_two))
+    far_one = sum_behind(far_one, (2, 1), (near_two, far_two))
+    next_middle[0] = swapped(next_middle[0], near_two)
+    next_middle[1] = swapped(next_middle[1], far_two)
+    middle_one = products(place, False, next_middle[0], both, [far_two])
+    middle_two = products(place, True, next_middle[1], both, [middle_one, near_one, far_one])
+    soon, late = (middle_one, middle_two), (middle_two, middle_two)
+    near = jnp.concatenate([near_one, sum_behind(near_two, (1, 2), soon)], axis=1)
+    far = jnp.concatenate([far_one, sum_behind(far_two, (2, 1), soon)], axis=1)
+    middle_one = sum_behind(middle_one, (2, 1), late)
 
     own, across, outside = [(p, p) for p in range(4)], [(1, 2), (2, 1)], [(1, 3), (2, 0)]
     parts = [
@@ -349,7 +366,6 @@
         for side in (0, 1)
     ]
     given = lax.ppermute(middle_two[1], "tensor", [(i, i ^ 1) for i in range(4)])
-    given, parts = after((given, parts))
     last_sum = (middle_two[0].astype(jnp.float32) + given.astype(jnp.float32)).astype(jnp.bfloat16)
     for side in (0, 1):
         last = send_all(last_sum[0], homeward(across, side))

time: 411 us -> 405 us (0.985)
  waiting for transfers between devices: 184 us -> 168 us
  local copies, waits for them, and re-layouts: 24.4 us -> 34.7 us
    ppermute x10, waiting for transfers between devices: 25.7 us -> 14.8 us  [sum_behind(): given = lax.ppermute(stack[1], 'tensor', [(i, i ^ step) for i in range(4)])]
    unnamed x34 -> x55, local copies, waits for them, and re-layouts: 5.97 us -> 15.9 us
    ppermute x24 -> x28, waiting for transfers between devices: 127 us -> 118 us  [body_planes(): send = lambda array, pairs: lax.ppermute(array, 'dp', pairs)]
    slice x0 -> x2, local copies, waits for them, and re-layouts: none -> 6.35 us  [the longest x1 3.74 us: body_planes(): part_next = own_next[i * quarter:(i + 1) * quarter]]
    ppermute x10, starting transfers between devices: 22.3 us -> 16.2 us  [body_planes(): send_all = lambda array, pairs: lax.ppermute(array, ('dp', 'tensor'), pairs)]
    ppermute x24 -> x28, starting transfers between devices: 38.7 us -> 44.4 us  [body_planes(): send = lambda array, pairs: lax.ppermute(array, 'dp', pairs)]
  transfers between devices with their start and end apart: 47 -> 51, of which waited for: 23 -> 24; matrix products, arithmetic and copies ran while one was open for 9% -> 10% of each run, Pallas kernels for 27% -> 28%
where the time goes in v4:
time: 405 us; the launch traced here: 404 us
  waiting for transfers between devices  168 us (41%)
  Pallas kernels  111 us (27%)
  starting transfers between devices  71.3 us (18%)
  local copies, waits for them, and re-layouts  34.7 us (9%)
  other arithmetic  17.6 us (4%)
    ppermute x28, waiting for transfers between devices, body_planes(): send = lambda array, pairs: lax.ppermute(array, 'dp', pairs)  118 us
    pallas_call x6, Pallas kernels, products(): pl.pallas_call(functools.partial(product_kernel, x_first, len(weights), t...  63.2 us
    pallas_call x3, Pallas kernels, step_rows(): pl.pallas_call(functools.partial(step_kernel, len(acts), len(operands) -...  48.3 us
    ppermute x28, starting transfers between devices, body_planes(): send = lambda array, pairs: lax.ppermute(array, 'dp', pairs)  44.4 us
    ppermute x10, waiting for transfers between devices, body_planes(): send_all = lambda array, pairs: lax.ppermute(array, ('dp', 'tensor'), pairs)  21.3 us
    ppermute x10, starting transfers between devices, body_planes(): send_all = lambda array, pairs: lax.ppermute(array, ('dp', 'tensor'), pairs)  16.2 us
    unnamed x55, local copies, waits for them, and re-layouts  15.9 us
    ppermute x10, waiting for transfers between devices, sum_behind(): given = lax.ppermute(stack[1], 'tensor', [(i, i ^ step) for i in range(4)])  14.8 us
  transfers between devices with their start and end apart: 51, of which 24 were waited for; matrix products, arithmetic and copies ran while one was open for 10% of the time, Pallas kernels for 28%

profile of v4, /device:TPU:13, one launch (start us, length us, event | category | flops | bytes accessed | tf_op | source)
XLA Modules:
  0.0 404.0 jit_solution(4843577724467137487)
XLA Ops:
  0.9 4.3 %collective-permute-start.1 = (bf16[256,3840]{1,0:T(8,128)(2,1)}, bf16[256,3840]{1,0:T(8,128)(2,1)}, u32[]{:S(2)}, u32[]{:S(2)}) collective-permute-start(bf16[256,3840]{1,0:T(8,128)(2,1)} %refs_1_.5), channel_id=1, source_target_pairs={{8,16},{12,20},{16,8},{20,12},{9,17},{13,21},{17,9},{21,13},{10,18... | collective-permute-start | bytes 5898248 | tf_op jit(solution)/shard_map/ppermute | solution.py:244
  8.5 2.3 multiply_convert_fusion
  13.9 2.2 fusion.13
  16.0 31.5 %collective-permute-done.2 = bf16[64,1024]{1,0:T(8,128)(2,1)S(1)} collective-permute-done((bf16[64,1024]{1,0:T(8,128)(2,1)S(1)}, bf16[64,1024]{1,0:T(8,128)(2,1)S(1)}, u32[]{:S(2)}, u32[]{:S(2)}) %collective-permute-start.2) | collective-permute-done | bytes 131104 | tf_op jit(solution)/shard_map/ppermute | solution.py:244
  47.5 7.5 %collective-permute-done.3 = bf16[64,1024]{1,0:T(8,128)(2,1)S(1)} collective-permute-done((bf16[64,1024]{1,0:T(8,128)(2,1)S(1)}, bf16[64,1024]{1,0:T(8,128)(2,1)S(1)}, u32[]{:S(2)}, u32[]{:S(2)}) %collective-permute-start.3) | collective-permute-done | bytes 131104 | tf_op jit(solution)/shard_map/ppermute | solution.py:244
  55.0 3.9 collective-permute-done.4
  60.8 3.4 collective-permute-start.5
  64.1 2.6 collective-permute-start.6
  67.4 3.7 fusion.12
  73.8 12.4 %collective-permute-done.10 = bf16[1,8,64,512]{3,2,1,0:T(8,128)(2,1)S(1)} collective-permute-done((bf16[1,8,64,512]{3,2,1,0:T(8,128)(2,1)S(1)}, bf16[1,8,64,512]{3,2,1,0:T(8,128)(2,1)S(1)}, u32[]{:S(2)}, u32[]{:S(2)}) %collective-permute-start.10) | collective-permute-done | bytes 524320 | tf_op jit(solution)/shard_map/ppermute | solution.py:292
  86.7 10.0 %collective-permute-done.17 = bf16[128,3840]{1,0:T(8,128)(2,1)S(1)} collective-permute-done((bf16[128,3840]{1,0:T(8,128)(2,1)}, bf16[128,3840]{1,0:T(8,128)(2,1)S(1)}, u32[]{:S(2)}, u32[]{:S(2)}) %collective-permute-start.17) | collective-permute-done | bytes 983072 | tf_op jit(solution)/shard_map/ppermute | solution.py:244
  98.0 8.8 %collective-permute-done.5 = bf16[256,3840]{1,0:T(8,128)(2,1)} collective-permute-done((bf16[256,3840]{1,0:T(8,128)(2,1)}, bf16[256,3840]{1,0:T(8,128)(2,1)}, u32[]{:S(2)}, u32[]{:S(2)}) %collective-permute-start.5) | collective-permute-done | bytes 1966112 | tf_op jit(solution)/shard_map/ppermute | solution.py:244
  113.1 5.0 %collective-permute-start.11 = (bf16[256,3840]{1,0:T(8,128)(2,1)}, bf16[256,3840]{1,0:T(8,128)(2,1)}, u32[]{:S(2)}, u32[]{:S(2)}) collective-permute-start(bf16[256,3840]{1,0:T(8,128)(2,1)} %collective-permute-done.5), channel_id=1, source_target_pairs={{8,0},{12,4},{16,24},{20,28},{9,1},{13,5},{17,25},{21,29},{10,2},{... | collective-permute-start | bytes 5898248 | tf_op jit(solution)/shard_map/ppermute | solution.py:244
  118.0 2.3 collective-permute-start.12
  123.5 2.3 constant_dynamic-update-slice_fusion.3
  125.8 20.1 %collective-permute-done.19 = bf16[128,3840]{1,0:T(8,128)(2,1)} collective-permute-done((bf16[128,3840]{1,0:T(8,128)(2,1)S(1)}, bf16[128,3840]{1,0:T(8,128)(2,1)}, u32[]{:S(2)}, u32[]{:S(2)}) %collective-permute-start.19) | collective-permute-done | bytes 983072 | tf_op jit(solution)/shard_map/ppermute | solution.py:244
  147.2 2.5 collective-permute-start.16
  152.7 6.6 %collective-permute-done.11 = bf16[256,3840]{1,0:T(8,128)(2,1)} collective-permute-done((bf16[256,3840]{1,0:T(8,128)(2,1)}, bf16[256,3840]{1,0:T(8,128)(2,1)}, u32[]{:S(2)}, u32[]{:S(2)}) %collective-permute-start.11) | collective-permute-done | bytes 1966112 | tf_op jit(solution)/shard_map/ppermute | solution.py:244
  159.3 5.0 %collective-permute-done.12.mine_ref = bf16[256,3840]{1,0:T(8,128)(2,1)} collective-permute-done((bf16[256,3840]{1,0:T(8,128)(2,1)}, bf16[256,3840]{1,0:T(8,128)(2,1)}, u32[]{:S(2)}, u32[]{:S(2)}) %collective-permute-start.12) | collective-permute-done | bytes 1966112 | tf_op jit(solution)/shard_map/ppermute | solution.py:244
  164.4 1.8 broadcast_select_fusion.refs_7_
  168.4 2.2 constant_dynamic-update-slice_fusion.1
  171.7 2.3 collective-permute-start.24
  175.3 1.9 copy-done.1
  177.2 14.1 %gradient_adam.3 = (f32[512,3840]{1,0:T(8,128)}, f32[512,3840]{1,0:T(8,128)}, f32[512,3840]{1,0:T(8,128)}, f32[512,3840]{1,0:T(8,128)}, bf16[128,3840]{1,0:T(8,128)(2,1)}) custom-call(bf16[2048,512]{1,0:T(8,128)(2,1)} %bitcast.100, bf16[256,3840]{1,0:T(8,128)(2,1)} %refs_1_.5, bf16[256,3840]{1,0:T(8,128)(2,1)} %collective-permute-done.7.refs_2_, ...), custom_call_target="tpu_custom_call" | custom-call | flops 1000 | bytes 1000 | tf_op jit(solution)/shard_map/gradient_adam/pallas_call | solution.py:151
  191.4 13.9 %gradient_adam.4 = (f32[512,3840]{1,0:T(8,128)}, f32[512,3840]{1,0:T(8,128)}, f32[512,3840]{1,0:T(8,128)}, f32[512,3840]{1,0:T(8,128)}, bf16[128,3840]{1,0:T(8,128)(2,1)}) custom-call(bf16[2048,512]{1,0:T(8,128)(2,1)} %bitcast.101, bf16[256,3840]{1,0:T(8,128)(2,1)} %refs_1_.5, ...), custom_call_target="tpu_custom_call", output_to_operand_aliasing={{0}: (12, {}), {1}: (13, {}), {2}: (14, {}), {3}: (15, {})} | custom-call | flops 1000 | bytes 1000 | tf_op jit(solution)/shard_map/gradient_adam/pallas_call | solution.py:151
  206.8 6.3 %collective-permute-done.21.refs_16_.refs_2_.refs_3_ = bf16[128,3840]{1,0:T(8,128)(2,1)S(1)} collective-permute-done((bf16[128,3840]{1,0:T(8,128)(2,1)}, bf16[128,3840]{1,0:T(8,128)(2,1)S(1)}, u32[]{:S(2)}, u32[]{:S(2)}) %collective-permute-start.21) | collective-permute-done | bytes 983072 | tf_op jit(solution)/shard_map/ppermute | solution.py:244
  214.1 20.2 %gradient_adam.5 = (f32[512,3840]{1,0:T(8,128)}, f32[512,3840]{1,0:T(8,128)}, f32[512,3840]{1,0:T(8,128)}, f32[512,3840]{1,0:T(8,128)}, bf16[256,3840]{1,0:T(8,128)(2,1)}) custom-call(bf16[2048,512]{1,0:T(8,128)(2,1)} %bitcast.102, bf16[256,3840]{1,0:T(8,128)(2,1)} %refs_1_.5, ...), custom_call_target="tpu_custom_call", output_to_operand_aliasing={{0}: (12, {}), {1}: (13, {}), {2}: (14, {}), {3}: (15, {})} | custom-call | flops 1000 | bytes 1000 | tf_op jit(solution)/shard_map/gradient_adam/pallas_call | solution.py:151
  234.4 2.6 fusion.15
  238.8 10.3 %product.6.refs_4_ = bf16[2,2,512,256]{3,2,1,0:T(8,128)(2,1)} custom-call(s32[2]{0:T(128)} %pad_add_fusion.place_ref, bf16[512,3840]{1,0:T(8,128)(2,1)} %mine_ref.3, bf16[512,3840]{1,0:T(8,128)(2,1)} %copy-done.1, bf16[128,3840]{1,0:T(8,128)(2,1)} %get-tuple-element.105.refs_0_, bf16[128,3840]{1,0:T(8,128)(2,1)} %get-tuple-element.110.refs_1_, ...), custom_call_target="tpu_custom_call" | custom-call | flops 1000 | bytes 1000 | tf_op jit(solution)/shard_map/product/pallas_call | solution.py:218
  249.1 9.7 %collective-permute-done.24.mine_ref = bf16[512,3840]{1,0:T(8,128)(2,1)} collective-permute-done((bf16[512,3840]{1,0:T(8,128)(2,1)}, bf16[512,3840]{1,0:T(8,128)(2,1)}, u32[]{:S(2)}, u32[]{:S(2)}) %collective-permute-start.24) | collective-permute-done | bytes 3932192 | tf_op jit(solution)/shard_map/ppermute | solution.py:244
  258.8 2.4 collective-permute-start.26
  261.3 3.1 collective-permute-start.32
  264.5 1.9 slice_bitcast_fusion.10
  267.9 1.9 copy-done.7
  269.8 10.3 %product.7.refs_3_ = bf16[2,2,512,256]{3,2,1,0:T(8,128)(2,1)} custom-call(s32[2]{0:T(128)} %pad_add_fusion.place_ref, bf16[512,3840]{1,0:T(8,128)(2,1)} %collective-permute-done.24.mine_ref, bf16[512,3840]{1,0:T(8,128)(2,1)} %copy-done.7, bf16[128,3840]{1,0:T(8,128)(2,1)} %get-tuple-element.105.refs_0_, bf16[128,3840]{1,0:T(8,128)(2,1)} %get-tuple-element.110.refs_1_, ...), custom_call_target="tpu_custom_call" | custom-call | flops 1000 | bytes 1000 | tf_op jit(solution)/shard_map/product/pallas_call | solution.py:218
  281.5 6.4 %collective-permute-done.28.refs_2_.refs_6_ = bf16[128,3840]{1,0:T(8,128)(2,1)} collective-permute-done((bf16[128,3840]{1,0:T(8,128)(2,1)}, bf16[128,3840]{1,0:T(8,128)(2,1)}, u32[]{:S(2)}, u32[]{:S(2)}) %collective-permute-start.28) | collective-permute-done | bytes 983072 | tf_op jit(solution)/shard_map/ppermute | solution.py:244
  287.8 10.3 %product.8.refs_3_ = bf16[2,2,512,256]{3,2,1,0:T(8,128)(2,1)} custom-call(s32[2]{0:T(128)} %pad_add_fusion.place_ref, bf16[512,3840]{1,0:T(8,128)(2,1)} %mine_ref.3, bf16[512,3840]{1,0:T(8,128)(2,1)} %copy-done.1, bf16[256,3840]{1,0:T(8,128)(2,1)} %get-tuple-element.111.refs_4_.refs_0_.refs_2_, bf16[128,3840]{1,0:T(8,128)(2,1)} %collective-permute-done.25.refs_1_.refs_5_, ...), custom_call_target="tpu_custom_call" | custom-call | flops 1000 | bytes 1000 | tf_op jit(solution)/shard_map/product/pallas_call | solution.py:218
  299.3 10.3 %product.9.refs_7_ = bf16[2,2,512,256]{3,2,1,0:T(8,128)(2,1)} custom-call(s32[2]{0:T(128)} %pad_add_fusion.place_ref, bf16[512,3840]{1,0:T(8,128)(2,1)} %collective-permute-done.24.mine_ref, bf16[512,3840]{1,0:T(8,128)(2,1)} %copy-done.7, bf16[256,3840]{1,0:T(8,128)(2,1)} %get-tuple-element.111.refs_4_.refs_0_.refs_2_, ...), custom_call_target="tpu_custom_call" | custom-call | flops 1000 | bytes 1000 | tf_op jit(solution)/shard_map/product/pallas_call | solution.py:218
  315.9 2.8 collective-permute-done.27
  321.4 10.9 %product.10.refs_7_ = bf16[2,2,256,512]{3,2,1,0:T(8,128)(2,1)} custom-call(s32[2]{0:T(128)} %pad_add_fusion.place_ref, bf16[256,3840]{1,0:T(8,128)(2,1)} %collective-permute-done.12.mine_ref, bf16[256,3840]{1,0:T(8,128)(2,1)} %collective-permute-done.30.other_ref, bf16[128,3840]{1,0:T(8,128)(2,1)} %get-tuple-element.105.refs_0_, ...), custom_call_target="tpu_custom_call" | custom-call | flops 1000 | bytes 1000 | tf_op jit(solution)/shard_map/product/pallas_call | solution.py:218
  333.6 11.1 %product.11 = bf16[2,2,256,512]{3,2,1,0:T(8,128)(2,1)} custom-call(s32[2]{0:T(128)} %pad_add_fusion.place_ref, bf16[256,3840]{1,0:T(8,128)(2,1)} %collective-permute-done.32.mine_ref, bf16[256,3840]{1,0:T(8,128)(2,1)} %copy-done.20, bf16[128,3840]{1,0:T(8,128)(2,1)} %get-tuple-element.105.refs_0_, bf16[128,3840]{1,0:T(8,128)(2,1)} %get-tuple-element.110.refs_1_, ...), custom_call_target="tpu_custom_call" | custom-call | flops 1000 | bytes 1000 | tf_op jit(solution)/shard_map/product/pallas_call | solution.py:218
  351.5 11.0 %collective-permute-done.38 = bf16[512,256]{1,0:T(8,128)(2,1)S(1)} collective-permute-done((bf16[512,256]{1,0:T(8,128)(2,1)S(1)}, bf16[512,256]{1,0:T(8,128)(2,1)S(1)}, u32[]{:S(2)}, u32[]{:S(2)}) %collective-permute-start.38) | collective-permute-done | bytes 262176 | tf_op jit(solution)/shard_map/ppermute | solution.py:337
  368.7 8.9 %collective-permute-done.44 = bf16[256,512]{1,0:T(8,128)(2,1)S(1)} collective-permute-done((bf16[256,512]{1,0:T(8,128)(2,1)S(1)}, bf16[256,512]{1,0:T(8,128)(2,1)S(1)}, u32[]{:S(2)}, u32[]{:S(2)}) %collective-permute-start.44) | collective-permute-done | bytes 262176 | tf_op jit(solution)/shard_map/ppermute | solution.py:246
  377.5 3.5 collective-permute-start.49
  381.1 2.1 collective-permute-start.50
  386.0 7.8 %collective-permute-done.50 = bf16[256,512]{1,0:T(8,128)(2,1)S(1)} collective-permute-done((bf16[256,512]{1,0:T(8,128)(2,1)S(1)}, bf16[256,512]{1,0:T(8,128)(2,1)S(1)}, u32[]{:S(2)}, u32[]{:S(2)}) %collective-permute-start.50) | collective-permute-done | bytes 262176 | tf_op jit(solution)/shard_map/ppermute | solution.py:246
  395.3 2.6 collective-permute-start.48
  398.1 3.1 collective-permute-done.46
  (173 shorter events, 70.2 us)
Async XLA Ops:
  0.6 58.2 %collective-permute-start = (bf16[256,3840]{1,0:T(8,128)(2,1)}, bf16[256,3840]{1,0:T(8,128)(2,1)}, u32[]{:S(2)}, u32[]{:S(2)}) collective-permute-start(bf16[256,3840]{1,0:T(8,128)(2,1)} %refs_1_.5), channel_id=1, source_target_pairs={{0,8},{4,12},{8,0},{12,4},{16,24},{20,28},{24,16},{28,20},{1,9},{5... | collective-permute-start | bytes 5898248 | tf_op jit(solution)/shard_map/ppermute | solution.py:244
  0.9 58.0 %collective-permute-start.1 = (bf16[256,3840]{1,0:T(8,128)(2,1)}, bf16[256,3840]{1,0:T(8,128)(2,1)}, u32[]{:S(2)}, u32[]{:S(2)}) collective-permute-start(bf16[256,3840]{1,0:T(8,128)(2,1)} %refs_1_.5), channel_id=1, source_target_pairs={{8,16},{12,20},{16,8},{20,12},{9,17},{13,21},{17,9},{21,13},{10,18... | collective-permute-start | bytes 5898248 | tf_op jit(solution)/shard_map/ppermute | solution.py:244
  11.2 36.4 %collective-permute-start.2 = (bf16[64,1024]{1,0:T(8,128)(2,1)S(1)}, bf16[64,1024]{1,0:T(8,128)(2,1)S(1)}, u32[]{:S(2)}, u32[]{:S(2)}) collective-permute-start(bf16[64,1024]{1,0:T(8,128)(2,1)S(1)} %get-tuple-element.139), channel_id=1, source_target_pairs={{0,8},{4,12},{8,0},{12,4},{16,24},{20,28},{24,16},{28,20},{1,9},{5... | collective-permute-start | bytes 393224 | tf_op jit(solution)/shard_map/ppermute | solution.py:244
  11.2 43.7 %collective-permute-start.3 = (bf16[64,1024]{1,0:T(8,128)(2,1)S(1)}, bf16[64,1024]{1,0:T(8,128)(2,1)S(1)}, u32[]{:S(2)}, u32[]{:S(2)}) collective-permute-start(bf16[64,1024]{1,0:T(8,128)(2,1)S(1)} %get-tuple-element.138), channel_id=1, source_target_pairs={{0,16},{4,20},{8,24},{12,28},{16,0},{20,4},{24,8},{28,12},{1,17},{... | collective-permute-start | bytes 393224 | tf_op jit(solution)/shard_map/ppermute | solution.py:244
  12.4 46.4 %collective-permute-start.4 = (bf16[64,1024]{1,0:T(8,128)(2,1)S(1)}, bf16[64,1024]{1,0:T(8,128)(2,1)S(1)}, u32[]{:S(2)}, u32[]{:S(2)}) collective-permute-start(bf16[64,1024]{1,0:T(8,128)(2,1)S(1)} %get-tuple-element.137), channel_id=1, source_target_pairs={{0,24},{4,28},{8,16},{12,20},{16,8},{20,12},{24,0},{28,4},{1,25},{... | collective-permute-start | bytes 393224 | tf_op jit(solution)/shard_map/ppermute | solution.py:244
  58.9 7.8 %collective-permute-start.7 = (bf16[256,3840]{1,0:T(8,128)(2,1)S(1)}, bf16[256,3840]{1,0:T(8,128)(2,1)}, u32[]{:S(2)}, u32[]{:S(2)}) collective-permute-start(bf16[256,3840]{1,0:T(8,128)(2,1)S(1)} %copy-done.5), channel_id=1, source_target_pairs={{0,4},{4,0},{8,12},{12,8},{16,20},{20,16},{24,28},{28,24},{1,5},{5... | collective-permute-start | bytes 5898248 | tf_op jit(solution)/shard_map/ppermute | solution.py:244
  60.6 11.8 %collective-permute-start.9 = (bf16[4,64,512]{2,1,0:T(8,128)(2,1)S(1)}, bf16[4,64,512]{2,1,0:T(8,128)(2,1)S(1)}, u32[]{:S(2)}, u32[]{:S(2)}) collective-permute-start(bf16[4,64,512]{2,1,0:T(8,128)(2,1)S(1)} %get-tuple-element.148), channel_id=1, source_target_pairs={{0,4},{4,0},{8,12},{12,8},{16,20},{20,16},{24,28},{28,24},{1,5},{5... | collective-permute-start | bytes 786440 | tf_op jit(solution)/shard_map/ppermute | solution.py:244
  60.8 46.1 %collective-permute-start.5 = (bf16[256,3840]{1,0:T(8,128)(2,1)}, bf16[256,3840]{1,0:T(8,128)(2,1)}, u32[]{:S(2)}, u32[]{:S(2)}) collective-permute-start(bf16[256,3840]{1,0:T(8,128)(2,1)} %collective-permute-done.refs_3_), channel_id=1, source_target_pairs={{8,16},{12,20},{16,8},{20,12},{9,17},{13,21},{17,9},{21,13},{10,18... | collective-permute-start | bytes 5898248 | tf_op jit(solution)/shard_map/ppermute | solution.py:244
  64.1 43.3 %collective-permute-start.6 = (bf16[256,3840]{1,0:T(8,128)(2,1)}, bf16[256,3840]{1,0:T(8,128)(2,1)}, u32[]{:S(2)}, u32[]{:S(2)}) collective-permute-start(bf16[256,3840]{1,0:T(8,128)(2,1)} %collective-permute-done.1), channel_id=1, source_target_pairs={{8,0},{12,4},{16,24},{20,28},{9,1},{13,5},{17,25},{21,29},{10,2},{... | collective-permute-start | bytes 5898248 | tf_op jit(solution)/shard_map/ppermute | solution.py:244
  66.7 40.8 %collective-permute-start.8 = (bf16[256,3840]{1,0:T(8,128)(2,1)}, bf16[256,3840]{1,0:T(8,128)(2,1)}, u32[]{:S(2)}, u32[]{:S(2)}) collective-permute-start(bf16[256,3840]{1,0:T(8,128)(2,1)} %collective-permute-done.refs_3_), channel_id=1, source_target_pairs={{0,4},{4,0},{8,12},{12,8},{16,20},{20,16},{24,28},{28,24},{1,5},{5... | collective-permute-start | bytes 5898248 | tf_op jit(solution)/shard_map/ppermute | solution.py:244
  71.2 25.6 %collective-permute-start.17 = (bf16[128,3840]{1,0:T(8,128)(2,1)}, bf16[128,3840]{1,0:T(8,128)(2,1)S(1)}, u32[]{:S(2)}, u32[]{:S(2)}) collective-permute-start(bf16[128,3840]{1,0:T(8,128)(2,1)} %get-tuple-element.131), channel_id=1, source_target_pairs={{0,8},{4,12},{24,16},{28,20},{1,9},{5,13},{25,17},{29,21},{2,10},{... | collective-permute-start | bytes 2949128 | tf_op jit(solution)/shard_map/ppermute | solution.py:244
  72.5 13.7 %collective-permute-start.10 = (bf16[1,8,64,512]{3,2,1,0:T(8,128)(2,1)S(1)}, bf16[1,8,64,512]{3,2,1,0:T(8,128)(2,1)S(1)}, u32[]{:S(2)}, u32[]{:S(2)}) collective-permute-start(bf16[1,8,64,512]{3,2,1,0:T(8,128)(2,1)S(1)} %bitcast.103), channel_id=1, source_target_pairs={{0,1},{1,0},{2,3},{3,2},{4,5},{5,4},{6,7},{7,6},{8,9},{9,8},{10,11... | collective-permute-start | bytes 1572872 | tf_op jit(solution)/shard_map/ppermute | solution.py:292
  86.4 24.1 %collective-permute-start.13 = (bf16[2,8,64,512]{3,2,1,0:T(8,128)(2,1)S(1)}, bf16[2,8,64,512]{3,2,1,0:T(8,128)(2,1)S(1)}, u32[]{:S(2)}, u32[]{:S(2)}) collective-permute-start(bf16[2,8,64,512]{3,2,1,0:T(8,128)(2,1)S(1)} %pad_maximum_fusion), channel_id=1, source_target_pairs={{0,2},{1,3},{2,0},{3,1},{4,6},{5,7},{6,4},{7,5},{8,10},{9,11},{10,... | collective-permute-start | bytes 3145736 | tf_op jit(solution)/shard_map/ppermute | solution.py:294
  96.7 24.5 %collective-permute-start.18 = (bf16[128,3840]{1,0:T(8,128)(2,1)S(1)}, bf16[128,3840]{1,0:T(8,128)(2,1)S(1)}, u32[]{:S(2)}, u32[]{:S(2)}) collective-permute-start(bf16[128,3840]{1,0:T(8,128)(2,1)S(1)} %copy-done.25), channel_id=1, source_target_pairs={{0,8},{4,12},{24,16},{28,20},{1,9},{5,13},{25,17},{29,21},{2,10},{... | collective-permute-start | bytes 2949128 | tf_op jit(solution)/shard_map/ppermute | solution.py:244
  111.5 35.7 %collective-permute-start.14 = (bf16[256,3840]{1,0:T(8,128)(2,1)S(1)}, bf16[256,3840]{1,0:T(8,128)(2,1)}, u32[]{:S(2)}, u32[]{:S(2)}) collective-permute-start(bf16[256,3840]{1,0:T(8,128)(2,1)S(1)} %broadcast_select_fusion.1.refs_5_), channel_id=1, source_target_pairs={{0,4},{4,0},{8,12},{12,8},{16,20},{20,16},{24,28},{28,24},{1,5},{5... | collective-permute-start | bytes 5898248 | tf_op jit(solution)/shard_map/ppermute | solution.py:244
  113.1 46.3 %collective-permute-start.11 = (bf16[256,3840]{1,0:T(8,128)(2,1)}, bf16[256,3840]{1,0:T(8,128)(2,1)}, u32[]{:S(2)}, u32[]{:S(2)}) collective-permute-start(bf16[256,3840]{1,0:T(8,128)(2,1)} %collective-permute-done.5), channel_id=1, source_target_pairs={{8,0},{12,4},{16,24},{20,28},{9,1},{13,5},{17,25},{21,29},{10,2},{... | collective-permute-start | bytes 5898248 | tf_op jit(solution)/shard_map/ppermute | solution.py:244
  118.0 46.3 %collective-permute-start.12 = (bf16[256,3840]{1,0:T(8,128)(2,1)}, bf16[256,3840]{1,0:T(8,128)(2,1)}, u32[]{:S(2)}, u32[]{:S(2)}) collective-permute-start(bf16[256,3840]{1,0:T(8,128)(2,1)} %get-tuple-element.78), channel_id=1, source_target_pairs={{8,16},{12,20},{16,8},{20,12},{9,17},{13,21},{17,9},{21,13},{10,18... | collective-permute-start | bytes 5898248 | tf_op jit(solution)/shard_map/ppermute | solution.py:244
  122.2 23.7 %collective-permute-start.19 = (bf16[128,3840]{1,0:T(8,128)(2,1)S(1)}, bf16[128,3840]{1,0:T(8,128)(2,1)}, u32[]{:S(2)}, u32[]{:S(2)}) collective-permute-start(bf16[128,3840]{1,0:T(8,128)(2,1)S(1)} %get-tuple-element.94), channel_id=1, source_target_pairs={{0,8},{4,12},{24,16},{28,20},{1,9},{5,13},{25,17},{29,21},{2,10},{... | collective-permute-start | bytes 2949128 | tf_op jit(solution)/shard_map/ppermute | solution.py:244
  145.9 24.7 %collective-permute-start.20 = (bf16[128,3840]{1,0:T(8,128)(2,1)}, bf16[128,3840]{1,0:T(8,128)(2,1)S(1)}, u32[]{:S(2)}, u32[]{:S(2)}) collective-permute-start(bf16[128,3840]{1,0:T(8,128)(2,1)} %get-tuple-element.96), channel_id=1, source_target_pairs={{0,8},{4,12},{24,16},{28,20},{1,9},{5,13},{25,17},{29,21},{2,10},{... | collective-permute-start | bytes 2949128 | tf_op jit(solution)/shard_map/ppermute | solution.py:244
  147.2 28.1 %collective-permute-start.16 = (bf16[512,3840]{1,0:T(8,128)(2,1)}, bf16[512,3840]{1,0:T(8,128)(2,1)S(1)}, u32[]{:S(2)}, u32[]{:S(2)}) collective-permute-start(bf16[512,3840]{1,0:T(8,128)(2,1)} %mine_ref.3), channel_id=1, source_target_pairs={{0,4},{4,0},{8,12},{12,8},{16,20},{20,16},{24,28},{28,24},{1,5},{5... | collective-permute-start | bytes 11796488 | tf_op jit(solution)/shard_map/ppermute | solution.py:244
  166.2 7.8 %collective-permute-start.15 = (bf16[256,3840]{1,0:T(8,128)(2,1)S(1)}, bf16[256,3840]{1,0:T(8,128)(2,1)S(1)}, u32[]{:S(2)}, u32[]{:S(2)}) collective-permute-start(bf16[256,3840]{1,0:T(8,128)(2,1)S(1)} %broadcast_select_fusion.refs_7_), channel_id=1, source_target_pairs={{0,4},{4,0},{8,12},{12,8},{16,20},{20,16},{24,28},{28,24},{1,5},{5... | collective-permute-start | bytes 5898248 | tf_op jit(solution)/shard_map/ppermute | solution.py:244
  171.7 87.1 %collective-permute-start.24 = (bf16[512,3840]{1,0:T(8,128)(2,1)}, bf16[512,3840]{1,0:T(8,128)(2,1)}, u32[]{:S(2)}, u32[]{:S(2)}) collective-permute-start(bf16[512,3840]{1,0:T(8,128)(2,1)} %constant_dynamic-update-slice_fusion.refs_13_.refs_17_), channel_id=1, source_target_pairs={{8,16},{12,20},{16,8},{20,12},{9,17},{13,21},{17,9},{21,13},{10,18... | collective-permute-start | bytes 11796488 | tf_op jit(solution)/shard_map/ppermute | solution.py:244
  191.3 21.8 %collective-permute-start.21 = (bf16[128,3840]{1,0:T(8,128)(2,1)}, bf16[128,3840]{1,0:T(8,128)(2,1)S(1)}, u32[]{:S(2)}, u32[]{:S(2)}) collective-permute-start(bf16[128,3840]{1,0:T(8,128)(2,1)} %get-tuple-element.105.refs_0_), channel_id=1, source_target_pairs={{0,8},{4,12},{8,0},{12,4},{16,24},{20,28},{24,16},{28,20},{1,9},{5... | collective-permute-start | bytes 2949128 | tf_op jit(solution)/shard_map/ppermute | solution.py:244
  205.3 32.5 %collective-permute-start.22 = (bf16[128,3840]{1,0:T(8,128)(2,1)}, bf16[128,3840]{1,0:T(8,128)(2,1)S(1)}, u32[]{:S(2)}, u32[]{:S(2)}) collective-permute-start(bf16[128,3840]{1,0:T(8,128)(2,1)} %get-tuple-element.110.refs_1_), channel_id=1, source_target_pairs={{0,8},{4,12},{8,0},{12,4},{16,24},{20,28},{24,16},{28,20},{1,9},{5... | collective-permute-start | bytes 2949128 | tf_op jit(solution)/shard_map/ppermute | solution.py:244
  237.0 21.8 %collective-permute-start.25 = (bf16[128,3840]{1,0:T(8,128)(2,1)S(1)}, bf16[128,3840]{1,0:T(8,128)(2,1)}, u32[]{:S(2)}, u32[]{:S(2)}) collective-permute-start(bf16[128,3840]{1,0:T(8,128)(2,1)S(1)} %get-tuple-element.142), channel_id=1, source_target_pairs={{0,8},{4,12},{8,0},{12,4},{16,24},{20,28},{24,16},{28,20},{1,9},{5... | collective-permute-start | bytes 2949128 | tf_op jit(solution)/shard_map/ppermute | solution.py:244
  258.8 9.1 %collective-permute-start.26 = (bf16[512,3840]{1,0:T(8,128)(2,1)}, bf16[512,3840]{1,0:T(8,128)(2,1)S(1)}, u32[]{:S(2)}, u32[]{:S(2)}) collective-permute-start(bf16[512,3840]{1,0:T(8,128)(2,1)} %collective-permute-done.24.mine_ref), channel_id=1, source_target_pairs={{0,4},{4,0},{8,12},{12,8},{16,20},{20,16},{24,28},{28,24},{1,5},{5... | collective-permute-start | bytes 11796488 | tf_op jit(solution)/shard_map/ppermute | solution.py:244
  261.3 48.4 %collective-permute-start.32 = (bf16[256,3840]{1,0:T(8,128)(2,1)}, bf16[256,3840]{1,0:T(8,128)(2,1)}, u32[]{:S(2)}, u32[]{:S(2)}) collective-permute-start(bf16[256,3840]{1,0:T(8,128)(2,1)} %get-tuple-element.118), channel_id=1, source_target_pairs={{8,16},{12,20},{16,8},{20,12},{9,17},{13,21},{17,9},{21,13},{10,18... | collective-permute-start | bytes 5898248 | tf_op jit(solution)/shard_map/ppermute | solution.py:244
  264.4 23.4 %collective-permute-start.28 = (bf16[128,3840]{1,0:T(8,128)(2,1)}, bf16[128,3840]{1,0:T(8,128)(2,1)}, u32[]{:S(2)}, u32[]{:S(2)}) collective-permute-start(bf16[128,3840]{1,0:T(8,128)(2,1)} %get-tuple-element.141), channel_id=1, source_target_pairs={{0,8},{4,12},{8,0},{12,4},{16,24},{20,28},{24,16},{28,20},{1,9},{5... | collective-permute-start | bytes 2949128 | tf_op jit(solution)/shard_map/ppermute | solution.py:244
  266.3 31.8 %collective-permute-start.23 = (bf16[2,512,256]{2,1,0:T(8,128)(2,1)}, bf16[2,512,256]{2,1,0:T(8,128)(2,1)}, u32[]{:S(2)}, u32[]{:S(2)}) collective-permute-start(bf16[2,512,256]{2,1,0:T(8,128)(2,1)} %slice_bitcast_fusion.10), channel_id=1, source_target_pairs={{0,1},{1,0},{2,3},{3,2},{4,5},{5,4},{6,7},{7,6},{8,9},{9,8},{10,11... | collective-permute-start | bytes 1572872 | tf_op jit(solution)/shard_map/ppermute | solution.py:337
  281.2 31.1 %collective-permute-start.34 = (bf16[2,512,256]{2,1,0:T(8,128)(2,1)S(1)}, bf16[2,512,256]{2,1,0:T(8,128)(2,1)S(1)}, u32[]{:S(2)}, u32[]{:S(2)}) collective-permute-start(bf16[2,512,256]{2,1,0:T(8,128)(2,1)S(1)} %slice_bitcast_fusion.6), channel_id=1, source_target_pairs={{0,2},{1,3},{2,0},{3,1},{4,6},{5,7},{6,4},{7,5},{8,10},{9,11},{10,... | collective-permute-start | bytes 1572872 | tf_op jit(solution)/shard_map/ppermute | solution.py:337
  298.1 23.3 %collective-permute-start.30 = (bf16[256,3840]{1,0:T(8,128)(2,1)}, bf16[256,3840]{1,0:T(8,128)(2,1)}, u32[]{:S(2)}, u32[]{:S(2)}) collective-permute-start(bf16[256,3840]{1,0:T(8,128)(2,1)} %collective-permute-done.12.mine_ref), channel_id=1, source_target_pairs={{0,4},{4,0},{8,12},{12,8},{16,20},{20,16},{24,28},{28,24},{1,5},{5... | collective-permute-start | bytes 5898248 | tf_op jit(solution)/shard_map/ppermute | solution.py:244
  309.7 22.7 %collective-permute-start.33 = (bf16[256,3840]{1,0:T(8,128)(2,1)}, bf16[256,3840]{1,0:T(8,128)(2,1)S(1)}, u32[]{:S(2)}, u32[]{:S(2)}) collective-permute-start(bf16[256,3840]{1,0:T(8,128)(2,1)} %collective-permute-done.32.mine_ref), channel_id=1, source_target_pairs={{0,4},{4,0},{8,12},{12,8},{16,20},{20,16},{24,28},{28,24},{1,5},{5... | collective-permute-start | bytes 5898248 | tf_op jit(solution)/shard_map/ppermute | solution.py:244
  311.2 7.5 %collective-permute-start.27 = (bf16[512,256]{1,0:T(8,128)(2,1)S(1)}, bf16[512,256]{1,0:T(8,128)(2,1)S(1)}, u32[]{:S(2)}, u32[]{:S(2)}) collective-permute-start(bf16[512,256]{1,0:T(8,128)(2,1)S(1)} %slice_bitcast_fusion.22), channel_id=1, source_target_pairs={{0,2},{1,3},{2,0},{3,1},{4,6},{5,7},{6,4},{7,5},{8,10},{9,11},{10,... | collective-permute-start | bytes 786440 | tf_op jit(solution)/shard_map/ppermute | solution.py:337
  312.5 8.2 %collective-permute-start.35 = (bf16[512,256]{1,0:T(8,128)(2,1)S(1)}, bf16[512,256]{1,0:T(8,128)(2,1)S(1)}, u32[]{:S(2)}, u32[]{:S(2)}) collective-permute-start(bf16[512,256]{1,0:T(8,128)(2,1)S(1)} %slice_bitcast_fusion.18), channel_id=1, source_target_pairs={{0,1},{1,0},{2,3},{3,2},{4,5},{5,4},{6,7},{7,6},{8,9},{9,8},{10,11... | collective-permute-start | bytes 786440 | tf_op jit(solution)/shard_map/ppermute | solution.py:337
  314.6 31.6 %collective-permute-start.37 = (bf16[2,512,256]{2,1,0:T(8,128)(2,1)}, bf16[2,512,256]{2,1,0:T(8,128)(2,1)}, u32[]{:S(2)}, u32[]{:S(2)}) collective-permute-start(bf16[2,512,256]{2,1,0:T(8,128)(2,1)} %slice_bitcast_fusion.4), channel_id=1, source_target_pairs={{0,2},{1,3},{2,0},{3,1},{4,6},{5,7},{6,4},{7,5},{8,10},{9,11},{10,... | collective-permute-start | bytes 1572872 | tf_op jit(solution)/shard_map/ppermute | solution.py:337
  318.7 30.0 %collective-permute-start.29 = (bf16[2,512,256]{2,1,0:T(8,128)(2,1)}, bf16[2,512,256]{2,1,0:T(8,128)(2,1)}, u32[]{:S(2)}, u32[]{:S(2)}) collective-permute-start(bf16[2,512,256]{2,1,0:T(8,128)(2,1)} %slice_bitcast_fusion.8), channel_id=1, source_target_pairs={{0,1},{1,0},{2,3},{3,2},{4,5},{5,4},{6,7},{7,6},{8,9},{9,8},{10,11... | collective-permute-start | bytes 1572872 | tf_op jit(solution)/shard_map/ppermute | solution.py:337
  345.9 17.5 %collective-permute-start.43 = (bf16[2,256,512]{2,1,0:T(8,128)(2,1)S(1)}, bf16[2,256,512]{2,1,0:T(8,128)(2,1)S(1)}, u32[]{:S(2)}, u32[]{:S(2)}) collective-permute-start(bf16[2,256,512]{2,1,0:T(8,128)(2,1)S(1)} %slice_bitcast_fusion), channel_id=1, source_target_pairs={{0,1},{1,0},{2,3},{3,2},{4,5},{5,4},{6,7},{7,6},{8,9},{9,8},{10,11... | collective-permute-start | bytes 1572872 | tf_op jit(solution)/shard_map/ppermute | solution.py:368
  347.4 15.1 %collective-permute-start.38 = (bf16[512,256]{1,0:T(8,128)(2,1)S(1)}, bf16[512,256]{1,0:T(8,128)(2,1)S(1)}, u32[]{:S(2)}, u32[]{:S(2)}) collective-permute-start(bf16[512,256]{1,0:T(8,128)(2,1)S(1)} %slice_bitcast_fusion.16), channel_id=1, source_target_pairs={{0,1},{1,0},{2,3},{3,2},{4,5},{5,4},{6,7},{7,6},{8,9},{9,8},{10,11... | collective-permute-start | bytes 786440 | tf_op jit(solution)/shard_map/ppermute | solution.py:337
  349.9 13.5 %collective-permute-start.31 = (bf16[512,256]{1,0:T(8,128)(2,1)S(1)}, bf16[512,256]{1,0:T(8,128)(2,1)S(1)}, u32[]{:S(2)}, u32[]{:S(2)}) collective-permute-start(bf16[512,256]{1,0:T(8,128)(2,1)S(1)} %slice_bitcast_fusion.20), channel_id=1, source_target_pairs={{0,2},{1,3},{2,0},{3,1},{4,6},{5,7},{6,4},{7,5},{8,10},{9,11},{10,... | collective-permute-start | bytes 786440 | tf_op jit(solution)/shard_map/ppermute | solution.py:337
  350.4 15.6 %collective-permute-start.40 = (bf16[2,256,512]{2,1,0:T(8,128)(2,1)S(1)}, bf16[2,256,512]{2,1,0:T(8,128)(2,1)S(1)}, u32[]{:S(2)}, u32[]{:S(2)}) collective-permute-start(bf16[2,256,512]{2,1,0:T(8,128)(2,1)S(1)} %slice_bitcast_fusion.2), channel_id=1, source_target_pairs={{0,2},{1,3},{2,0},{3,1},{4,6},{5,7},{6,4},{7,5},{8,10},{9,11},{10,... | collective-permute-start | bytes 1572872 | tf_op jit(solution)/shard_map/ppermute | solution.py:337
  362.7 32.6 %collective-permute-start.39 = (bf16[512,512]{1,0:T(8,128)(2,1)S(1)}, bf16[512,512]{1,0:T(8,128)(2,1)S(1)}, u32[]{:S(2)}, u32[]{:S(2)}) collective-permute-start(bf16[512,512]{1,0:T(8,128)(2,1)S(1)} %pad_maximum_fusion.5), channel_id=1, source_target_pairs={{8,24},{9,25},{10,28},{11,29},{16,2},{17,3},{18,6},{19,7}} | collective-permute-start | bytes 1572872 | tf_op jit(solution)/shard_map/ppermute | solution.py:246
  363.6 14.0 %collective-permute-start.44 = (bf16[256,512]{1,0:T(8,128)(2,1)S(1)}, bf16[256,512]{1,0:T(8,128)(2,1)S(1)}, u32[]{:S(2)}, u32[]{:S(2)}) collective-permute-start(bf16[256,512]{1,0:T(8,128)(2,1)S(1)} %get-tuple-element.146), channel_id=1, source_target_pairs={{8,16},{9,17},{10,20},{11,21},{16,10},{17,11},{18,14},{19,15}} | collective-permute-start | bytes 786440 | tf_op jit(solution)/shard_map/ppermute | solution.py:246
  366.2 14.9 %collective-permute-start.41 = (bf16[256,512]{1,0:T(8,128)(2,1)S(1)}, bf16[256,512]{1,0:T(8,128)(2,1)S(1)}, u32[]{:S(2)}, u32[]{:S(2)}) collective-permute-start(bf16[256,512]{1,0:T(8,128)(2,1)S(1)} %slice_bitcast_fusion.14), channel_id=1, source_target_pairs={{0,1},{1,0},{2,3},{3,2},{4,5},{5,4},{6,7},{7,6},{8,9},{9,8},{10,11... | collective-permute-start | bytes 786440 | tf_op jit(solution)/shard_map/ppermute | solution.py:337
  366.7 31.2 %collective-permute-start.36 = (bf16[512,512]{1,0:T(8,128)(2,1)S(1)}, bf16[512,512]{1,0:T(8,128)(2,1)S(1)}, u32[]{:S(2)}, u32[]{:S(2)}) collective-permute-start(bf16[512,512]{1,0:T(8,128)(2,1)S(1)} %pad_maximum_fusion.4), channel_id=1, source_target_pairs={{0,0},{1,1},{2,4},{3,5},{8,8},{9,9},{10,12},{11,13},{16,18},{17,19... | collective-permute-start | bytes 1572872 | tf_op jit(solution)/shard_map/ppermute | solution.py:246
  367.4 15.9 %collective-permute-start.45 = (bf16[256,512]{1,0:T(8,128)(2,1)S(1)}, bf16[256,512]{1,0:T(8,128)(2,1)S(1)}, u32[]{:S(2)}, u32[]{:S(2)}) collective-permute-start(bf16[256,512]{1,0:T(8,128)(2,1)S(1)} %get-tuple-element.145), channel_id=1, source_target_pairs={{8,20},{9,21},{10,16},{11,17},{16,14},{17,15},{18,10},{19,11}} | collective-permute-start | bytes 786440 | tf_op jit(solution)/shard_map/ppermute | solution.py:246
  381.1 12.7 %collective-permute-start.50 = (bf16[256,512]{1,0:T(8,128)(2,1)S(1)}, bf16[256,512]{1,0:T(8,128)(2,1)S(1)}, u32[]{:S(2)}, u32[]{:S(2)}) collective-permute-start(bf16[256,512]{1,0:T(8,128)(2,1)S(1)} %get-tuple-element.145), channel_id=1, source_target_pairs={{12,20},{13,21},{14,16},{15,17},{20,14},{21,15},{22,10},{23,11}} | collective-permute-start | bytes 786440 | tf_op jit(solution)/shard_map/ppermute | solution.py:246
  383.3 14.6 %collective-permute-start.42 = (bf16[256,512]{1,0:T(8,128)(2,1)S(1)}, bf16[256,512]{1,0:T(8,128)(2,1)S(1)}, u32[]{:S(2)}, u32[]{:S(2)}) collective-permute-start(bf16[256,512]{1,0:T(8,128)(2,1)S(1)} %fusion.6), channel_id=1, source_target_pairs={{8,16},{9,17},{10,20},{11,21},{16,10},{17,11},{18,14},{19,15}} | collective-permute-start | bytes 786440 | tf_op jit(solution)/shard_map/ppermute | solution.py:246
  384.7 13.4 %collective-permute-start.47 = (bf16[512,512]{1,0:T(8,128)(2,1)S(1)}, bf16[512,512]{1,0:T(8,128)(2,1)S(1)}, u32[]{:S(2)}, u32[]{:S(2)}) collective-permute-start(bf16[512,512]{1,0:T(8,128)(2,1)S(1)} %pad_maximum_fusion.5), channel_id=1, source_target_pairs={{12,24},{13,25},{14,28},{15,29},{20,2},{21,3},{22,6},{23,7}} | collective-permute-start | bytes 1572872 | tf_op jit(solution)/shard_map/ppermute | solution.py:246
  (29 other events, 272.1 us)

commit v5 on v4

--- a/solution.py
+++ b/solution.py
@@ -130,7 +130,7 @@
     rows = rows_all // 8 * part[1]
     r = part[0] // part[1]
     tokens = acts[0].shape[0]
-    tile = 768
+    tile = 1280
     state = pl.BlockSpec((rows, tile), lambda t: (r, t))
     in_specs = (
         [pl.BlockSpec((scaled_all.shape[0], rows), lambda t: (0, r))]

time: 405 us -> 406 us (level)
  no operation moved by 1% of the time
where the time goes in v5:
time: 406 us; the launch traced here: 404 us
  waiting for transfers between devices  168 us (41%)
  Pallas kernels  111 us (27%)
  starting transfers between devices  71.7 us (18%)
  local copies, waits for them, and re-layouts  34.7 us (9%)
  other arithmetic  17.6 us (4%)
    ppermute x28, waiting for transfers between devices, body_planes(): send = lambda array, pairs: lax.ppermute(array, 'dp', pairs)  118 us
    pallas_call x6, Pallas kernels, products(): pl.pallas_call(functools.partial(product_kernel, x_first, len(weights), t...  63.3 us
    pallas_call x3, Pallas kernels, step_rows(): pl.pallas_call(functools.partial(step_kernel, len(acts), len(operands) -...  48 us
    ppermute x28, starting transfers between devices, body_planes(): send = lambda array, pairs: lax.ppermute(array, 'dp', pairs)  44.8 us
    ppermute x10, waiting for transfers between devices, body_planes(): send_all = lambda array, pairs: lax.ppermute(array, ('dp', 'tensor'), pairs)  21.3 us
    ppermute x10, starting transfers between devices, body_planes(): send_all = lambda array, pairs: lax.ppermute(array, ('dp', 'tensor'), pairs)  16.2 us
    unnamed x55, local copies, waits for them, and re-layouts  15.9 us
    ppermute x10, waiting for transfers between devices, sum_behind(): given = lax.ppermute(stack[1], 'tensor', [(i, i ^ step) for i in range(4)])  14.8 us
  transfers between devices with their start and end apart: 51, of which 24 were waited for; matrix products, arithmetic and copies ran while one was open for 10% of the time, Pallas kernels for 28%

profile of v5, /device:TPU:13, one launch (start us, length us, event | category | flops | bytes accessed | tf_op | source)
XLA Modules:
  0.0 404.1 jit_solution(14202378350196705472)
XLA Ops:
  0.9 4.3 %collective-permute-start.1 = (bf16[256,3840]{1,0:T(8,128)(2,1)}, bf16[256,3840]{1,0:T(8,128)(2,1)}, u32[]{:S(2)}, u32[]{:S(2)}) collective-permute-start(bf16[256,3840]{1,0:T(8,128)(2,1)} %refs_1_.5), channel_id=1, source_target_pairs={{8,16},{12,20},{16,8},{20,12},{9,17},{13,21},{17,9},{21,13},{10,18... | collective-permute-start | bytes 5898248 | tf_op jit(solution)/shard_map/ppermute | solution.py:244
  8.5 2.3 multiply_convert_fusion
  13.9 2.2 fusion.13
  16.0 31.5 %collective-permute-done.2 = bf16[64,1024]{1,0:T(8,128)(2,1)S(1)} collective-permute-done((bf16[64,1024]{1,0:T(8,128)(2,1)S(1)}, bf16[64,1024]{1,0:T(8,128)(2,1)S(1)}, u32[]{:S(2)}, u32[]{:S(2)}) %collective-permute-start.2) | collective-permute-done | bytes 131104 | tf_op jit(solution)/shard_map/ppermute | solution.py:244
  47.5 7.5 %collective-permute-done.3 = bf16[64,1024]{1,0:T(8,128)(2,1)S(1)} collective-permute-done((bf16[64,1024]{1,0:T(8,128)(2,1)S(1)}, bf16[64,1024]{1,0:T(8,128)(2,1)S(1)}, u32[]{:S(2)}, u32[]{:S(2)}) %collective-permute-start.3) | collective-permute-done | bytes 131104 | tf_op jit(solution)/shard_map/ppermute | solution.py:244
  55.0 3.9 collective-permute-done.4
  60.8 3.4 collective-permute-start.5
  64.1 2.6 collective-permute-start.6
  67.4 3.7 fusion.12
  73.8 12.4 %collective-permute-done.10 = bf16[1,8,64,512]{3,2,1,0:T(8,128)(2,1)S(1)} collective-permute-done((bf16[1,8,64,512]{3,2,1,0:T(8,128)(2,1)S(1)}, bf16[1,8,64,512]{3,2,1,0:T(8,128)(2,1)S(1)}, u32[]{:S(2)}, u32[]{:S(2)}) %collective-permute-start.10) | collective-permute-done | bytes 524320 | tf_op jit(solution)/shard_map/ppermute | solution.py:292
  86.7 10.0 %collective-permute-done.17 = bf16[128,3840]{1,0:T(8,128)(2,1)S(1)} collective-permute-done((bf16[128,3840]{1,0:T(8,128)(2,1)}, bf16[128,3840]{1,0:T(8,128)(2,1)S(1)}, u32[]{:S(2)}, u32[]{:S(2)}) %collective-permute-start.17) | collective-permute-done | bytes 983072 | tf_op jit(solution)/shard_map/ppermute | solution.py:244
  98.0 8.8 %collective-permute-done.5 = bf16[256,3840]{1,0:T(8,128)(2,1)} collective-permute-done((bf16[256,3840]{1,0:T(8,128)(2,1)}, bf16[256,3840]{1,0:T(8,128)(2,1)}, u32[]{:S(2)}, u32[]{:S(2)}) %collective-permute-start.5) | collective-permute-done | bytes 1966112 | tf_op jit(solution)/shard_map/ppermute | solution.py:244
  113.1 5.0 %collective-permute-start.11 = (bf16[256,3840]{1,0:T(8,128)(2,1)}, bf16[256,3840]{1,0:T(8,128)(2,1)}, u32[]{:S(2)}, u32[]{:S(2)}) collective-permute-start(bf16[256,3840]{1,0:T(8,128)(2,1)} %collective-permute-done.5), channel_id=1, source_target_pairs={{8,0},{12,4},{16,24},{20,28},{9,1},{13,5},{17,25},{21,29},{10,2},{... | collective-permute-start | bytes 5898248 | tf_op jit(solution)/shard_map/ppermute | solution.py:244
  118.0 2.3 collective-permute-start.12
  123.5 2.3 constant_dynamic-update-slice_fusion.3
  125.8 20.1 %collective-permute-done.19 = bf16[128,3840]{1,0:T(8,128)(2,1)} collective-permute-done((bf16[128,3840]{1,0:T(8,128)(2,1)S(1)}, bf16[128,3840]{1,0:T(8,128)(2,1)}, u32[]{:S(2)}, u32[]{:S(2)}) %collective-permute-start.19) | collective-permute-done | bytes 983072 | tf_op jit(solution)/shard_map/ppermute | solution.py:244
  147.2 2.5 collective-permute-start.16
  152.7 6.6 %collective-permute-done.11 = bf16[256,3840]{1,0:T(8,128)(2,1)} collective-permute-done((bf16[256,3840]{1,0:T(8,128)(2,1)}, bf16[256,3840]{1,0:T(8,128)(2,1)}, u32[]{:S(2)}, u32[]{:S(2)}) %collective-permute-start.11) | collective-permute-done | bytes 1966112 | tf_op jit(solution)/shard_map/ppermute | solution.py:244
  159.3 5.0 %collective-permute-done.12.mine_ref = bf16[256,3840]{1,0:T(8,128)(2,1)} collective-permute-done((bf16[256,3840]{1,0:T(8,128)(2,1)}, bf16[256,3840]{1,0:T(8,128)(2,1)}, u32[]{:S(2)}, u32[]{:S(2)}) %collective-permute-start.12) | collective-permute-done | bytes 1966112 | tf_op jit(solution)/shard_map/ppermute | solution.py:244
  164.4 1.8 broadcast_select_fusion.refs_7_
  168.4 2.2 constant_dynamic-update-slice_fusion.1
  171.7 2.5 collective-permute-start.24
  175.4 1.9 copy-done.1
  177.4 13.9 %gradient_adam.3 = (f32[512,3840]{1,0:T(8,128)}, f32[512,3840]{1,0:T(8,128)}, f32[512,3840]{1,0:T(8,128)}, f32[512,3840]{1,0:T(8,128)}, bf16[128,3840]{1,0:T(8,128)(2,1)}) custom-call(bf16[2048,512]{1,0:T(8,128)(2,1)} %bitcast.100, bf16[256,3840]{1,0:T(8,128)(2,1)} %refs_1_.5, bf16[256,3840]{1,0:T(8,128)(2,1)} %collective-permute-done.7.refs_2_, ...), custom_call_target="tpu_custom_call" | custom-call | flops 1000 | bytes 1000 | tf_op jit(solution)/shard_map/gradient_adam/pallas_call | solution.py:151
  191.3 13.8 %gradient_adam.4 = (f32[512,3840]{1,0:T(8,128)}, f32[512,3840]{1,0:T(8,128)}, f32[512,3840]{1,0:T(8,128)}, f32[512,3840]{1,0:T(8,128)}, bf16[128,3840]{1,0:T(8,128)(2,1)}) custom-call(bf16[2048,512]{1,0:T(8,128)(2,1)} %bitcast.101, bf16[256,3840]{1,0:T(8,128)(2,1)} %refs_1_.5, ...), custom_call_target="tpu_custom_call", output_to_operand_aliasing={{0}: (12, {}), {1}: (13, {}), {2}: (14, {}), {3}: (15, {})} | custom-call | flops 1000 | bytes 1000 | tf_op jit(solution)/shard_map/gradient_adam/pallas_call | solution.py:151
  206.6 6.5 %collective-permute-done.21.refs_16_.refs_2_.refs_3_ = bf16[128,3840]{1,0:T(8,128)(2,1)S(1)} collective-permute-done((bf16[128,3840]{1,0:T(8,128)(2,1)}, bf16[128,3840]{1,0:T(8,128)(2,1)S(1)}, u32[]{:S(2)}, u32[]{:S(2)}) %collective-permute-start.21) | collective-permute-done | bytes 983072 | tf_op jit(solution)/shard_map/ppermute | solution.py:244
  214.1 20.4 %gradient_adam.5 = (f32[512,3840]{1,0:T(8,128)}, f32[512,3840]{1,0:T(8,128)}, f32[512,3840]{1,0:T(8,128)}, f32[512,3840]{1,0:T(8,128)}, bf16[256,3840]{1,0:T(8,128)(2,1)}) custom-call(bf16[2048,512]{1,0:T(8,128)(2,1)} %bitcast.102, bf16[256,3840]{1,0:T(8,128)(2,1)} %refs_1_.5, ...), custom_call_target="tpu_custom_call", output_to_operand_aliasing={{0}: (12, {}), {1}: (13, {}), {2}: (14, {}), {3}: (15, {})} | custom-call | flops 1000 | bytes 1000 | tf_op jit(solution)/shard_map/gradient_adam/pallas_call | solution.py:151
  234.5 2.6 fusion.15
  238.9 10.3 %product.6.refs_4_ = bf16[2,2,512,256]{3,2,1,0:T(8,128)(2,1)} custom-call(s32[2]{0:T(128)} %pad_add_fusion.place_ref, bf16[512,3840]{1,0:T(8,128)(2,1)} %mine_ref.3, bf16[512,3840]{1,0:T(8,128)(2,1)} %copy-done.1, bf16[128,3840]{1,0:T(8,128)(2,1)} %get-tuple-element.105.refs_0_, bf16[128,3840]{1,0:T(8,128)(2,1)} %get-tuple-element.110.refs_1_, ...), custom_call_target="tpu_custom_call" | custom-call | flops 1000 | bytes 1000 | tf_op jit(solution)/shard_map/product/pallas_call | solution.py:218
  249.2 9.6 %collective-permute-done.24.mine_ref = bf16[512,3840]{1,0:T(8,128)(2,1)} collective-permute-done((bf16[512,3840]{1,0:T(8,128)(2,1)}, bf16[512,3840]{1,0:T(8,128)(2,1)}, u32[]{:S(2)}, u32[]{:S(2)}) %collective-permute-start.24) | collective-permute-done | bytes 3932192 | tf_op jit(solution)/shard_map/ppermute | solution.py:244
  258.8 2.5 collective-permute-start.26
  261.4 3.2 collective-permute-start.32
  264.6 1.9 slice_bitcast_fusion.10
  268.0 1.9 copy-done.7
  269.9 10.3 %product.7.refs_3_ = bf16[2,2,512,256]{3,2,1,0:T(8,128)(2,1)} custom-call(s32[2]{0:T(128)} %pad_add_fusion.place_ref, bf16[512,3840]{1,0:T(8,128)(2,1)} %collective-permute-done.24.mine_ref, bf16[512,3840]{1,0:T(8,128)(2,1)} %copy-done.7, bf16[128,3840]{1,0:T(8,128)(2,1)} %get-tuple-element.105.refs_0_, bf16[128,3840]{1,0:T(8,128)(2,1)} %get-tuple-element.110.refs_1_, ...), custom_call_target="tpu_custom_call" | custom-call | flops 1000 | bytes 1000 | tf_op jit(solution)/shard_map/product/pallas_call | solution.py:218
  281.6 6.4 %collective-permute-done.28.refs_2_.refs_6_ = bf16[128,3840]{1,0:T(8,128)(2,1)} collective-permute-done((bf16[128,3840]{1,0:T(8,128)(2,1)}, bf16[128,3840]{1,0:T(8,128)(2,1)}, u32[]{:S(2)}, u32[]{:S(2)}) %collective-permute-start.28) | collective-permute-done | bytes 983072 | tf_op jit(solution)/shard_map/ppermute | solution.py:244
  288.0 10.3 %product.8.refs_3_ = bf16[2,2,512,256]{3,2,1,0:T(8,128)(2,1)} custom-call(s32[2]{0:T(128)} %pad_add_fusion.place_ref, bf16[512,3840]{1,0:T(8,128)(2,1)} %mine_ref.3, bf16[512,3840]{1,0:T(8,128)(2,1)} %copy-done.1, bf16[256,3840]{1,0:T(8,128)(2,1)} %get-tuple-element.111.refs_4_.refs_0_.refs_2_, bf16[128,3840]{1,0:T(8,128)(2,1)} %collective-permute-done.25.refs_1_.refs_5_, ...), custom_call_target="tpu_custom_call" | custom-call | flops 1000 | bytes 1000 | tf_op jit(solution)/shard_map/product/pallas_call | solution.py:218
  299.5 10.3 %product.9.refs_7_ = bf16[2,2,512,256]{3,2,1,0:T(8,128)(2,1)} custom-call(s32[2]{0:T(128)} %pad_add_fusion.place_ref, bf16[512,3840]{1,0:T(8,128)(2,1)} %collective-permute-done.24.mine_ref, bf16[512,3840]{1,0:T(8,128)(2,1)} %copy-done.7, bf16[256,3840]{1,0:T(8,128)(2,1)} %get-tuple-element.111.refs_4_.refs_0_.refs_2_, ...), custom_call_target="tpu_custom_call" | custom-call | flops 1000 | bytes 1000 | tf_op jit(solution)/shard_map/product/pallas_call | solution.py:218
  316.0 2.8 collective-permute-done.27
  321.6 10.9 %product.10.refs_7_ = bf16[2,2,256,512]{3,2,1,0:T(8,128)(2,1)} custom-call(s32[2]{0:T(128)} %pad_add_fusion.place_ref, bf16[256,3840]{1,0:T(8,128)(2,1)} %collective-permute-done.12.mine_ref, bf16[256,3840]{1,0:T(8,128)(2,1)} %collective-permute-done.30.other_ref, bf16[128,3840]{1,0:T(8,128)(2,1)} %get-tuple-element.105.refs_0_, ...), custom_call_target="tpu_custom_call" | custom-call | flops 1000 | bytes 1000 | tf_op jit(solution)/shard_map/product/pallas_call | solution.py:218
  333.8 11.2 %product.11 = bf16[2,2,256,512]{3,2,1,0:T(8,128)(2,1)} custom-call(s32[2]{0:T(128)} %pad_add_fusion.place_ref, bf16[256,3840]{1,0:T(8,128)(2,1)} %collective-permute-done.32.mine_ref, bf16[256,3840]{1,0:T(8,128)(2,1)} %copy-done.20, bf16[128,3840]{1,0:T(8,128)(2,1)} %get-tuple-element.105.refs_0_, bf16[128,3840]{1,0:T(8,128)(2,1)} %get-tuple-element.110.refs_1_, ...), custom_call_target="tpu_custom_call" | custom-call | flops 1000 | bytes 1000 | tf_op jit(solution)/shard_map/product/pallas_call | solution.py:218
  351.7 11.0 %collective-permute-done.38 = bf16[512,256]{1,0:T(8,128)(2,1)S(1)} collective-permute-done((bf16[512,256]{1,0:T(8,128)(2,1)S(1)}, bf16[512,256]{1,0:T(8,128)(2,1)S(1)}, u32[]{:S(2)}, u32[]{:S(2)}) %collective-permute-start.38) | collective-permute-done | bytes 262176 | tf_op jit(solution)/shard_map/ppermute | solution.py:337
  368.9 8.9 %collective-permute-done.44 = bf16[256,512]{1,0:T(8,128)(2,1)S(1)} collective-permute-done((bf16[256,512]{1,0:T(8,128)(2,1)S(1)}, bf16[256,512]{1,0:T(8,128)(2,1)S(1)}, u32[]{:S(2)}, u32[]{:S(2)}) %collective-permute-start.44) | collective-permute-done | bytes 262176 | tf_op jit(solution)/shard_map/ppermute | solution.py:246
  377.7 3.6 collective-permute-start.49
  381.3 2.1 collective-permute-start.50
  386.1 7.8 %collective-permute-done.50 = bf16[256,512]{1,0:T(8,128)(2,1)S(1)} collective-permute-done((bf16[256,512]{1,0:T(8,128)(2,1)S(1)}, bf16[256,512]{1,0:T(8,128)(2,1)S(1)}, u32[]{:S(2)}, u32[]{:S(2)}) %collective-permute-start.50) | collective-permute-done | bytes 262176 | tf_op jit(solution)/shard_map/ppermute | solution.py:246
  395.4 2.6 collective-permute-start.48
  398.3 3.1 collective-permute-done.46
  (173 shorter events, 70.2 us)
Async XLA Ops:
  0.6 58.2 %collective-permute-start = (bf16[256,3840]{1,0:T(8,128)(2,1)}, bf16[256,3840]{1,0:T(8,128)(2,1)}, u32[]{:S(2)}, u32[]{:S(2)}) collective-permute-start(bf16[256,3840]{1,0:T(8,128)(2,1)} %refs_1_.5), channel_id=1, source_target_pairs={{0,8},{4,12},{8,0},{12,4},{16,24},{20,28},{24,16},{28,20},{1,9},{5... | collective-permute-start | bytes 5898248 | tf_op jit(solution)/shard_map/ppermute | solution.py:244
  0.9 58.0 %collective-permute-start.1 = (bf16[256,3840]{1,0:T(8,128)(2,1)}, bf16[256,3840]{1,0:T(8,128)(2,1)}, u32[]{:S(2)}, u32[]{:S(2)}) collective-permute-start(bf16[256,3840]{1,0:T(8,128)(2,1)} %refs_1_.5), channel_id=1, source_target_pairs={{8,16},{12,20},{16,8},{20,12},{9,17},{13,21},{17,9},{21,13},{10,18... | collective-permute-start | bytes 5898248 | tf_op jit(solution)/shard_map/ppermute | solution.py:244
  11.2 36.4 %collective-permute-start.2 = (bf16[64,1024]{1,0:T(8,128)(2,1)S(1)}, bf16[64,1024]{1,0:T(8,128)(2,1)S(1)}, u32[]{:S(2)}, u32[]{:S(2)}) collective-permute-start(bf16[64,1024]{1,0:T(8,128)(2,1)S(1)} %get-tuple-element.139), channel_id=1, source_target_pairs={{0,8},{4,12},{8,0},{12,4},{16,24},{20,28},{24,16},{28,20},{1,9},{5... | collective-permute-start | bytes 393224 | tf_op jit(solution)/shard_map/ppermute | solution.py:244
  11.2 43.7 %collective-permute-start.3 = (bf16[64,1024]{1,0:T(8,128)(2,1)S(1)}, bf16[64,1024]{1,0:T(8,128)(2,1)S(1)}, u32[]{:S(2)}, u32[]{:S(2)}) collective-permute-start(bf16[64,1024]{1,0:T(8,128)(2,1)S(1)} %get-tuple-element.138), channel_id=1, source_target_pairs={{0,16},{4,20},{8,24},{12,28},{16,0},{20,4},{24,8},{28,12},{1,17},{... | collective-permute-start | bytes 393224 | tf_op jit(solution)/shard_map/ppermute | solution.py:244
  12.4 46.4 %collective-permute-start.4 = (bf16[64,1024]{1,0:T(8,128)(2,1)S(1)}, bf16[64,1024]{1,0:T(8,128)(2,1)S(1)}, u32[]{:S(2)}, u32[]{:S(2)}) collective-permute-start(bf16[64,1024]{1,0:T(8,128)(2,1)S(1)} %get-tuple-element.137), channel_id=1, source_target_pairs={{0,24},{4,28},{8,16},{12,20},{16,8},{20,12},{24,0},{28,4},{1,25},{... | collective-permute-start | bytes 393224 | tf_op jit(solution)/shard_map/ppermute | solution.py:244
  58.9 7.8 %collective-permute-start.7 = (bf16[256,3840]{1,0:T(8,128)(2,1)S(1)}, bf16[256,3840]{1,0:T(8,128)(2,1)}, u32[]{:S(2)}, u32[]{:S(2)}) collective-permute-start(bf16[256,3840]{1,0:T(8,128)(2,1)S(1)} %copy-done.5), channel_id=1, source_target_pairs={{0,4},{4,0},{8,12},{12,8},{16,20},{20,16},{24,28},{28,24},{1,5},{5... | collective-permute-start | bytes 5898248 | tf_op jit(solution)/shard_map/ppermute | solution.py:244
  60.6 11.8 %collective-permute-start.9 = (bf16[4,64,512]{2,1,0:T(8,128)(2,1)S(1)}, bf16[4,64,512]{2,1,0:T(8,128)(2,1)S(1)}, u32[]{:S(2)}, u32[]{:S(2)}) collective-permute-start(bf16[4,64,512]{2,1,0:T(8,128)(2,1)S(1)} %get-tuple-element.148), channel_id=1, source_target_pairs={{0,4},{4,0},{8,12},{12,8},{16,20},{20,16},{24,28},{28,24},{1,5},{5... | collective-permute-start | bytes 786440 | tf_op jit(solution)/shard_map/ppermute | solution.py:244
  60.8 46.1 %collective-permute-start.5 = (bf16[256,3840]{1,0:T(8,128)(2,1)}, bf16[256,3840]{1,0:T(8,128)(2,1)}, u32[]{:S(2)}, u32[]{:S(2)}) collective-permute-start(bf16[256,3840]{1,0:T(8,128)(2,1)} %collective-permute-done.refs_3_), channel_id=1, source_target_pairs={{8,16},{12,20},{16,8},{20,12},{9,17},{13,21},{17,9},{21,13},{10,18... | collective-permute-start | bytes 5898248 | tf_op jit(solution)/shard_map/ppermute | solution.py:244
  64.1 43.3 %collective-permute-start.6 = (bf16[256,3840]{1,0:T(8,128)(2,1)}, bf16[256,3840]{1,0:T(8,128)(2,1)}, u32[]{:S(2)}, u32[]{:S(2)}) collective-permute-start(bf16[256,3840]{1,0:T(8,128)(2,1)} %collective-permute-done.1), channel_id=1, source_target_pairs={{8,0},{12,4},{16,24},{20,28},{9,1},{13,5},{17,25},{21,29},{10,2},{... | collective-permute-start | bytes 5898248 | tf_op jit(solution)/shard_map/ppermute | solution.py:244
  66.7 40.8 %collective-permute-start.8 = (bf16[256,3840]{1,0:T(8,128)(2,1)}, bf16[256,3840]{1,0:T(8,128)(2,1)}, u32[]{:S(2)}, u32[]{:S(2)}) collective-permute-start(bf16[256,3840]{1,0:T(8,128)(2,1)} %collective-permute-done.refs_3_), channel_id=1, source_target_pairs={{0,4},{4,0},{8,12},{12,8},{16,20},{20,16},{24,28},{28,24},{1,5},{5... | collective-permute-start | bytes 5898248 | tf_op jit(solution)/shard_map/ppermute | solution.py:244
  71.2 25.6 %collective-permute-start.17 = (bf16[128,3840]{1,0:T(8,128)(2,1)}, bf16[128,3840]{1,0:T(8,128)(2,1)S(1)}, u32[]{:S(2)}, u32[]{:S(2)}) collective-permute-start(bf16[128,3840]{1,0:T(8,128)(2,1)} %get-tuple-element.131), channel_id=1, source_target_pairs={{0,8},{4,12},{24,16},{28,20},{1,9},{5,13},{25,17},{29,21},{2,10},{... | collective-permute-start | bytes 2949128 | tf_op jit(solution)/shard_map/ppermute | solution.py:244
  72.5 13.7 %collective-permute-start.10 = (bf16[1,8,64,512]{3,2,1,0:T(8,128)(2,1)S(1)}, bf16[1,8,64,512]{3,2,1,0:T(8,128)(2,1)S(1)}, u32[]{:S(2)}, u32[]{:S(2)}) collective-permute-start(bf16[1,8,64,512]{3,2,1,0:T(8,128)(2,1)S(1)} %bitcast.103), channel_id=1, source_target_pairs={{0,1},{1,0},{2,3},{3,2},{4,5},{5,4},{6,7},{7,6},{8,9},{9,8},{10,11... | collective-permute-start | bytes 1572872 | tf_op jit(solution)/shard_map/ppermute | solution.py:292
  86.4 24.1 %collective-permute-start.13 = (bf16[2,8,64,512]{3,2,1,0:T(8,128)(2,1)S(1)}, bf16[2,8,64,512]{3,2,1,0:T(8,128)(2,1)S(1)}, u32[]{:S(2)}, u32[]{:S(2)}) collective-permute-start(bf16[2,8,64,512]{3,2,1,0:T(8,128)(2,1)S(1)} %pad_maximum_fusion), channel_id=1, source_target_pairs={{0,2},{1,3},{2,0},{3,1},{4,6},{5,7},{6,4},{7,5},{8,10},{9,11},{10,... | collective-permute-start | bytes 3145736 | tf_op jit(solution)/shard_map/ppermute | solution.py:294
  96.7 24.5 %collective-permute-start.18 = (bf16[128,3840]{1,0:T(8,128)(2,1)S(1)}, bf16[128,3840]{1,0:T(8,128)(2,1)S(1)}, u32[]{:S(2)}, u32[]{:S(2)}) collective-permute-start(bf16[128,3840]{1,0:T(8,128)(2,1)S(1)} %copy-done.25), channel_id=1, source_target_pairs={{0,8},{4,12},{24,16},{28,20},{1,9},{5,13},{25,17},{29,21},{2,10},{... | collective-permute-start | bytes 2949128 | tf_op jit(solution)/shard_map/ppermute | solution.py:244
  111.5 35.7 %collective-permute-start.14 = (bf16[256,3840]{1,0:T(8,128)(2,1)S(1)}, bf16[256,3840]{1,0:T(8,128)(2,1)}, u32[]{:S(2)}, u32[]{:S(2)}) collective-permute-start(bf16[256,3840]{1,0:T(8,128)(2,1)S(1)} %broadcast_select_fusion.1.refs_5_), channel_id=1, source_target_pairs={{0,4},{4,0},{8,12},{12,8},{16,20},{20,16},{24,28},{28,24},{1,5},{5... | collective-permute-start | bytes 5898248 | tf_op jit(solution)/shard_map/ppermute | solution.py:244
  113.1 46.3 %collective-permute-start.11 = (bf16[256,3840]{1,0:T(8,128)(2,1)}, bf16[256,3840]{1,0:T(8,128)(2,1)}, u32[]{:S(2)}, u32[]{:S(2)}) collective-permute-start(bf16[256,3840]{1,0:T(8,128)(2,1)} %collective-permute-done.5), channel_id=1, source_target_pairs={{8,0},{12,4},{16,24},{20,28},{9,1},{13,5},{17,25},{21,29},{10,2},{... | collective-permute-start | bytes 5898248 | tf_op jit(solution)/shard_map/ppermute | solution.py:244
  118.0 46.3 %collective-permute-start.12 = (bf16[256,3840]{1,0:T(8,128)(2,1)}, bf16[256,3840]{1,0:T(8,128)(2,1)}, u32[]{:S(2)}, u32[]{:S(2)}) collective-permute-start(bf16[256,3840]{1,0:T(8,128)(2,1)} %get-tuple-element.78), channel_id=1, source_target_pairs={{8,16},{12,20},{16,8},{20,12},{9,17},{13,21},{17,9},{21,13},{10,18... | collective-permute-start | bytes 5898248 | tf_op jit(solution)/shard_map/ppermute | solution.py:244
  122.2 23.7 %collective-permute-start.19 = (bf16[128,3840]{1,0:T(8,128)(2,1)S(1)}, bf16[128,3840]{1,0:T(8,128)(2,1)}, u32[]{:S(2)}, u32[]{:S(2)}) collective-permute-start(bf16[128,3840]{1,0:T(8,128)(2,1)S(1)} %get-tuple-element.94), channel_id=1, source_target_pairs={{0,8},{4,12},{24,16},{28,20},{1,9},{5,13},{25,17},{29,21},{2,10},{... | collective-permute-start | bytes 2949128 | tf_op jit(solution)/shard_map/ppermute | solution.py:244
  145.9 24.7 %collective-permute-start.20 = (bf16[128,3840]{1,0:T(8,128)(2,1)}, bf16[128,3840]{1,0:T(8,128)(2,1)S(1)}, u32[]{:S(2)}, u32[]{:S(2)}) collective-permute-start(bf16[128,3840]{1,0:T(8,128)(2,1)} %get-tuple-element.96), channel_id=1, source_target_pairs={{0,8},{4,12},{24,16},{28,20},{1,9},{5,13},{25,17},{29,21},{2,10},{... | collective-permute-start | bytes 2949128 | tf_op jit(solution)/shard_map/ppermute | solution.py:244
  147.2 28.3 %collective-permute-start.16 = (bf16[512,3840]{1,0:T(8,128)(2,1)}, bf16[512,3840]{1,0:T(8,128)(2,1)S(1)}, u32[]{:S(2)}, u32[]{:S(2)}) collective-permute-start(bf16[512,3840]{1,0:T(8,128)(2,1)} %mine_ref.3), channel_id=1, source_target_pairs={{0,4},{4,0},{8,12},{12,8},{16,20},{20,16},{24,28},{28,24},{1,5},{5... | collective-permute-start | bytes 11796488 | tf_op jit(solution)/shard_map/ppermute | solution.py:244
  166.2 8.0 %collective-permute-start.15 = (bf16[256,3840]{1,0:T(8,128)(2,1)S(1)}, bf16[256,3840]{1,0:T(8,128)(2,1)S(1)}, u32[]{:S(2)}, u32[]{:S(2)}) collective-permute-start(bf16[256,3840]{1,0:T(8,128)(2,1)S(1)} %broadcast_select_fusion.refs_7_), channel_id=1, source_target_pairs={{0,4},{4,0},{8,12},{12,8},{16,20},{20,16},{24,28},{28,24},{1,5},{5... | collective-permute-start | bytes 5898248 | tf_op jit(solution)/shard_map/ppermute | solution.py:244
  171.7 87.1 %collective-permute-start.24 = (bf16[512,3840]{1,0:T(8,128)(2,1)}, bf16[512,3840]{1,0:T(8,128)(2,1)}, u32[]{:S(2)}, u32[]{:S(2)}) collective-permute-start(bf16[512,3840]{1,0:T(8,128)(2,1)} %constant_dynamic-update-slice_fusion.refs_13_.refs_17_), channel_id=1, source_target_pairs={{8,16},{12,20},{16,8},{20,12},{9,17},{13,21},{17,9},{21,13},{10,18... | collective-permute-start | bytes 11796488 | tf_op jit(solution)/shard_map/ppermute | solution.py:244
  191.3 21.8 %collective-permute-start.21 = (bf16[128,3840]{1,0:T(8,128)(2,1)}, bf16[128,3840]{1,0:T(8,128)(2,1)S(1)}, u32[]{:S(2)}, u32[]{:S(2)}) collective-permute-start(bf16[128,3840]{1,0:T(8,128)(2,1)} %get-tuple-element.105.refs_0_), channel_id=1, source_target_pairs={{0,8},{4,12},{8,0},{12,4},{16,24},{20,28},{24,16},{28,20},{1,9},{5... | collective-permute-start | bytes 2949128 | tf_op jit(solution)/shard_map/ppermute | solution.py:244
  205.1 32.8 %collective-permute-start.22 = (bf16[128,3840]{1,0:T(8,128)(2,1)}, bf16[128,3840]{1,0:T(8,128)(2,1)S(1)}, u32[]{:S(2)}, u32[]{:S(2)}) collective-permute-start(bf16[128,3840]{1,0:T(8,128)(2,1)} %get-tuple-element.110.refs_1_), channel_id=1, source_target_pairs={{0,8},{4,12},{8,0},{12,4},{16,24},{20,28},{24,16},{28,20},{1,9},{5... | collective-permute-start | bytes 2949128 | tf_op jit(solution)/shard_map/ppermute | solution.py:244
  237.1 21.7 %collective-permute-start.25 = (bf16[128,3840]{1,0:T(8,128)(2,1)S(1)}, bf16[128,3840]{1,0:T(8,128)(2,1)}, u32[]{:S(2)}, u32[]{:S(2)}) collective-permute-start(bf16[128,3840]{1,0:T(8,128)(2,1)S(1)} %get-tuple-element.142), channel_id=1, source_target_pairs={{0,8},{4,12},{8,0},{12,4},{16,24},{20,28},{24,16},{28,20},{1,9},{5... | collective-permute-start | bytes 2949128 | tf_op jit(solution)/shard_map/ppermute | solution.py:244
  258.8 9.2 %collective-permute-start.26 = (bf16[512,3840]{1,0:T(8,128)(2,1)}, bf16[512,3840]{1,0:T(8,128)(2,1)S(1)}, u32[]{:S(2)}, u32[]{:S(2)}) collective-permute-start(bf16[512,3840]{1,0:T(8,128)(2,1)} %collective-permute-done.24.mine_ref), channel_id=1, source_target_pairs={{0,4},{4,0},{8,12},{12,8},{16,20},{20,16},{24,28},{28,24},{1,5},{5... | collective-permute-start | bytes 11796488 | tf_op jit(solution)/shard_map/ppermute | solution.py:244
  261.4 48.4 %collective-permute-start.32 = (bf16[256,3840]{1,0:T(8,128)(2,1)}, bf16[256,3840]{1,0:T(8,128)(2,1)}, u32[]{:S(2)}, u32[]{:S(2)}) collective-permute-start(bf16[256,3840]{1,0:T(8,128)(2,1)} %get-tuple-element.118), channel_id=1, source_target_pairs={{8,16},{12,20},{16,8},{20,12},{9,17},{13,21},{17,9},{21,13},{10,18... | collective-permute-start | bytes 5898248 | tf_op jit(solution)/shard_map/ppermute | solution.py:244
  264.5 23.4 %collective-permute-start.28 = (bf16[128,3840]{1,0:T(8,128)(2,1)}, bf16[128,3840]{1,0:T(8,128)(2,1)}, u32[]{:S(2)}, u32[]{:S(2)}) collective-permute-start(bf16[128,3840]{1,0:T(8,128)(2,1)} %get-tuple-element.141), channel_id=1, source_target_pairs={{0,8},{4,12},{8,0},{12,4},{16,24},{20,28},{24,16},{28,20},{1,9},{5... | collective-permute-start | bytes 2949128 | tf_op jit(solution)/shard_map/ppermute | solution.py:244
  266.5 31.8 %collective-permute-start.23 = (bf16[2,512,256]{2,1,0:T(8,128)(2,1)}, bf16[2,512,256]{2,1,0:T(8,128)(2,1)}, u32[]{:S(2)}, u32[]{:S(2)}) collective-permute-start(bf16[2,512,256]{2,1,0:T(8,128)(2,1)} %slice_bitcast_fusion.10), channel_id=1, source_target_pairs={{0,1},{1,0},{2,3},{3,2},{4,5},{5,4},{6,7},{7,6},{8,9},{9,8},{10,11... | collective-permute-start | bytes 1572872 | tf_op jit(solution)/shard_map/ppermute | solution.py:337
  281.3 31.2 %collective-permute-start.34 = (bf16[2,512,256]{2,1,0:T(8,128)(2,1)S(1)}, bf16[2,512,256]{2,1,0:T(8,128)(2,1)S(1)}, u32[]{:S(2)}, u32[]{:S(2)}) collective-permute-start(bf16[2,512,256]{2,1,0:T(8,128)(2,1)S(1)} %slice_bitcast_fusion.6), channel_id=1, source_target_pairs={{0,2},{1,3},{2,0},{3,1},{4,6},{5,7},{6,4},{7,5},{8,10},{9,11},{10,... | collective-permute-start | bytes 1572872 | tf_op jit(solution)/shard_map/ppermute | solution.py:337
  298.3 23.3 %collective-permute-start.30 = (bf16[256,3840]{1,0:T(8,128)(2,1)}, bf16[256,3840]{1,0:T(8,128)(2,1)}, u32[]{:S(2)}, u32[]{:S(2)}) collective-permute-start(bf16[256,3840]{1,0:T(8,128)(2,1)} %collective-permute-done.12.mine_ref), channel_id=1, source_target_pairs={{0,4},{4,0},{8,12},{12,8},{16,20},{20,16},{24,28},{28,24},{1,5},{5... | collective-permute-start | bytes 5898248 | tf_op jit(solution)/shard_map/ppermute | solution.py:244
  309.8 22.7 %collective-permute-start.33 = (bf16[256,3840]{1,0:T(8,128)(2,1)}, bf16[256,3840]{1,0:T(8,128)(2,1)S(1)}, u32[]{:S(2)}, u32[]{:S(2)}) collective-permute-start(bf16[256,3840]{1,0:T(8,128)(2,1)} %collective-permute-done.32.mine_ref), channel_id=1, source_target_pairs={{0,4},{4,0},{8,12},{12,8},{16,20},{20,16},{24,28},{28,24},{1,5},{5... | collective-permute-start | bytes 5898248 | tf_op jit(solution)/shard_map/ppermute | solution.py:244
  311.3 7.5 %collective-permute-start.27 = (bf16[512,256]{1,0:T(8,128)(2,1)S(1)}, bf16[512,256]{1,0:T(8,128)(2,1)S(1)}, u32[]{:S(2)}, u32[]{:S(2)}) collective-permute-start(bf16[512,256]{1,0:T(8,128)(2,1)S(1)} %slice_bitcast_fusion.22), channel_id=1, source_target_pairs={{0,2},{1,3},{2,0},{3,1},{4,6},{5,7},{6,4},{7,5},{8,10},{9,11},{10,... | collective-permute-start | bytes 786440 | tf_op jit(solution)/shard_map/ppermute | solution.py:337
  312.6 8.2 %collective-permute-start.35 = (bf16[512,256]{1,0:T(8,128)(2,1)S(1)}, bf16[512,256]{1,0:T(8,128)(2,1)S(1)}, u32[]{:S(2)}, u32[]{:S(2)}) collective-permute-start(bf16[512,256]{1,0:T(8,128)(2,1)S(1)} %slice_bitcast_fusion.18), channel_id=1, source_target_pairs={{0,1},{1,0},{2,3},{3,2},{4,5},{5,4},{6,7},{7,6},{8,9},{9,8},{10,11... | collective-permute-start | bytes 786440 | tf_op jit(solution)/shard_map/ppermute | solution.py:337
  314.7 31.6 %collective-permute-start.37 = (bf16[2,512,256]{2,1,0:T(8,128)(2,1)}, bf16[2,512,256]{2,1,0:T(8,128)(2,1)}, u32[]{:S(2)}, u32[]{:S(2)}) collective-permute-start(bf16[2,512,256]{2,1,0:T(8,128)(2,1)} %slice_bitcast_fusion.4), channel_id=1, source_target_pairs={{0,2},{1,3},{2,0},{3,1},{4,6},{5,7},{6,4},{7,5},{8,10},{9,11},{10,... | collective-permute-start | bytes 1572872 | tf_op jit(solution)/shard_map/ppermute | solution.py:337
  318.8 30.0 %collective-permute-start.29 = (bf16[2,512,256]{2,1,0:T(8,128)(2,1)}, bf16[2,512,256]{2,1,0:T(8,128)(2,1)}, u32[]{:S(2)}, u32[]{:S(2)}) collective-permute-start(bf16[2,512,256]{2,1,0:T(8,128)(2,1)} %slice_bitcast_fusion.8), channel_id=1, source_target_pairs={{0,1},{1,0},{2,3},{3,2},{4,5},{5,4},{6,7},{7,6},{8,9},{9,8},{10,11... | collective-permute-start | bytes 1572872 | tf_op jit(solution)/shard_map/ppermute | solution.py:337
  346.0 17.5 %collective-permute-start.43 = (bf16[2,256,512]{2,1,0:T(8,128)(2,1)S(1)}, bf16[2,256,512]{2,1,0:T(8,128)(2,1)S(1)}, u32[]{:S(2)}, u32[]{:S(2)}) collective-permute-start(bf16[2,256,512]{2,1,0:T(8,128)(2,1)S(1)} %slice_bitcast_fusion), channel_id=1, source_target_pairs={{0,1},{1,0},{2,3},{3,2},{4,5},{5,4},{6,7},{7,6},{8,9},{9,8},{10,11... | collective-permute-start | bytes 1572872 | tf_op jit(solution)/shard_map/ppermute | solution.py:368
  347.6 15.1 %collective-permute-start.38 = (bf16[512,256]{1,0:T(8,128)(2,1)S(1)}, bf16[512,256]{1,0:T(8,128)(2,1)S(1)}, u32[]{:S(2)}, u32[]{:S(2)}) collective-permute-start(bf16[512,256]{1,0:T(8,128)(2,1)S(1)} %slice_bitcast_fusion.16), channel_id=1, source_target_pairs={{0,1},{1,0},{2,3},{3,2},{4,5},{5,4},{6,7},{7,6},{8,9},{9,8},{10,11... | collective-permute-start | bytes 786440 | tf_op jit(solution)/shard_map/ppermute | solution.py:337
  350.1 13.5 %collective-permute-start.31 = (bf16[512,256]{1,0:T(8,128)(2,1)S(1)}, bf16[512,256]{1,0:T(8,128)(2,1)S(1)}, u32[]{:S(2)}, u32[]{:S(2)}) collective-permute-start(bf16[512,256]{1,0:T(8,128)(2,1)S(1)} %slice_bitcast_fusion.20), channel_id=1, source_target_pairs={{0,2},{1,3},{2,0},{3,1},{4,6},{5,7},{6,4},{7,5},{8,10},{9,11},{10,... | collective-permute-start | bytes 786440 | tf_op jit(solution)/shard_map/ppermute | solution.py:337
  350.6 15.6 %collective-permute-start.40 = (bf16[2,256,512]{2,1,0:T(8,128)(2,1)S(1)}, bf16[2,256,512]{2,1,0:T(8,128)(2,1)S(1)}, u32[]{:S(2)}, u32[]{:S(2)}) collective-permute-start(bf16[2,256,512]{2,1,0:T(8,128)(2,1)S(1)} %slice_bitcast_fusion.2), channel_id=1, source_target_pairs={{0,2},{1,3},{2,0},{3,1},{4,6},{5,7},{6,4},{7,5},{8,10},{9,11},{10,... | collective-permute-start | bytes 1572872 | tf_op jit(solution)/shard_map/ppermute | solution.py:337
  362.8 32.6 %collective-permute-start.39 = (bf16[512,512]{1,0:T(8,128)(2,1)S(1)}, bf16[512,512]{1,0:T(8,128)(2,1)S(1)}, u32[]{:S(2)}, u32[]{:S(2)}) collective-permute-start(bf16[512,512]{1,0:T(8,128)(2,1)S(1)} %pad_maximum_fusion.5), channel_id=1, source_target_pairs={{8,24},{9,25},{10,28},{11,29},{16,2},{17,3},{18,6},{19,7}} | collective-permute-start | bytes 1572872 | tf_op jit(solution)/shard_map/ppermute | solution.py:246
  363.8 14.0 %collective-permute-start.44 = (bf16[256,512]{1,0:T(8,128)(2,1)S(1)}, bf16[256,512]{1,0:T(8,128)(2,1)S(1)}, u32[]{:S(2)}, u32[]{:S(2)}) collective-permute-start(bf16[256,512]{1,0:T(8,128)(2,1)S(1)} %get-tuple-element.146), channel_id=1, source_target_pairs={{8,16},{9,17},{10,20},{11,21},{16,10},{17,11},{18,14},{19,15}} | collective-permute-start | bytes 786440 | tf_op jit(solution)/shard_map/ppermute | solution.py:246
  366.4 14.9 %collective-permute-start.41 = (bf16[256,512]{1,0:T(8,128)(2,1)S(1)}, bf16[256,512]{1,0:T(8,128)(2,1)S(1)}, u32[]{:S(2)}, u32[]{:S(2)}) collective-permute-start(bf16[256,512]{1,0:T(8,128)(2,1)S(1)} %slice_bitcast_fusion.14), channel_id=1, source_target_pairs={{0,1},{1,0},{2,3},{3,2},{4,5},{5,4},{6,7},{7,6},{8,9},{9,8},{10,11... | collective-permute-start | bytes 786440 | tf_op jit(solution)/shard_map/ppermute | solution.py:337
  366.9 31.2 %collective-permute-start.36 = (bf16[512,512]{1,0:T(8,128)(2,1)S(1)}, bf16[512,512]{1,0:T(8,128)(2,1)S(1)}, u32[]{:S(2)}, u32[]{:S(2)}) collective-permute-start(bf16[512,512]{1,0:T(8,128)(2,1)S(1)} %pad_maximum_fusion.4), channel_id=1, source_target_pairs={{0,0},{1,1},{2,4},{3,5},{8,8},{9,9},{10,12},{11,13},{16,18},{17,19... | collective-permute-start | bytes 1572872 | tf_op jit(solution)/shard_map/ppermute | solution.py:246
  367.6 15.9 %collective-permute-start.45 = (bf16[256,512]{1,0:T(8,128)(2,1)S(1)}, bf16[256,512]{1,0:T(8,128)(2,1)S(1)}, u32[]{:S(2)}, u32[]{:S(2)}) collective-permute-start(bf16[256,512]{1,0:T(8,128)(2,1)S(1)} %get-tuple-element.145), channel_id=1, source_target_pairs={{8,20},{9,21},{10,16},{11,17},{16,14},{17,15},{18,10},{19,11}} | collective-permute-start | bytes 786440 | tf_op jit(solution)/shard_map/ppermute | solution.py:246
  381.3 12.7 %collective-permute-start.50 = (bf16[256,512]{1,0:T(8,128)(2,1)S(1)}, bf16[256,512]{1,0:T(8,128)(2,1)S(1)}, u32[]{:S(2)}, u32[]{:S(2)}) collective-permute-start(bf16[256,512]{1,0:T(8,128)(2,1)S(1)} %get-tuple-element.145), channel_id=1, source_target_pairs={{12,20},{13,21},{14,16},{15,17},{20,14},{21,15},{22,10},{23,11}} | collective-permute-start | bytes 786440 | tf_op jit(solution)/shard_map/ppermute | solution.py:246
  383.5 14.6 %collective-permute-start.42 = (bf16[256,512]{1,0:T(8,128)(2,1)S(1)}, bf16[256,512]{1,0:T(8,128)(2,1)S(1)}, u32[]{:S(2)}, u32[]{:S(2)}) collective-permute-start(bf16[256,512]{1,0:T(8,128)(2,1)S(1)} %fusion.6), channel_id=1, source_target_pairs={{8,16},{9,17},{10,20},{11,21},{16,10},{17,11},{18,14},{19,15}} | collective-permute-start | bytes 786440 | tf_op jit(solution)/shard_map/ppermute | solution.py:246
  384.8 13.4 %collective-permute-start.47 = (bf16[512,512]{1,0:T(8,128)(2,1)S(1)}, bf16[512,512]{1,0:T(8,128)(2,1)S(1)}, u32[]{:S(2)}, u32[]{:S(2)}) collective-permute-start(bf16[512,512]{1,0:T(8,128)(2,1)S(1)} %pad_maximum_fusion.5), channel_id=1, source_target_pairs={{12,24},{13,25},{14,28},{15,29},{20,2},{21,3},{22,6},{23,7}} | collective-permute-start | bytes 1572872 | tf_op jit(solution)/shard_map/ppermute | solution.py:246
  (29 other events, 272.1 us)
